TPU v7x, 32 devices: a whole 2x2x4 slice. The times are simulated.
32 devices in a mesh: rep: 2 (over x), dp: 2 (over y), seq: 8 (over z, core).
Axes of the slice: x: 2, y: 2, z: 4, core: 2. Of those that a mesh axis runs over, the one named last changes fastest.
Arguments:
- tokens: bfloat16 [4, 16, 8, 16, 768], P(('rep', 'dp'), 'seq'), may hold values from -6 to 6
- cotangent: bfloat16 [4, 16, 8, 16, 768], P(('rep', 'dp'), 'seq'), may hold values from -6 to 6
- w_qkv: bfloat16 [768, 2304], P('dp'), may hold values from -0.21875 to 0.21875
- w_proj: bfloat16 [768, 768], P('dp'), may hold values from -0.21875 to 0.21875
- conv_weight: float32 [27, 768], replicated, may hold values from -1.25 to 1.25
- norm_gain: float32 [768], replicated, may hold values from 0.5 to 1.5
- head_scale: float32 [24], replicated, may hold values from 2 to 20
- shift_offsets: int32 [2], replicated, may hold values from 1 to 7, as said below
Outputs:
- output: bfloat16 [4, 16, 8, 16, 768], P(('rep', 'dp'), 'seq')
- grad_tokens: bfloat16 [4, 16, 8, 16, 768], P(('rep', 'dp'), 'seq')
- grad_qkv: float32 [768, 2304], P('dp')
- grad_proj: float32 [768, 768], P('dp')
- grad_conv: float32 [27, 768], replicated
- grad_gain: float32 [768], replicated
- grad_scale: float32 [24], replicated
Inputs may be any that keep to these rules, and one draw needn't show every extreme that they name: `shift_offsets`: the two offsets differ.
All inputs are finite; a program needn't handle non-finite values.
Results may differ from a plain program's by a relative error of at most 0.014.
The roundings to bfloat16 on the way count: a program that leaves them out, or rounds other values in their place, can miss the bound.
Values may be sent and summed in bfloat16 or wider, within the bound.
No kernel may reach another device: no remote copies, remote signals or barrier semaphores. Data moves between devices by JAX's collectives and lax.ppermute only.
A program may use at most 128 MiB of HBM per device.

v0:
```python
import math

import jax
import jax.numpy as jnp
from jax import lax
from jax.sharding import PartitionSpec as P

WH = 8
WW = 8


def passed_along(x, axis, by):
    count = lax.axis_size(axis)
    return lax.ppermute(x, axis, [(i, (i + by) % count) for i in range(count)])


def with_halo(x, sides, width):
    for axis, dim in sides:
        count, length = (lax.axis_size(axis), x.shape[dim])
        up = [(i, (i + 1) % count) for i in range(count - 1)]
        down = [(j, i) for i, j in up]
        last = lax.slice_in_dim(x, length - width, length, axis=dim)
        initial = lax.slice_in_dim(x, 0, width, axis=dim)
        before = lax.ppermute(last, axis, up)
        after = lax.ppermute(initial, axis, down)
        x = jnp.concatenate([before, x, after], axis=dim)
    return x


def from_partner(x, axis, bit):
    return lax.ppermute(x, axis, [(i, i ^ 1 << bit) for i in range(lax.axis_size(axis))])


def tap_sum(padded, weight, slab_depth, height, grid_width, flipped):
    summed = jnp.zeros((slab_depth, height, grid_width, padded.shape[-1]), jnp.float32)
    for depth_tap in range(3):
        for row_tap in range(3):
            for col_tap in range(3):
                tap_index = 9 * depth_tap + 3 * row_tap + col_tap
                if flipped:
                    starts = (2 - depth_tap, 2 - row_tap, 2 - col_tap)
                else:
                    starts = (depth_tap, row_tap, col_tap)
                window_part = padded[
                    starts[0] : starts[0] + slab_depth,
                    starts[1] : starts[1] + height,
                    starts[2] : starts[2] + grid_width,
                ]
                summed = summed + weight[tap_index] * window_part.astype(jnp.float32)
    return summed


def into_blocks(field):
    slab_depth, height, grid_width, channels = field.shape
    shaped = field.reshape(slab_depth, height // WH, WH, grid_width // WW, WW, channels)
    shaped = shaped.transpose(1, 3, 0, 2, 4, 5)
    return shaped.reshape(height // WH * (grid_width // WW), slab_depth * WH * WW, channels)


def out_of_blocks(blocks, slab_depth, height, grid_width):
    channels = blocks.shape[-1]
    shaped = blocks.reshape(height // WH, grid_width // WW, slab_depth, WH, WW, channels)
    shaped = shaped.transpose(2, 0, 3, 1, 4, 5)
    return shaped.reshape(slab_depth, height, grid_width, channels)


def roll_local(field, rows_shift, cols_shift, direction):
    return jnp.roll(field, (direction * rows_shift, direction * cols_shift), axis=(1, 2))


def into_frame(field, rows_shift, cols_shift):
    return passed_along(roll_local(field, rows_shift, cols_shift, -1), "seq", -1)


def out_of_frame(field, rows_shift, cols_shift):
    moved = passed_along(field, "seq", 1)
    return roll_local(moved, rows_shift, cols_shift, 1)


def unit_rows(values):
    as_float = values.astype(jnp.float32)
    radius = jnp.sqrt(jnp.sum(as_float * as_float, axis=-1, keepdims=True) + 1.0)
    return (as_float, radius, (as_float / radius).astype(jnp.bfloat16))


def radius_back(as_float, radius, back_unit):
    inner = jnp.sum(as_float * back_unit, axis=-1, keepdims=True)
    return back_unit / radius - as_float * inner / (radius * radius * radius)


def window_forward(unit_query, unit_key, values, allowed, head_scale):
    cosine = jnp.einsum("wqhe,wkhe->whqk", unit_query, unit_key, preferred_element_type=jnp.float32)
    expo = jnp.exp(head_scale[:, None, None] * cosine) * allowed[:, None]
    probability = expo / jnp.sum(expo, axis=-1, keepdims=True)
    weights = probability.astype(jnp.bfloat16)
    attended = jnp.einsum(
        "whqk,wkhe->wqhe", weights, values, preferred_element_type=jnp.float32
    ).astype(jnp.bfloat16)
    return (cosine, probability, weights, attended)


def window_backward(unit_query, unit_key, values, head_scale, back_attended, forward_parts):
    cosine, probability, weights = forward_parts
    back_value = jnp.einsum(
        "whqk,wqhe->wkhe", weights, back_attended, preferred_element_type=jnp.float32
    )
    back_prob = jnp.einsum(
        "wqhe,wkhe->whqk", back_attended, values, preferred_element_type=jnp.float32
    )
    back_score = probability * (
        back_prob - jnp.sum(probability * back_prob, axis=-1, keepdims=True)
    )
    scale_rows = jnp.sum(back_score * cosine, axis=-1)
    scaled = (back_score * head_scale[:, None, None]).astype(jnp.bfloat16)
    back_uq = jnp.einsum("whqk,wkhe->wqhe", scaled, unit_key, preferred_element_type=jnp.float32)
    back_uk = jnp.einsum("whqk,wqhe->wkhe", scaled, unit_query, preferred_element_type=jnp.float32)
    return (back_uq, back_uk, back_value, scale_rows)


def order_halves(mine, other, upper_half):
    return jnp.where(
        upper_half, jnp.concatenate([other, mine], axis=1), jnp.concatenate([mine, other], axis=1)
    )


def pick_half(both, upper_half):
    middle = both.shape[1] // 2
    lower = both[:, :middle]
    higher = both[:, middle:]
    return (jnp.where(upper_half, higher, lower), jnp.where(upper_half, lower, higher))


def per_device(tokens, cotangent, w_qkv, w_proj, conv_weight, norm_gain, head_scale, shift_offsets):
    full_qkv, full_proj = (
        lax.all_gather(w_qkv, "dp", axis=0, tiled=True),
        lax.all_gather(w_proj, "dp", axis=0, tiled=True),
    )
    slab = tokens[0]
    slab_depth, height, grid_width, channels = slab.shape
    head_count = head_scale.shape[0]
    head_dim = channels // head_count
    seq_count = lax.axis_size("seq")
    seq_index = lax.axis_index("seq")
    rows_shift = shift_offsets[0]
    cols_shift = shift_offsets[1]
    spatial = ((0, 0), (1, 1), (1, 1), (0, 0))
    padded_tokens = jnp.pad(with_halo(slab, (("seq", 0),), 1), spatial)
    mixed_field = slab.astype(jnp.float32) + tap_sum(
        padded_tokens, conv_weight, slab_depth, height, grid_width, False
    )
    centred = mixed_field - jnp.mean(mixed_field, axis=-1, keepdims=True)
    inverse_std = lax.rsqrt(jnp.mean(centred * centred, axis=-1, keepdims=True) + 1e-05)
    unit_field = centred * inverse_std
    normed = (unit_field * norm_gain).astype(jnp.bfloat16)
    position_count = slab_depth * height * grid_width
    row_code = 2 * (jnp.arange(height) >= height - rows_shift).astype(jnp.int32)
    col_code = (jnp.arange(grid_width) >= grid_width - cols_shift).astype(jnp.int32)
    plane_code = row_code[:, None] + col_code[None, :]
    grid_code = jnp.broadcast_to(plane_code[None, :, :, None], (slab_depth, height, grid_width, 1))
    block_code = into_blocks(grid_code)[..., 0]
    cotangent_rows = cotangent[0].reshape(position_count, channels)
    back_restored = jnp.einsum(
        "tc,dc->td", cotangent_rows, full_proj, preferred_element_type=jnp.float32
    ).astype(jnp.bfloat16)
    back_restored_field = back_restored.reshape(slab_depth, height, grid_width, channels)
    shifted = into_frame(normed, rows_shift, cols_shift)
    shifted_rows = shifted.reshape(position_count, channels)
    qkv = jnp.dot(shifted_rows, full_qkv, preferred_element_type=jnp.float32).astype(jnp.bfloat16)
    qkv = qkv.reshape(slab_depth, height, grid_width, 3 * channels)
    upper_half = seq_index % 2 == 1
    partner_kv = from_partner(qkv[..., channels:], "seq", 0)
    key_code = order_halves(block_code, block_code, upper_half)
    my_allowed = (block_code[:, :, None] == key_code[:, None, :]).astype(jnp.float32)
    my_blocks = into_blocks(qkv)
    block_count = my_blocks.shape[0]
    half_positions = my_blocks.shape[1]

    def split_heads(part):
        return part.reshape(block_count, half_positions, head_count, head_dim)

    def merge_heads(part):
        return part.reshape(block_count, half_positions, channels)

    query = split_heads(my_blocks[..., :channels])
    my_key = split_heads(my_blocks[..., channels : 2 * channels])
    my_value = split_heads(my_blocks[..., 2 * channels :])
    partner_blocks = into_blocks(partner_kv)
    partner_key = split_heads(partner_blocks[..., :channels])
    partner_value = split_heads(partner_blocks[..., channels:])
    query_float, query_radius, unit_query = unit_rows(query)
    key_float, key_radius, my_unit_key = unit_rows(my_key)
    unused_a, unused_b, partner_unit_key = unit_rows(partner_key)
    unit_key = order_halves(my_unit_key, partner_unit_key, upper_half)
    all_values = order_halves(my_value, partner_value, upper_half)
    forward_all = window_forward(unit_query, unit_key, all_values, my_allowed, head_scale)
    restored = out_of_frame(
        out_of_blocks(merge_heads(forward_all[3]), slab_depth, height, grid_width),
        rows_shift,
        cols_shift,
    )
    back_attended = into_frame(back_restored_field, rows_shift, cols_shift)
    back_heads = split_heads(into_blocks(back_attended))
    back_uq, back_uk, back_value, scale_rows = window_backward(
        unit_query, unit_key, all_values, head_scale, back_heads, forward_all[:3]
    )
    scale_part = jnp.sum(scale_rows, axis=(0, 2))
    mine_uk, other_uk = pick_half(back_uk, upper_half)
    mine_value, other_value = pick_half(back_value, upper_half)
    received = from_partner(
        jnp.stack([other_uk, other_value]).astype(jnp.bfloat16), "seq", 0
    ).astype(jnp.float32)
    mine_uk = mine_uk + received[0]
    mine_value = mine_value + received[1]
    back_query = radius_back(query_float, query_radius, back_uq)
    back_key = radius_back(key_float, key_radius, mine_uk)
    back_blocks = jnp.concatenate(
        [merge_heads(back_query), merge_heads(back_key), merge_heads(mine_value)], axis=-1
    ).astype(jnp.bfloat16)
    back_qkv_rows = out_of_blocks(back_blocks, slab_depth, height, grid_width).reshape(
        position_count, 3 * channels
    )
    back_shifted = jnp.einsum(
        "tj,cj->tc", back_qkv_rows, full_qkv, preferred_element_type=jnp.float32
    ).astype(jnp.bfloat16)
    back_normed = out_of_frame(
        back_shifted.reshape(slab_depth, height, grid_width, channels), rows_shift, cols_shift
    )
    restored_rows = restored.reshape(position_count, channels)
    projected = jnp.dot(restored_rows, full_proj, preferred_element_type=jnp.float32)
    output = (mixed_field + projected.reshape(slab_depth, height, grid_width, channels)).astype(
        jnp.bfloat16
    )
    back_float = back_normed.astype(jnp.float32)
    gain_part = jnp.sum(back_float * unit_field, axis=(0, 1, 2))
    grad_unit = back_float * norm_gain
    back_mixed = cotangent[0].astype(jnp.float32) + inverse_std * (
        grad_unit
        - jnp.mean(grad_unit, axis=-1, keepdims=True)
        - unit_field * jnp.mean(grad_unit * unit_field, axis=-1, keepdims=True)
    )
    padded_back = jnp.pad(
        with_halo(back_mixed.astype(jnp.bfloat16), (("seq", 0),), 1).astype(back_mixed.dtype),
        spatial,
    )
    grad_tokens = (
        back_mixed + tap_sum(padded_back, conv_weight, slab_depth, height, grid_width, True)
    ).astype(jnp.bfloat16)
    conv_rows = []
    for depth_tap in range(3):
        for row_tap in range(3):
            for col_tap in range(3):
                window_part = padded_tokens[
                    depth_tap : depth_tap + slab_depth,
                    row_tap : row_tap + height,
                    col_tap : col_tap + grid_width,
                ]
                conv_rows.append(
                    jnp.sum(back_mixed * window_part.astype(jnp.float32), axis=(0, 1, 2))
                )
    conv_part = jnp.stack(conv_rows)
    qkv_term = jnp.einsum(
        "tc,tj->cj", shifted_rows, back_qkv_rows, preferred_element_type=jnp.float32
    )
    proj_term = jnp.einsum(
        "tc,tj->cj", restored_rows, cotangent_rows, preferred_element_type=jnp.float32
    )
    halves = lax.psum_scatter(
        jnp.concatenate([qkv_term, proj_term], axis=1).astype(jnp.bfloat16),
        "dp",
        scatter_dimension=0,
        tiled=True,
    ).astype(jnp.float32)
    totals = lax.psum(halves, ("rep", "seq"))
    conv_total, gain_total, scale_total = lax.psum(
        (conv_part, gain_part, scale_part), ("rep", "dp", "seq")
    )
    factor = 1.0 / math.sqrt(
        lax.axis_size("rep") * lax.axis_size("dp") * seq_count * position_count
    )
    return (
        output[None],
        grad_tokens[None],
        totals[:, : 3 * channels] * factor,
        totals[:, 3 * channels :] * factor,
        conv_total * factor,
        gain_total * factor,
        scale_total * factor,
    )


def solution(mesh):
    in_specs = (
        P(("rep", "dp"), "seq", None, None, None),
        P(("rep", "dp"), "seq", None, None, None),
        P("dp", None),
        P("dp", None),
        P(),
        P(),
        P(),
        P(),
    )
    out_specs = (
        P(("rep", "dp"), "seq", None, None, None),
        P(("rep", "dp"), "seq", None, None, None),
        P("dp", None),
        P("dp", None),
        P(),
        P(),
        P(),
    )
    return jax.shard_map(
        per_device, mesh=mesh, in_specs=in_specs, out_specs=out_specs, check_vma=False
    )
```

profile of v0, /device:TPU:0, one launch (start us, length us, event | category | flops | bytes accessed | tf_op | source)
XLA Modules:
  0.0 503.8 jit_solution(11831638646250330356)
XLA Ops:
  17.5 3.7 fusion.190
  23.0 5.0 collective-permute-start.2
  28.0 7.1 %all-gather.5.cloned.1.call-done = bf16[768,768]{1,0:T(8,128)(2,1)} async-done(((bf16[384,768]{1,0:T(8,128)(2,1)}), bf16[768,768]{1,0:T(8,128)(2,1)}) %all-gather.5.cloned.1.call-update) | async-done | bytes 1179664 | tf_op jit(solution)/shard_map/all_gather | solution.py:136
  38.1 2.8 collective-permute-start.5
  53.2 32.8 %all-gather.3.cloned.1.call-done = bf16[768,2304]{1,0:T(8,128)(2,1)} async-done(((bf16[384,2304]{1,0:T(8,128)(2,1)}), bf16[768,2304]{1,0:T(8,128)(2,1)}) %all-gather.3.cloned.1.call-update) | async-done | bytes 3538960 | tf_op jit(solution)/shard_map/all_gather | solution.py:135
  86.0 3.1 convolution_convert_fusion.1
  118.2 10.6 %convolution_bitcast_fusion = f32[2,256,24,32]{1,3,2,0:T(8,128)} fusion(f32[2,128,24,32]{1,3,2,0:T(8,128)} %bitcast.140, f32[2,128,24]{1,2,0:T(8,128)} %get-tuple-element.90, f32[24]{0:T(128)} %param.16, f32[2,24,128,256]{3,2,1,0:T(8,128)} %copy-done, bf16[2,128,24,32]{1,3,2,0:T(8,128)(2,1)} %copy.44, bf16[2,128,24,32]{1,3,2,0:T(8,128)(2,1)} %bitcast.123, ...), kind=kOutput, calls=%fused_computation.52 | convolution fusion | flops 317331712 | bytes 9855073 | tf_op jit(solution)/shard_map/whqk,wqhe->wkhe/dot_general | solution.py:116
  128.8 3.6 fusion.15
  136.8 3.0 reshape_reshape.13
  141.8 10.7 %convolution_bitcast_fusion.1 = f32[2,128,24,32]{1,3,2,0:T(8,128)} fusion(bf16[2,128,24,32]{1,3,2,0:T(8,128)(2,1)} %divide_convert_fusion, bf16[2,128,24,32]{1,3,2,0:T(8,128)(2,1)} %copy-done.30, pred[]{:T(512)S(6)} %eq.27, f32[24]{0:T(128)} %param.16, f32[2,24,128,256]{3,2,1,0:T(8,128)} %copy-done, bf16[2,128,24,32]{1,3,2,0:T(8,128)(2,1)} %copy.44, ...), kind=kOutput, calls=%fused_computation.63 | convolution fusion | flops 320477440 | bytes 9044065 | tf_op jit(solution)/shard_map/whqk,wkhe->wqhe/dot_general | solution.py:115
  152.5 2.9 fusion.27
  157.9 2.9 concatenate.70
  169.2 3.0 concatenate.71
  173.8 3.0 concatenate.72
  183.5 2.9 convolution_convert_fusion
  186.4 2.9 collective-permute-done.7
  197.7 5.1 %pad_maximum_fusion = bf16[768,3072]{1,0:T(8,128)(2,1)} fusion(bf16[768,768]{1,0:T(8,128)(2,1)} %convolution_convert_fusion.2, bf16[768,2304]{1,0:T(8,128)(2,1)} %convolution_convert_fusion), kind=kLoop, calls=%fused_computation.36 | loop fusion | flops 9437184 | bytes 9437184 | tf_op jit(solution)/shard_map/concatenate | solution.py:268
  204.0 8.1 %multiply_reduce_fusion = f32[24]{0:T(128)S(1)} fusion(f32[2,24,128,256]{3,2,1,0:T(8,128)} %copy-done.1, f32[2,24,128,256]{3,2,1,0:T(8,128)} %copy-done, bf16[2,128,24,32]{1,3,2,0:T(8,128)(2,1)S(1)} %copy-done.5, bf16[2,128,24,32]{1,3,2,0:T(8,128)(2,1)S(1)} %bitcast.126, bf16[2,128,24,32]{1,3,2,0:T(8,128)(2,1)S(1)} %bitcast.130, pred[]{:T(512)S(6)} %eq.27), kind=kOutput, calls=%fused_computation.27 | convolution fusion | flops 216275168 | bytes 13762657 | tf_op jit(solution)/shard_map/sub | solution.py:111
  217.5 40.6 %all-reduce.2 = (f32[768]{0:T(1024)S(1)}, f32[24]{0:T(128)S(1)}) all-reduce(f32[768]{0:T(1024)S(1)} %copy-done.67, f32[24]{0:T(128)S(1)} %multiply_reduce_fusion), channel_id=1, replica_groups=mesh['rep'=2,'dp'=2,'seq'=8] {'rep','dp','seq'}, use_global_device_ids=true, to_apply=%region_42.44 | all-reduce | flops 792 | bytes 6336 | tf_op jit(solution)/shard_map/psum | solution.py:274
  259.2 57.5 %all-reduce.6.cloned.1.call-done = f32[27,768]{1,0:T(8,128)} async-done(((f32[27,768]{1,0:T(8,128)}), f32[27,768]{1,0:T(8,128)}) %all-reduce.6.cloned.1.call-update) | async-done | bytes 82960 | tf_op jit(solution)/shard_map/psum | solution.py:274
  318.5 3.9 fusion.168
  322.4 57.3 %reduce-scatter.2.cloned.1.call-done = bf16[384,3072]{1,0:T(8,128)(2,1)} async-done(((bf16[768,3072]{1,0:T(8,128)(2,1)}), bf16[384,3072]{1,0:T(8,128)(2,1)}) %reduce-scatter.2.cloned.1.call-update) | async-done | bytes 2359312 | tf_op jit(solution)/shard_map/reduce_scatter | solution.py:267
  379.7 110.6 %all-reduce.7 = f32[384,3072]{1,0:T(8,128)} all-reduce(bf16[384,3072]{1,0:T(8,128)(2,1)} %reduce-scatter.2.cloned.1.call-done), channel_id=1, replica_groups=mesh['rep'=2,'dp'=2,'seq'=8] {'rep','seq'}, use_global_device_ids=true, to_apply=%region_12.14 | all-reduce | flops 1179648 | bytes 7077888 | tf_op jit(solution)/shard_map/psum | solution.py:273
  492.7 4.1 slice_multiply_fusion
  (269 shorter events, 94.5 us)
Async XLA Ops:
  7.2 27.9 %all-gather.5.cloned.1.call-start = ((), (), s32[]{:S(2)}) async-start(), calls=%async_computation.2 | async-start | bytes 1769472 | tf_op jit(solution)/shard_map/all_gather | solution.py:136
  7.9 78.1 %all-gather.3.cloned.1.call-start = ((), (), s32[]{:S(2)}) async-start(), calls=%async_computation.1 | async-start | bytes 5308416 | tf_op jit(solution)/shard_map/all_gather | solution.py:135
  9.0 7.5 %collective-permute-start = (bf16[1,8,16,768]{3,2,1,0:T(8,128)(2,1)S(1)}, bf16[1,8,16,768]{3,2,1,0:T(8,128)(2,1)S(1)}, u32[]{:S(2)}, u32[]{:S(2)}) collective-permute-start(bf16[1,8,16,768]{3,2,1,0:T(8,128)(2,1)S(1)} %get-tuple-element.87), channel_id=1, source_target_pairs={{0,1},{1,2},{2,3},{3,4},{4,5},{5,6},{6,7},{8,9},{9,10},{10,11},{11... | collective-permute-start | bytes 589832 | tf_op jit(solution)/shard_map/ppermute | solution.py:24
  11.4 5.5 %collective-permute-start.1 = (bf16[1,8,16,768]{3,2,1,0:T(8,128)(2,1)S(1)}, bf16[1,8,16,768]{3,2,1,0:T(8,128)(2,1)S(1)}, u32[]{:S(2)}, u32[]{:S(2)}) collective-permute-start(bf16[1,8,16,768]{3,2,1,0:T(8,128)(2,1)S(1)} %get-tuple-element.88), channel_id=1, source_target_pairs={{1,0},{2,1},{3,2},{4,3},{5,4},{6,5},{7,6},{9,8},{10,9},{11,10},{12... | collective-permute-start | bytes 589832 | tf_op jit(solution)/shard_map/ppermute | solution.py:25
  12.7 304.0 %all-reduce.6.cloned.1.call-start = ((), (), s32[]{:S(2)}) async-start(), calls=%async_computation.4 | async-start | bytes 196608 | tf_op jit(solution)/shard_map/psum | solution.py:274
  23.0 30.2 %collective-permute-start.2 = (bf16[2,8,16,768]{3,2,1,0:T(8,128)(2,1)}, bf16[2,8,16,768]{3,2,1,0:T(8,128)(2,1)S(1)}, u32[]{:S(2)}, u32[]{:S(2)}) collective-permute-start(bf16[2,8,16,768]{3,2,1,0:T(8,128)(2,1)} %fusion.166), channel_id=1, source_target_pairs={{0,7},{1,0},{2,1},{3,2},{4,3},{5,4},{6,5},{7,6},{8,15},{9,8},{10,9... | collective-permute-start | bytes 1179656 | tf_op jit(solution)/shard_map/ppermute | solution.py:14
  38.1 8.4 %collective-permute-start.5 = (bf16[2,8,16,768]{3,2,1,0:T(8,128)(2,1)}, bf16[2,8,16,768]{3,2,1,0:T(8,128)(2,1)S(1)}, u32[]{:S(2)}, u32[]{:S(2)}) collective-permute-start(bf16[2,8,16,768]{3,2,1,0:T(8,128)(2,1)} %fusion.162), channel_id=1, source_target_pairs={{0,7},{1,0},{2,1},{3,2},{4,3},{5,4},{6,5},{7,6},{8,15},{9,8},{10,9... | collective-permute-start | bytes 1179656 | tf_op jit(solution)/shard_map/ppermute | solution.py:14
  90.1 9.4 %collective-permute-start.3 = (bf16[2,8,16,1536]{3,2,1,0:T(8,128)(2,1)}, bf16[2,8,16,1536]{3,2,1,0:T(8,128)(2,1)}, u32[]{:S(2)}, u32[]{:S(2)}) collective-permute-start(bf16[2,8,16,1536]{3,2,1,0:T(8,128)(2,1)} %slice.496), channel_id=1, source_target_pairs={{0,1},{1,0},{2,3},{3,2},{4,5},{5,4},{6,7},{7,6},{8,9},{9,8},{10,11... | collective-permute-start | bytes 2359304 | tf_op jit(solution)/shard_map/ppermute | solution.py:31
  133.8 29.3 %collective-permute-start.6 = (bf16[2,2,128,24,32]{2,4,3,1,0:T(8,128)(2,1)}, bf16[2,2,128,24,32]{2,4,3,1,0:T(8,128)(2,1)}, u32[]{:S(2)}, u32[]{:S(2)}) collective-permute-start(bf16[2,2,128,24,32]{2,4,3,1,0:T(8,128)(2,1)} %pad_maximum_fusion.1), channel_id=1, source_target_pairs={{0,1},{1,0},{2,3},{3,2},{4,5},{5,4},{6,7},{7,6},{8,9},{9,8},{10,11... | collective-permute-start | bytes 2359304 | tf_op jit(solution)/shard_map/ppermute | solution.py:31
  141.6 19.3 %collective-permute-start.4 = (bf16[2,8,16,768]{3,2,1,0:T(8,128)(2,1)}, bf16[2,8,16,768]{3,2,1,0:T(8,128)(2,1)}, u32[]{:S(2)}, u32[]{:S(2)}) collective-permute-start(bf16[2,8,16,768]{3,2,1,0:T(8,128)(2,1)} %copy_bitcast_fusion), channel_id=1, source_target_pairs={{0,1},{1,2},{2,3},{3,4},{4,5},{5,6},{6,7},{7,0},{8,9},{9,10},{10,1... | collective-permute-start | bytes 1179656 | tf_op jit(solution)/shard_map/ppermute | solution.py:14
  180.1 9.3 %collective-permute-start.7 = (bf16[2,8,16,768]{3,2,1,0:T(8,128)(2,1)S(1)}, bf16[2,8,16,768]{3,2,1,0:T(8,128)(2,1)S(1)}, u32[]{:S(2)}, u32[]{:S(2)}) collective-permute-start(bf16[2,8,16,768]{3,2,1,0:T(8,128)(2,1)S(1)} %bitcast.148), channel_id=1, source_target_pairs={{0,1},{1,2},{2,3},{3,4},{4,5},{5,6},{6,7},{7,0},{8,9},{9,10},{10,1... | collective-permute-start | bytes 1179656 | tf_op jit(solution)/shard_map/ppermute | solution.py:14
  197.7 182.0 %reduce-scatter.2.cloned.1.call-start = ((), (), s32[]{:S(2)}) async-start(), calls=%async_computation.3 | async-start | bytes 7077888 | tf_op jit(solution)/shard_map/reduce_scatter | solution.py:267
  214.7 103.7 %copy-start.40 = (f32[768]{0:T(1024)S(1)}, f32[768]{0:T(1024)}, u32[]{:S(2)}) copy-start(f32[768]{0:T(1024)} %copy-done.39) | copy-start | bytes 9220
  214.7 103.7 %copy-start.42 = (f32[768]{0:T(1024)S(1)}, f32[768]{0:T(1024)}, u32[]{:S(2)}) copy-start(f32[768]{0:T(1024)} %copy-done.41) | copy-start | bytes 9220
  214.7 103.7 %copy-start.44 = (f32[768]{0:T(1024)S(1)}, f32[768]{0:T(1024)}, u32[]{:S(2)}) copy-start(f32[768]{0:T(1024)} %copy-done.43) | copy-start | bytes 9220
  214.7 103.7 %copy-start.46 = (f32[768]{0:T(1024)S(1)}, f32[768]{0:T(1024)}, u32[]{:S(2)}) copy-start(f32[768]{0:T(1024)} %copy-done.45) | copy-start | bytes 9220
  214.7 103.7 %copy-start.48 = (f32[768]{0:T(1024)S(1)}, f32[768]{0:T(1024)}, u32[]{:S(2)}) copy-start(f32[768]{0:T(1024)} %copy-done.47) | copy-start | bytes 9220
  214.7 103.7 %copy-start.50 = (f32[768]{0:T(1024)S(1)}, f32[768]{0:T(1024)}, u32[]{:S(2)}) copy-start(f32[768]{0:T(1024)} %copy-done.49) | copy-start | bytes 9220
  214.7 103.7 %copy-start.52 = (f32[768]{0:T(1024)S(1)}, f32[768]{0:T(1024)}, u32[]{:S(2)}) copy-start(f32[768]{0:T(1024)} %copy-done.51) | copy-start | bytes 9220
  214.8 103.7 %copy-start.54 = (f32[768]{0:T(1024)S(1)}, f32[768]{0:T(1024)}, u32[]{:S(2)}) copy-start(f32[768]{0:T(1024)} %copy-done.53) | copy-start | bytes 9220
  214.8 103.7 %copy-start.56 = (f32[768]{0:T(1024)S(1)}, f32[768]{0:T(1024)}, u32[]{:S(2)}) copy-start(f32[768]{0:T(1024)} %copy-done.55) | copy-start | bytes 9220
  214.8 103.7 %copy-start.58 = (f32[768]{0:T(1024)S(1)}, f32[768]{0:T(1024)}, u32[]{:S(2)}) copy-start(f32[768]{0:T(1024)} %copy-done.57) | copy-start | bytes 9220
  214.9 103.4 %collective-permute-start.8 = (bf16[1,8,16,768]{3,2,1,0:T(8,128)(2,1)S(1)}, bf16[1,8,16,768]{3,2,1,0:T(8,128)(2,1)S(1)}, u32[]{:S(2)}, u32[]{:S(2)}) collective-permute-start(bf16[1,8,16,768]{3,2,1,0:T(8,128)(2,1)S(1)} %get-tuple-element.85), channel_id=1, source_target_pairs={{0,1},{1,2},{2,3},{3,4},{4,5},{5,6},{6,7},{8,9},{9,10},{10,11},{11... | collective-permute-start | bytes 589832 | tf_op jit(solution)/shard_map/ppermute | solution.py:24
  216.2 102.1 %collective-permute-start.9 = (bf16[1,8,16,768]{3,2,1,0:T(8,128)(2,1)S(1)}, bf16[1,8,16,768]{3,2,1,0:T(8,128)(2,1)S(1)}, u32[]{:S(2)}, u32[]{:S(2)}) collective-permute-start(bf16[1,8,16,768]{3,2,1,0:T(8,128)(2,1)S(1)} %get-tuple-element.86), channel_id=1, source_target_pairs={{1,0},{2,1},{3,2},{4,3},{5,4},{6,5},{7,6},{9,8},{10,9},{11,10},{12... | collective-permute-start | bytes 589832 | tf_op jit(solution)/shard_map/ppermute | solution.py:25
  (61 other events, 929.1 us)
Sparse Core Ops, SparseCore 0:
  9.6 25.4 all-gather.4
  36.6 49.3 all-gather.2
  197.8 118.8 all-reduce.5
  318.9 60.8 reduce-scatter.1
where the time goes:
time: 510 us; the launch traced here: 504 us
  waiting for transfers between devices  160 us (31%)
  blocking collectives  151 us (30%)
  other arithmetic  52.5 us (10%)
  local copies, waits for them, and re-layouts  51.6 us (10%)
  matrix products  50 us (10%)
  between operations  22.1 us (4%)
  starting transfers between devices  16.7 us (3%)
    psum x1, blocking collectives, per_device(): totals = lax.psum(halves, ('rep', 'seq'))  111 us
    psum x1, waiting for transfers between devices, per_device(): lax.psum((conv_part, gain_part, scale_part), ('rep', 'dp', 'seq'))  57.5 us
    reduce_scatter x1, waiting for transfers between devices, per_device(): lax.psum_scatter(jnp.concatenate([qkv_term, proj_term], axis=1).astype(jn...  57.3 us
    psum x1, blocking collectives, per_device(): lax.psum((conv_part, gain_part, scale_part), ('rep', 'dp', 'seq'))  40.6 us
    all_gather x1, waiting for transfers between devices, per_device(): lax.all_gather(w_qkv, 'dp', axis=0, tiled=True)  32.8 us
    dot_general x1, matrix products, window_backward(): jnp.einsum('whqk,wkhe->wqhe', scaled, unit_key, preferred_element_type=jn...  10.7 us
    dot_general x1, matrix products, window_backward(): jnp.einsum('whqk,wqhe->wkhe', scaled, unit_query, preferred_element_type=...  10.6 us
  transfers between devices with their start and end apart: 14, of which 7 were waited for; matrix products, arithmetic and copies ran while one was open for 16% of the time, Pallas kernels for 0%

commit v1 on v0

v1 whole, which is shorter than its diff:
```python
import functools
import math

import jax
import jax.numpy as jnp
from jax import lax
from jax.experimental import pallas as pl
from jax.experimental.pallas import tpu as pltpu
from jax.sharding import PartitionSpec as P

HALF = 8
BF = jnp.bfloat16
F32 = jnp.float32


def swapped(x, axis, flip):
    count = 1
    for name in (axis,) if isinstance(axis, str) else axis:
        count = count * lax.axis_size(name)
    return lax.ppermute(x, axis, [(i, i ^ flip) for i in range(count)])


def window_partner(x):
    count = lax.axis_size("seq")
    pairs = [(i, (i + 1) % count if i % 2 else (i - 1) % count) for i in range(count)]
    return lax.ppermute(x, "seq", pairs)


def with_halo(x):
    count = lax.axis_size("seq")
    up = [(i, i + 1) for i in range(count - 1)]
    down = [(j, i) for i, j in up]
    before = lax.ppermute(x[-1:], "seq", up)
    after = lax.ppermute(x[:1], "seq", down)
    return jnp.concatenate([before, x, after], axis=0)


def tap_sum(padded, weight, slab_depth, height, grid_width, flipped):
    summed = jnp.zeros((slab_depth, height, grid_width, padded.shape[-1]), F32)
    for a in range(3):
        for b in range(3):
            for e in range(3):
                starts = (2 - a, 2 - b, 2 - e) if flipped else (a, b, e)
                part = padded[
                    starts[0] : starts[0] + slab_depth,
                    starts[1] : starts[1] + height,
                    starts[2] : starts[2] + grid_width,
                ]
                summed = summed + weight[9 * a + 3 * b + e] * part.astype(F32)
    return summed


def attention_kernel(head_dim, head_count, nums, scale, qkv, ba, att, back, gs):
    n = qkv.shape[1]
    channels = head_count * head_dim
    rows_shift, cols_shift, second = nums[0], nums[1], nums[2]

    def code(dim):
        t = lax.broadcasted_iota(jnp.int32, (n, n), dim)
        row = (t >> 3) & 7
        col = t & 7
        first_bit = jnp.where(row < rows_shift, 2, 0)
        return first_bit + jnp.where(col < cols_shift, second, 0)

    allowed = jnp.where(code(0) == code(1), 1.0, 0.0).astype(F32)
    over_rows = (((0,), (0,)), ((), ()))
    over_lanes = (((1,), (1,)), ((), ()))

    def unit(raw):
        inverse = lax.rsqrt(jnp.sum(raw * raw, axis=0, keepdims=True) + 1.0)
        return inverse, (raw * inverse).astype(BF)

    def radius_back(raw, inverse, grad):
        inner = jnp.sum(raw * grad, axis=0, keepdims=True)
        return grad * inverse - raw * (inner * (inverse * inverse * inverse))

    def one_head(h):
        def rows(base):
            return pl.ds(pl.multiple_of(base + h * head_dim, head_dim), head_dim)

        s = scale[h]
        qf = qkv[rows(0), :].astype(F32)
        kf = qkv[rows(channels), :].astype(F32)
        v = qkv[rows(2 * channels), :]
        b = ba[rows(0), :]
        iq, uq = unit(qf)
        ik, uk = unit(kf)
        cosine = lax.dot_general(uk, uq, over_rows, preferred_element_type=F32)
        expo = jnp.exp(cosine * s) * allowed
        prob = expo * (1.0 / jnp.sum(expo, axis=0, keepdims=True))
        weights = prob.astype(BF)
        att[rows(0), :] = jnp.dot(v, weights, preferred_element_type=F32).astype(BF)
        back_prob = lax.dot_general(v, b, over_rows, preferred_element_type=F32)
        mean = jnp.sum(prob * back_prob, axis=0, keepdims=True)
        back_score = prob * (back_prob - mean)
        gs[pl.ds(h, 1), :] = jnp.sum(back_score * cosine, axis=0, keepdims=True)
        scaled = (back_score * s).astype(BF)
        buq = jnp.dot(uk, scaled, preferred_element_type=F32)
        buk = lax.dot_general(uq, scaled, over_lanes, preferred_element_type=F32)
        bv = lax.dot_general(b, weights, over_lanes, preferred_element_type=F32)
        back[rows(0), :] = radius_back(qf, iq, buq).astype(BF)
        back[rows(channels), :] = radius_back(kf, ik, buk).astype(BF)
        back[rows(2 * channels), :] = bv.astype(BF)

    def body(i, carry):
        for u in range(4):
            one_head(i * 4 + u)
        return carry

    lax.fori_loop(0, head_count // 4, body, 0)


def window_attention(nums, scale, qkv, ba):
    head_count = scale.shape[0]
    channels, n = ba.shape
    vmem = pl.BlockSpec(memory_space=pltpu.VMEM)
    smem = pl.BlockSpec(memory_space=pltpu.SMEM)
    return pl.pallas_call(
        functools.partial(attention_kernel, channels // head_count, head_count),
        out_shape=(
            jax.ShapeDtypeStruct((channels, n), BF),
            jax.ShapeDtypeStruct((3 * channels, n), BF),
            jax.ShapeDtypeStruct((head_count, n), F32),
        ),
        in_specs=[smem, smem, vmem, vmem],
        out_specs=(vmem, vmem, vmem),
        compiler_params=pltpu.CompilerParams(vmem_limit_bytes=32 * 1024 * 1024),
        cost_estimate=pl.CostEstimate(
            flops=14 * n * n * channels,
            bytes_accessed=16 * n * channels,
            transcendentals=n * n * head_count,
        ),
        name="window_attention",
    )(nums, scale, qkv, ba)


def pick(x, index, axis):
    return lax.dynamic_index_in_dim(x, index, axis, keepdims=False)


def tree_sum(parts):
    while len(parts) > 1:
        parts = [a + b for a, b in zip(parts[::2], parts[1::2])]
    return parts[0]


def chip_stages(chips):
    stages = []
    left = chips
    while left > 1:
        radix = 4 if left % 4 == 0 else 2
        left = left // radix
        stages.append((radix, left))
    return stages


def scatter_sum(grad, where):
    rep, dp, chip, core, chips = where
    rows = grad.shape[0] // (8 * chips)
    parts = grad.reshape(2, 2, chips, 2, rows, grad.shape[1])
    other = swapped(pick(parts, 1 - core, 3).astype(BF), "seq", 1)
    total = pick(parts, core, 3) + other.astype(F32)
    got = []
    for k in range(4):
        block = pick(pick(total, dp ^ (k & 1), 0), rep ^ (k >> 1), 0)
        got.append(swapped(block.astype(BF), ("rep", "dp"), k).astype(F32) if k else block)
    total = tree_sum(got)
    for radix, stride in chip_stages(chips):
        digit = (chip // stride) % radix
        parts = total.reshape((radix, stride) + total.shape[1:])
        got = []
        for k in range(radix):
            block = pick(parts, digit ^ k, 0)
            got.append(swapped(block.astype(BF), "seq", 2 * k * stride).astype(F32) if k else block)
        total = tree_sum(got)
    return total[0]


def gather_rows(block, where):
    rep, dp, chip, core, chips = where
    held = block.astype(BF)[None]
    for radix, stride in chip_stages(chips)[::-1]:
        digit = (chip // stride) % radix
        got = [swapped(held, "seq", 2 * k * stride) if k else held for k in range(radix)]
        bunch = jnp.stack(got)
        held = jnp.concatenate([pick(bunch, digit ^ j, 0) for j in range(radix)])
    got = swapped(held, "rep", 1)
    held = jnp.stack([jnp.where(rep == 0, held, got), jnp.where(rep == 0, got, held)])
    got = swapped(held, "seq", 1)
    first = jnp.where(core == 0, held, got)
    second = jnp.where(core == 0, got, held)
    return jnp.stack([first, second], axis=2).reshape(-1, block.shape[1])


def sum_everywhere(x, where):
    chips = where[4]
    x = x + swapped(x, "seq", 1)
    x = tree_sum([swapped(x, ("rep", "dp"), k) if k else x for k in range(4)])
    for radix, stride in chip_stages(chips):
        x = tree_sum([swapped(x, "seq", 2 * k * stride) if k else x for k in range(radix)])
    return x


def full_weights(mine, dp, core):
    half = mine.shape[0] // 2
    part = lax.dynamic_slice_in_dim(mine, core * half, half, 0)
    got = swapped(part, "dp", 1)
    other = swapped(got, "seq", 1)
    m0, m1 = mine[:half], mine[half:]
    p0, p1 = jnp.where(core == 0, got, other), jnp.where(core == 0, other, got)
    low = dp == 0
    return jnp.concatenate(
        [jnp.where(low, a, b) for a, b in ((m0, p0), (m1, p1), (p0, m0), (p1, m1))]
    )


def per_device(tokens, cotangent, w_qkv, w_proj, conv_weight, norm_gain, head_scale, shift_offsets):
    slab = tokens[0]
    cot = cotangent[0]
    depth, height, width, channels = slab.shape
    head_count = head_scale.shape[0]
    seq_count = lax.axis_size("seq")
    seq_index = lax.axis_index("seq")
    core = seq_index % 2
    rep, dp = lax.axis_index("rep"), lax.axis_index("dp")
    where = (rep, dp, seq_index // 2, core, seq_count // 2)
    rows_shift, cols_shift = shift_offsets[0], shift_offsets[1]
    positions = depth * height * width
    half = positions // 2
    columns = jnp.arange(HALF)[None, None, :, None]
    straight = (columns >= cols_shift) == (core == 1)

    def split_columns(field):
        low, high = field[:, :, :HALF], field[:, :, HALF:]
        return (
            jnp.where(straight, low, high).reshape(half, -1),
            jnp.where(straight, high, low).reshape(half, -1),
        )

    def join_columns(mine, theirs):
        mine = mine.reshape(depth, height, HALF, -1)
        theirs = theirs.reshape(depth, height, HALF, -1)
        return jnp.concatenate(
            [jnp.where(straight, mine, theirs), jnp.where(straight, theirs, mine)], axis=2
        )

    weights = full_weights(jnp.concatenate([w_qkv, w_proj], axis=1), dp, core)
    full_qkv, full_proj = weights[:, : 3 * channels], weights[:, 3 * channels :]

    spatial = ((0, 0), (1, 1), (1, 1), (0, 0))
    padded_tokens = jnp.pad(with_halo(slab), spatial)
    cot_mine, cot_theirs = split_columns(cot)
    cot_window = jnp.concatenate([cot_mine, window_partner(cot_theirs)])
    mixed_field = slab.astype(F32) + tap_sum(
        padded_tokens, conv_weight, depth, height, width, False
    )
    centred = mixed_field - jnp.mean(mixed_field, axis=-1, keepdims=True)
    inverse_std = lax.rsqrt(jnp.mean(centred * centred, axis=-1, keepdims=True) + 1e-05)
    unit_field = centred * inverse_std
    normed = (unit_field * norm_gain).astype(BF)
    x_mine, x_theirs = split_columns(normed)
    x_window = jnp.concatenate([x_mine, window_partner(x_theirs)])

    qkv = jnp.einsum("tk,kc->ct", x_window, full_qkv, preferred_element_type=F32).astype(BF)
    back_attended = jnp.einsum(
        "td,cd->ct", cot_window, full_proj, preferred_element_type=F32
    ).astype(BF)
    nums = jnp.stack([rows_shift, cols_shift, 1 - core]).astype(jnp.int32)
    attended, back_qkv, scale_rows = window_attention(nums, head_scale, qkv, back_attended)

    proj_term = jnp.einsum("ct,td->cd", attended, cot_window, preferred_element_type=F32)
    qkv_term = jnp.einsum("tc,jt->cj", x_window, back_qkv, preferred_element_type=F32)
    back_shifted = jnp.einsum(
        "jt,cj->tc", back_qkv, full_qkv, preferred_element_type=F32
    ).astype(BF)
    back_normed = join_columns(back_shifted[:half], window_partner(back_shifted[half:]))

    grads = scatter_sum(jnp.concatenate([qkv_term, proj_term], axis=1), where)
    factor = 1.0 / math.sqrt(
        lax.axis_size("rep") * lax.axis_size("dp") * seq_count * positions
    )
    grads = gather_rows(grads, where).astype(F32) * factor

    att_theirs = window_partner(attended[:, half:])
    att_mine = attended[:, :half]
    lane_straight = ((jnp.arange(half) % HALF)[None, :] >= cols_shift) == (core == 1)
    projected = [
        jnp.einsum("ct,cd->td", side, full_proj, preferred_element_type=F32).reshape(
            depth, height, HALF, channels
        )
        for side in (
            jnp.where(lane_straight, att_mine, att_theirs),
            jnp.where(lane_straight, att_theirs, att_mine),
        )
    ]
    output = (mixed_field + jnp.concatenate(projected, axis=2)).astype(BF)

    back_float = back_normed.astype(F32)
    gain_part = jnp.sum(back_float * unit_field, axis=(0, 1, 2))
    grad_unit = back_float * norm_gain
    back_mixed = cot.astype(F32) + inverse_std * (
        grad_unit
        - jnp.mean(grad_unit, axis=-1, keepdims=True)
        - unit_field * jnp.mean(grad_unit * unit_field, axis=-1, keepdims=True)
    )
    padded_back = jnp.pad(with_halo(back_mixed.astype(BF)).astype(F32), spatial)
    grad_tokens = (
        back_mixed + tap_sum(padded_back, conv_weight, depth, height, width, True)
    ).astype(BF)
    conv_rows = []
    for a in range(3):
        for b in range(3):
            for e in range(3):
                part = padded_tokens[a : a + depth, b : b + height, e : e + width]
                conv_rows.append(jnp.sum(back_mixed * part.astype(F32), axis=(0, 1, 2)))
    scale_part = jnp.sum(scale_rows, axis=1)
    small = jnp.stack(conv_rows + [gain_part, jnp.pad(scale_part, (0, channels - head_count))])
    small = sum_everywhere(small, where) * factor
    taps = conv_weight.shape[0]
    return (
        output[None],
        grad_tokens[None],
        grads[:, : 3 * channels],
        grads[:, 3 * channels :],
        small[:taps],
        small[taps],
        small[taps + 1, :head_count],
    )


def solution(mesh):
    block = P(("rep", "dp"), "seq", None, None, None)
    rows = P("dp", None)
    return jax.shard_map(
        per_device,
        mesh=mesh,
        in_specs=(block, block, rows, rows, P(), P(), P(), P()),
        out_specs=(block, block, rows, rows, P(), P(), P()),
        check_vma=False,
    )
```

time: 510 us -> 203 us (0.40); the launches traced: 504 us -> 202 us
  blocking collectives: 151 us -> 0 us
  waiting for transfers between devices: 160 us -> 83 us
  matrix products: 50 us -> 12.8 us
  local copies, waits for them, and re-layouts: 51.6 us -> 18.9 us
  starting transfers between devices: 16.7 us -> 37.5 us
  between operations: 22.1 us -> 1.8 us
  other arithmetic: 52.5 us -> 32.8 us
  Pallas kernels: 0 us -> 15.5 us
    psum x2 -> x0, blocking collectives: 151 us -> none  [the longest x1 111 us: per_device(): totals = lax.psum(halves, ('rep', 'seq'))]
    ppermute x10 -> x29, waiting for transfers between devices: 4.07 us -> 83 us  [the longest x21 72.9 us: swapped(): return lax.ppermute(x, axis, [(i, i ^ flip) for i in range(count)])]
    psum x1 -> x0, waiting for transfers between devices: 57.5 us -> none  [per_device(): lax.psum((conv_part, gain_part, scale_part), ('rep', 'dp', 'seq'))]
    reduce_scatter x1 -> x0, waiting for transfers between devices: 57.3 us -> none  [per_device(): lax.psum_scatter(jnp.concatenate([qkv_term, proj_term], axis=1).astype(jn...]
    all_gather x2 -> x0, waiting for transfers between devices: 40 us -> none  [the longest x1 32.8 us: per_device(): lax.all_gather(w_qkv, 'dp', axis=0, tiled=True)]
    dot_general x11 -> x7, matrix products: 42 us -> 12.8 us  [the longest x1 3.98 us: per_device(): jnp.einsum('tc,jt->cj', x_window, back_qkv, preferred_element_type=F32)]
    ppermute x10 -> x29, starting transfers between devices: 16.6 us -> 37.5 us  [the longest x21 24.5 us: swapped(): return lax.ppermute(x, axis, [(i, i ^ flip) for i in range(count)])]
    another operation x35 -> x30, local copies, waits for them, and re-layouts: 17.4 us -> 1.55 us  [per_device(): jnp.stack(conv_rows + [gain_part, jnp.pad(scale_part, (0, channels - head...]
  transfers between devices with their start and end apart: 14 -> 29, of which waited for: 7 -> 15; matrix products, arithmetic and copies ran while one was open for 16% -> 16% of each run, Pallas kernels for 0% -> 0%
where the time goes in v1:
time: 203 us; the launch traced here: 202 us
  waiting for transfers between devices  83 us (41%)
  starting transfers between devices  37.5 us (18%)
  other arithmetic  32.8 us (16%)
  local copies, waits for them, and re-layouts  18.9 us (9%)
  Pallas kernels  15.5 us (8%)
  matrix products  12.8 us (6%)
    ppermute x21, waiting for transfers between devices, swapped(): return lax.ppermute(x, axis, [(i, i ^ flip) for i in range(count)])  72.9 us
    ppermute x21, starting transfers between devices, swapped(): return lax.ppermute(x, axis, [(i, i ^ flip) for i in range(count)])  24.5 us
    pallas_call x1, Pallas kernels, window_attention(): pl.pallas_call(functools.partial(attention_kernel, channels // head_count...  15.5 us
    concatenate x1, other arithmetic, per_device(): grads = scatter_sum(jnp.concatenate([qkv_term, proj_term], axis=1), where)  8.74 us
    ppermute x4, waiting for transfers between devices, window_partner(): return lax.ppermute(x, 'seq', pairs)  8.08 us
    ppermute x4, starting transfers between devices, window_partner(): return lax.ppermute(x, 'seq', pairs)  7.68 us
    convert_element_type x1, local copies, waits for them, and re-layouts, scatter_sum(): other = swapped(pick(parts, 1 - core, 3).astype(BF), 'seq', 1)  4.08 us
    unnamed x103, local copies, waits for them, and re-layouts  4.08 us
  transfers between devices with their start and end apart: 29, of which 15 were waited for; matrix products, arithmetic and copies ran while one was open for 16% of the time, Pallas kernels for 0%

profile of v1, /device:TPU:0, one launch (start us, length us, event | category | flops | bytes accessed | tf_op | source)
XLA Modules:
  0.0 202.3 jit_solution(3765433844710860042)
XLA Ops:
  0.7 2.9 %constant_dynamic-update-slice_fusion.1 = bf16[384,3072]{1,0:T(8,128)(2,1)} fusion(bf16[384,2304]{1,0:T(8,128)(2,1)} %param.10), kind=kLoop, calls=%fused_computation.286 | loop fusion | bytes 3538944
  5.8 3.0 %collective-permute-start.2 = (bf16[192,3072]{1,0:T(8,128)(2,1)S(1)}, bf16[192,3072]{1,0:T(8,128)(2,1)}, u32[]{:S(2)}, u32[]{:S(2)}) collective-permute-start(bf16[192,3072]{1,0:T(8,128)(2,1)S(1)} %constant_dynamic-slice_fusion), channel_id=1, source_target_pairs={{0,8},{8,0},{1,9},{9,1},{2,10},{10,2},{3,11},{11,3},{4,12},{12,4},... | collective-permute-start | bytes 3538952 | tf_op jit(solution)/shard_map/ppermute | solution.py:20
  15.8 19.1 %collective-permute-done.2 = bf16[192,3072]{1,0:T(8,128)(2,1)} collective-permute-done((bf16[192,3072]{1,0:T(8,128)(2,1)S(1)}, bf16[192,3072]{1,0:T(8,128)(2,1)}, u32[]{:S(2)}, u32[]{:S(2)}) %collective-permute-start.2) | collective-permute-done | bytes 1179680 | tf_op jit(solution)/shard_map/ppermute | solution.py:20
  34.9 3.6 %fusion.148 = (f32[2,8,16]{2,1,0:T(8,128)S(1)}, f32[2,8,16,768]{3,2,1,0:T(8,128)S(1)}) fusion(bf16[4,10,18,768]{3,2,1,0:T(8,128)(2,1)S(1)} %select_maximum_fusion, f32[768]{0:T(1024)S(1)} %get-tuple-element.74, f32[768]{0:T(1024)S(1)} %get-tuple-element.75, f32[768]{0:T(1024)S(1)} %get-tuple-element.50, f32[768]{0:T(1024)S(1)} %get-tuple-element.51, ...), kind=kLoop, calls=%fused_computation.328 | loop fusion | flops 16514816 | bytes 11094016 | tf_op jit(solution)/shard_map/reduce_sum | solution.py:257
  40.1 4.0 %collective-permute-start.5 = (bf16[128,768]{1,0:T(8,128)(2,1)S(1)}, bf16[128,768]{1,0:T(8,128)(2,1)S(1)}, u32[]{:S(2)}, u32[]{:S(2)}) collective-permute-start(bf16[128,768]{1,0:T(8,128)(2,1)S(1)} %bitcast.88), channel_id=1, source_target_pairs={{0,7},{1,2},{2,1},{3,4},{4,3},{5,6},{6,5},{7,0},{8,15},{9,10},{10,... | collective-permute-start | bytes 589832 | tf_op jit(solution)/shard_map/ppermute | solution.py:26
  46.4 2.4 %collective-permute-done.5 = bf16[128,768]{1,0:T(8,128)(2,1)S(1)} collective-permute-done((bf16[128,768]{1,0:T(8,128)(2,1)S(1)}, bf16[128,768]{1,0:T(8,128)(2,1)S(1)}, u32[]{:S(2)}, u32[]{:S(2)}) %collective-permute-start.5) | collective-permute-done | bytes 196640 | tf_op jit(solution)/shard_map/ppermute | solution.py:26
  49.3 3.8 %collective-permute-done.4 = bf16[128,768]{1,0:T(8,128)(2,1)S(1)} collective-permute-done((bf16[128,768]{1,0:T(8,128)(2,1)S(1)}, bf16[128,768]{1,0:T(8,128)(2,1)S(1)}, u32[]{:S(2)}, u32[]{:S(2)}) %collective-permute-start.4) | collective-permute-done | bytes 196640 | tf_op jit(solution)/shard_map/ppermute | solution.py:26
  54.3 15.5 %window_attention.1 = (bf16[768,256]{1,0:T(8,128)(2,1)S(1)}, bf16[2304,256]{1,0:T(8,128)(2,1)S(1)}, f32[24,256]{1,0:T(8,128)S(1)}) custom-call(s32[3]{0:T(128)S(1)} %pad_add_fusion.nums, f32[24]{0:T(128)S(1)} %copy-done, bf16[2304,256]{1,0:T(8,128)(2,1)S(1)} %convolution_convert_fusion.qkv, bf16[768,256]{1,0:T(8,128)(2,1)S(1)} %convolution_convert_fusion.1.ba), custom_call_target="tpu_custom_call" | custom-call | flops 704643072 | bytes 3145728 | tf_op jit(solution)/shard_map/window_attention/pallas_call | solution.py:118
  71.8 4.0 %fusion.134 = f32[768,2304]{1,0:T(8,128)} fusion(bf16[2304,256]{1,0:T(8,128)(2,1)S(1)} %get-tuple-element.11, bf16[128,768]{1,0:T(8,128)(2,1)S(1)} %collective-permute-done.4, bf16[128,768]{1,0:T(8,128)(2,1)S(1)} %bitcast.84), kind=kOutput, calls=%fused_computation.261 | convolution fusion | flops 906756096 | bytes 8650752 | tf_op jit(solution)/shard_map/tc,jt->cj/dot_general | solution.py:272
  75.7 8.7 %pad_maximum_fusion = f32[768,3072]{1,0:T(8,128)} fusion(f32[768,768]{1,0:T(8,128)} %fusion.133, f32[768,2304]{1,0:T(8,128)} %fusion.134), kind=kLoop, calls=%fused_computation.24 | loop fusion | flops 2359296 | bytes 18874368 | tf_op jit(solution)/shard_map/concatenate | solution.py:278
  84.5 4.1 %fusion.6 = bf16[2,2,4,24,3072]{4,3,2,1,0:T(8,128)(2,1)} fusion(f32[2,2,4,2,24,3072]{5,4,3,2,1,0:T(8,128)} %bitcast.70, s32[]{:T(128)S(6)} %select_n.185), kind=kLoop, calls=%fused_computation.40 | loop fusion | bytes 4718596 | tf_op jit(solution)/shard_map/convert_element_type | solution.py:161
  92.4 2.4 %collective-permute-start.6 = (bf16[768,128]{1,0:T(8,128)(2,1)}, bf16[768,128]{1,0:T(8,128)(2,1)S(1)}, u32[]{:S(2)}, u32[]{:S(2)}) collective-permute-start(bf16[768,128]{1,0:T(8,128)(2,1)} %slice.444), channel_id=1, source_target_pairs={{0,7},{1,2},{2,1},{3,4},{4,3},{5,6},{6,5},{7,0},{8,15},{9,10},{10,... | collective-permute-start | bytes 589832 | tf_op jit(solution)/shard_map/ppermute | solution.py:26
  94.7 3.3 %fusion.10 = bf16[256,768]{1,0:T(8,128)(2,1)S(1)} fusion(bf16[2304,256]{1,0:T(8,128)(2,1)S(1)} %get-tuple-element.11, bf16[768,3072]{1,0:T(8,128)(2,1)} %copy-done.8), kind=kOutput, calls=%fused_computation.46 | convolution fusion | flops 906166272 | bytes 5111808 | tf_op jit(solution)/shard_map/jt,cj->tc/dot_general | solution.py:273
  102.8 2.6 %bitcast_add_fusion = f32[2,2,4,24,3072]{4,3,2,1,0:T(8,128)S(1)} fusion(bf16[2,2,4,24,3072]{4,3,2,1,0:T(8,128)(2,1)} %collective-permute-done.10, f32[2,2,4,2,24,3072]{5,4,3,2,1,0:T(8,128)S(1)} %bitcast.71, s32[]{:T(128)S(6)} %select_n.184), kind=kLoop, calls=%fused_computation.26 | loop fusion | flops 2359296 | bytes 11796484 | tf_op jit(solution)/shard_map/add | solution.py:162
  111.0 21.1 %collective-permute-done.11 = bf16[4,24,3072]{2,1,0:T(8,128)(2,1)S(1)} collective-permute-done((bf16[4,24,3072]{2,1,0:T(8,128)(2,1)S(1)}, bf16[4,24,3072]{2,1,0:T(8,128)(2,1)S(1)}, u32[]{:S(2)}, u32[]{:S(2)}) %collective-permute-start.11) | collective-permute-done | bytes 589856 | tf_op jit(solution)/shard_map/ppermute | solution.py:20
  138.9 4.2 %collective-permute-done.16 = bf16[1,24,3072]{2,1,0:T(8,128)(2,1)S(1)} collective-permute-done((bf16[1,24,3072]{2,1,0:T(8,128)(2,1)S(1)}, bf16[1,24,3072]{2,1,0:T(8,128)(2,1)S(1)}, u32[]{:S(2)}, u32[]{:S(2)}) %collective-permute-start.16) | collective-permute-done | bytes 147488 | tf_op jit(solution)/shard_map/ppermute | solution.py:20
  143.1 6.7 %collective-permute-done.15 = bf16[1,24,3072]{2,1,0:T(8,128)(2,1)S(1)} collective-permute-done((bf16[1,24,3072]{2,1,0:T(8,128)(2,1)S(1)}, bf16[1,24,3072]{2,1,0:T(8,128)(2,1)S(1)}, u32[]{:S(2)}, u32[]{:S(2)}) %collective-permute-start.15) | collective-permute-done | bytes 147488 | tf_op jit(solution)/shard_map/ppermute | solution.py:20
  149.9 2.3 %collective-permute-start.19 = (bf16[1,24,3072]{2,1,0:T(8,128)(2,1)S(1)}, bf16[1,24,3072]{2,1,0:T(8,128)(2,1)S(1)}, u32[]{:S(2)}, u32[]{:S(2)}) collective-permute-start(bf16[1,24,3072]{2,1,0:T(8,128)(2,1)S(1)} %add_convert_fusion), channel_id=1, source_target_pairs={{0,6},{1,7},{2,4},{3,5},{4,2},{5,3},{6,0},{7,1},{8,14},{9,15},{10,... | collective-permute-start | bytes 442376 | tf_op jit(solution)/shard_map/ppermute | solution.py:20
  152.2 2.1 %collective-permute-start.17 = (bf16[1,24,3072]{2,1,0:T(8,128)(2,1)S(1)}, bf16[1,24,3072]{2,1,0:T(8,128)(2,1)S(1)}, u32[]{:S(2)}, u32[]{:S(2)}) collective-permute-start(bf16[1,24,3072]{2,1,0:T(8,128)(2,1)S(1)} %add_convert_fusion), channel_id=1, source_target_pairs={{0,2},{1,3},{2,0},{3,1},{4,6},{5,7},{6,4},{7,5},{8,10},{9,11},{10,... | collective-permute-start | bytes 442376 | tf_op jit(solution)/shard_map/ppermute | solution.py:20
  154.3 2.6 %fusion.68 = (f32[768]{0:T(1024)S(1)}, f32[768]{0:T(1024)S(1)}, f32[768]{0:T(1024)S(1)}, f32[768]{0:T(1024)S(1)}, f32[768]{0:T(1024)S(1)}, /*index=5*/f32[768]{0...) fusion(bf16[4,10,18,768]{3,2,1,0:T(8,128)(2,1)S(1)} %select_max, ...), kind=kLoop, calls=%fused_computation.174 | loop fusion | flops 13158912 | bytes 9499648 | tf_op jit(solution)/shard_map/reduce_sum | solution.py:315
  158.5 5.0 %collective-permute-done.18 = bf16[1,24,3072]{2,1,0:T(8,128)(2,1)S(1)} collective-permute-done((bf16[1,24,3072]{2,1,0:T(8,128)(2,1)S(1)}, bf16[1,24,3072]{2,1,0:T(8,128)(2,1)S(1)}, u32[]{:S(2)}, u32[]{:S(2)}) %collective-permute-start.18) | collective-permute-done | bytes 147488 | tf_op jit(solution)/shard_map/ppermute | solution.py:20
  174.4 9.1 %collective-permute-done.25 = f32[29,768]{1,0:T(8,128)S(1)} collective-permute-done((f32[29,768]{1,0:T(8,128)S(1)}, f32[29,768]{1,0:T(8,128)S(1)}, u32[]{:S(2)}, u32[]{:S(2)}) %collective-permute-start.25) | collective-permute-done | bytes 89120 | tf_op jit(solution)/shard_map/ppermute | solution.py:20
  184.8 2.7 %collective-permute-start.28 = (f32[29,768]{1,0:T(8,128)S(1)}, f32[29,768]{1,0:T(8,128)S(1)}, u32[]{:S(2)}, u32[]{:S(2)}) collective-permute-start(f32[29,768]{1,0:T(8,128)S(1)} %add_add_fusion), channel_id=1, source_target_pairs={{0,6},{1,7},{2,4},{3,5},{4,2},{5,3},{6,0},{7,1},{8,14},{9,15},{10,... | collective-permute-start | bytes 267272 | tf_op jit(solution)/shard_map/ppermute | solution.py:20
  191.4 3.8 %fusion.132 = bf16[1,2,8,16,768]{4,3,2,1,0:T(8,128)(2,1)} fusion(f32[2,8,16,768]{3,2,1,0:T(8,128)S(1)} %get-tuple-element.76, f32[4,8,16,768]{3,2,1,0:T(8,128)S(1)} %maximum_convert_fusion, f32[768]{0:T(1024)S(1)} %get-tuple-element.74, f32[768]{0:T(1024)S(1)} %get-tuple-element.75, f32[768]{0:T(1024)S(1)} %get-tuple-element.50, ...), kind=kLoop, calls=%fused_computation.255 | loop fusion | flops 10813440 | bytes 5222400 | tf_op jit(solution)/shard_map/broadcast_in_dim | solution.py:322
  (227 shorter events, 61.4 us)
Async XLA Ops:
  5.8 29.1 %collective-permute-start.2 = (bf16[192,3072]{1,0:T(8,128)(2,1)S(1)}, bf16[192,3072]{1,0:T(8,128)(2,1)}, u32[]{:S(2)}, u32[]{:S(2)}) collective-permute-start(bf16[192,3072]{1,0:T(8,128)(2,1)S(1)} %constant_dynamic-slice_fusion), channel_id=1, source_target_pairs={{0,8},{8,0},{1,9},{9,1},{2,10},{10,2},{3,11},{11,3},{4,12},{12,4},... | collective-permute-start | bytes 3538952 | tf_op jit(solution)/shard_map/ppermute | solution.py:20
  34.9 9.3 %collective-permute-start.3 = (bf16[192,3072]{1,0:T(8,128)(2,1)}, bf16[192,3072]{1,0:T(8,128)(2,1)S(1)}, u32[]{:S(2)}, u32[]{:S(2)}) collective-permute-start(bf16[192,3072]{1,0:T(8,128)(2,1)} %collective-permute-done.2), channel_id=1, source_target_pairs={{0,1},{1,0},{2,3},{3,2},{4,5},{5,4},{6,7},{7,6},{8,9},{9,8},{10,11... | collective-permute-start | bytes 3538952 | tf_op jit(solution)/shard_map/ppermute | solution.py:20
  40.1 8.8 %collective-permute-start.5 = (bf16[128,768]{1,0:T(8,128)(2,1)S(1)}, bf16[128,768]{1,0:T(8,128)(2,1)S(1)}, u32[]{:S(2)}, u32[]{:S(2)}) collective-permute-start(bf16[128,768]{1,0:T(8,128)(2,1)S(1)} %bitcast.88), channel_id=1, source_target_pairs={{0,7},{1,2},{2,1},{3,4},{4,3},{5,6},{6,5},{7,0},{8,15},{9,10},{10,... | collective-permute-start | bytes 589832 | tf_op jit(solution)/shard_map/ppermute | solution.py:26
  44.1 9.1 %collective-permute-start.4 = (bf16[128,768]{1,0:T(8,128)(2,1)S(1)}, bf16[128,768]{1,0:T(8,128)(2,1)S(1)}, u32[]{:S(2)}, u32[]{:S(2)}) collective-permute-start(bf16[128,768]{1,0:T(8,128)(2,1)S(1)} %bitcast.87), channel_id=1, source_target_pairs={{0,7},{1,2},{2,1},{3,4},{4,3},{5,6},{6,5},{7,0},{8,15},{9,10},{10,... | collective-permute-start | bytes 589832 | tf_op jit(solution)/shard_map/ppermute | solution.py:26
  88.6 14.3 %collective-permute-start.10 = (bf16[2,2,4,24,3072]{4,3,2,1,0:T(8,128)(2,1)}, bf16[2,2,4,24,3072]{4,3,2,1,0:T(8,128)(2,1)}, u32[]{:S(2)}, u32[]{:S(2)}) collective-permute-start(bf16[2,2,4,24,3072]{4,3,2,1,0:T(8,128)(2,1)} %fusion.6), channel_id=1, source_target_pairs={{0,1},{1,0},{2,3},{3,2},{4,5},{5,4},{6,7},{7,6},{8,9},{9,8},{10,11... | collective-permute-start | bytes 7077896 | tf_op jit(solution)/shard_map/ppermute | solution.py:20
  92.4 8.8 %collective-permute-start.6 = (bf16[768,128]{1,0:T(8,128)(2,1)}, bf16[768,128]{1,0:T(8,128)(2,1)S(1)}, u32[]{:S(2)}, u32[]{:S(2)}) collective-permute-start(bf16[768,128]{1,0:T(8,128)(2,1)} %slice.444), channel_id=1, source_target_pairs={{0,7},{1,2},{2,1},{3,4},{4,3},{5,6},{6,5},{7,0},{8,15},{9,10},{10,... | collective-permute-start | bytes 589832 | tf_op jit(solution)/shard_map/ppermute | solution.py:26
  98.0 11.3 %collective-permute-start.7 = (bf16[128,768]{1,0:T(8,128)(2,1)S(1)}, bf16[128,768]{1,0:T(8,128)(2,1)S(1)}, u32[]{:S(2)}, u32[]{:S(2)}) collective-permute-start(bf16[128,768]{1,0:T(8,128)(2,1)S(1)} %get-tuple-element.108), channel_id=1, source_target_pairs={{0,7},{1,2},{2,1},{3,4},{4,3},{5,6},{6,5},{7,0},{8,15},{9,10},{10,... | collective-permute-start | bytes 589832 | tf_op jit(solution)/shard_map/ppermute | solution.py:26
  105.8 26.3 %collective-permute-start.11 = (bf16[4,24,3072]{2,1,0:T(8,128)(2,1)S(1)}, bf16[4,24,3072]{2,1,0:T(8,128)(2,1)S(1)}, u32[]{:S(2)}, u32[]{:S(2)}) collective-permute-start(bf16[4,24,3072]{2,1,0:T(8,128)(2,1)S(1)} %get-tuple-element.79), channel_id=1, source_target_pairs={{0,8},{8,0},{16,24},{24,16},{1,9},{9,1},{17,25},{25,17},{2,10},{10... | collective-permute-start | bytes 1769480 | tf_op jit(solution)/shard_map/ppermute | solution.py:20
  107.3 24.7 %collective-permute-start.13 = (bf16[4,24,3072]{2,1,0:T(8,128)(2,1)S(1)}, bf16[4,24,3072]{2,1,0:T(8,128)(2,1)S(1)}, u32[]{:S(2)}, u32[]{:S(2)}) collective-permute-start(bf16[4,24,3072]{2,1,0:T(8,128)(2,1)S(1)} %get-tuple-element.80), channel_id=1, source_target_pairs={{0,24},{8,16},{16,8},{24,0},{1,25},{9,17},{17,9},{25,1},{2,26},{10... | collective-permute-start | bytes 1769480 | tf_op jit(solution)/shard_map/ppermute | solution.py:20
  108.8 24.5 %collective-permute-start.12 = (bf16[4,24,3072]{2,1,0:T(8,128)(2,1)S(1)}, bf16[4,24,3072]{2,1,0:T(8,128)(2,1)S(1)}, u32[]{:S(2)}, u32[]{:S(2)}) collective-permute-start(bf16[4,24,3072]{2,1,0:T(8,128)(2,1)S(1)} %get-tuple-element.81), channel_id=1, source_target_pairs={{0,16},{8,24},{16,0},{24,8},{1,17},{9,25},{17,1},{25,9},{2,18},{10... | collective-permute-start | bytes 1769480 | tf_op jit(solution)/shard_map/ppermute | solution.py:20
  133.7 9.4 %collective-permute-start.16 = (bf16[1,24,3072]{2,1,0:T(8,128)(2,1)S(1)}, bf16[1,24,3072]{2,1,0:T(8,128)(2,1)S(1)}, u32[]{:S(2)}, u32[]{:S(2)}) collective-permute-start(bf16[1,24,3072]{2,1,0:T(8,128)(2,1)S(1)} %get-tuple-element.91), channel_id=1, source_target_pairs={{0,6},{1,7},{2,4},{3,5},{4,2},{5,3},{6,0},{7,1},{8,14},{9,15},{10,... | collective-permute-start | bytes 442376 | tf_op jit(solution)/shard_map/ppermute | solution.py:20
  135.2 14.6 %collective-permute-start.15 = (bf16[1,24,3072]{2,1,0:T(8,128)(2,1)S(1)}, bf16[1,24,3072]{2,1,0:T(8,128)(2,1)S(1)}, u32[]{:S(2)}, u32[]{:S(2)}) collective-permute-start(bf16[1,24,3072]{2,1,0:T(8,128)(2,1)S(1)} %get-tuple-element.92), channel_id=1, source_target_pairs={{0,4},{1,5},{2,6},{3,7},{4,0},{5,1},{6,2},{7,3},{8,12},{9,13},{10,... | collective-permute-start | bytes 442376 | tf_op jit(solution)/shard_map/ppermute | solution.py:20
  149.9 8.6 %collective-permute-start.19 = (bf16[1,24,3072]{2,1,0:T(8,128)(2,1)S(1)}, bf16[1,24,3072]{2,1,0:T(8,128)(2,1)S(1)}, u32[]{:S(2)}, u32[]{:S(2)}) collective-permute-start(bf16[1,24,3072]{2,1,0:T(8,128)(2,1)S(1)} %add_convert_fusion), channel_id=1, source_target_pairs={{0,6},{1,7},{2,4},{3,5},{4,2},{5,3},{6,0},{7,1},{8,14},{9,15},{10,... | collective-permute-start | bytes 442376 | tf_op jit(solution)/shard_map/ppermute | solution.py:20
  152.2 11.3 %collective-permute-start.18 = (bf16[1,24,3072]{2,1,0:T(8,128)(2,1)S(1)}, bf16[1,24,3072]{2,1,0:T(8,128)(2,1)S(1)}, u32[]{:S(2)}, u32[]{:S(2)}) collective-permute-start(bf16[1,24,3072]{2,1,0:T(8,128)(2,1)S(1)} %add_convert_fusion), channel_id=1, source_target_pairs={{0,4},{1,5},{2,6},{3,7},{4,0},{5,1},{6,2},{7,3},{8,12},{9,13},{10,... | collective-permute-start | bytes 442376 | tf_op jit(solution)/shard_map/ppermute | solution.py:20
  152.2 11.3 %collective-permute-start.17 = (bf16[1,24,3072]{2,1,0:T(8,128)(2,1)S(1)}, bf16[1,24,3072]{2,1,0:T(8,128)(2,1)S(1)}, u32[]{:S(2)}, u32[]{:S(2)}) collective-permute-start(bf16[1,24,3072]{2,1,0:T(8,128)(2,1)S(1)} %add_convert_fusion), channel_id=1, source_target_pairs={{0,2},{1,3},{2,0},{3,1},{4,6},{5,7},{6,4},{7,5},{8,10},{9,11},{10,... | collective-permute-start | bytes 442376 | tf_op jit(solution)/shard_map/ppermute | solution.py:20
  164.6 22.9 %collective-permute-start.20 = (bf16[4,24,3072]{2,1,0:T(8,128)(2,1)}, bf16[4,24,3072]{2,1,0:T(8,128)(2,1)}, u32[]{:S(2)}, u32[]{:S(2)}) collective-permute-start(bf16[4,24,3072]{2,1,0:T(8,128)(2,1)} %pad_maximum_fusion.5), channel_id=1, source_target_pairs={{0,16},{16,0},{1,17},{17,1},{2,18},{18,2},{3,19},{19,3},{4,20},{20... | collective-permute-start | bytes 1769480 | tf_op jit(solution)/shard_map/ppermute | solution.py:20
  169.5 14.0 %collective-permute-start.25 = (f32[29,768]{1,0:T(8,128)S(1)}, f32[29,768]{1,0:T(8,128)S(1)}, u32[]{:S(2)}, u32[]{:S(2)}) collective-permute-start(f32[29,768]{1,0:T(8,128)S(1)} %add.393), channel_id=1, source_target_pairs={{0,24},{8,16},{16,8},{24,0},{1,25},{9,17},{17,9},{25,1},{2,26},{10... | collective-permute-start | bytes 267272 | tf_op jit(solution)/shard_map/ppermute | solution.py:20
  171.1 13.7 %collective-permute-start.24 = (f32[29,768]{1,0:T(8,128)S(1)}, f32[29,768]{1,0:T(8,128)S(1)}, u32[]{:S(2)}, u32[]{:S(2)}) collective-permute-start(f32[29,768]{1,0:T(8,128)S(1)} %add.393), channel_id=1, source_target_pairs={{0,16},{8,24},{16,0},{24,8},{1,17},{9,25},{17,1},{25,9},{2,18},{10... | collective-permute-start | bytes 267272 | tf_op jit(solution)/shard_map/ppermute | solution.py:20
  172.5 12.2 %collective-permute-start.23 = (f32[29,768]{1,0:T(8,128)S(1)}, f32[29,768]{1,0:T(8,128)S(1)}, u32[]{:S(2)}, u32[]{:S(2)}) collective-permute-start(f32[29,768]{1,0:T(8,128)S(1)} %add.393), channel_id=1, source_target_pairs={{0,8},{8,0},{16,24},{24,16},{1,9},{9,1},{17,25},{25,17},{2,10},{10... | collective-permute-start | bytes 267272 | tf_op jit(solution)/shard_map/ppermute | solution.py:20
  173.0 17.6 %collective-permute-start.8 = (bf16[1,8,16,768]{3,2,1,0:T(8,128)(2,1)S(1)}, bf16[1,8,16,768]{3,2,1,0:T(8,128)(2,1)S(1)}, u32[]{:S(2)}, u32[]{:S(2)}) collective-permute-start(bf16[1,8,16,768]{3,2,1,0:T(8,128)(2,1)S(1)} %get-tuple-element.105), channel_id=1, source_target_pairs={{0,1},{1,2},{2,3},{3,4},{4,5},{5,6},{6,7},{8,9},{9,10},{10,11},{11... | collective-permute-start | bytes 589832 | tf_op jit(solution)/shard_map/ppermute | solution.py:33
  184.8 10.4 %collective-permute-start.28 = (f32[29,768]{1,0:T(8,128)S(1)}, f32[29,768]{1,0:T(8,128)S(1)}, u32[]{:S(2)}, u32[]{:S(2)}) collective-permute-start(f32[29,768]{1,0:T(8,128)S(1)} %add_add_fusion), channel_id=1, source_target_pairs={{0,6},{1,7},{2,4},{3,5},{4,2},{5,3},{6,0},{7,1},{8,14},{9,15},{10,... | collective-permute-start | bytes 267272 | tf_op jit(solution)/shard_map/ppermute | solution.py:20
  187.5 9.7 %collective-permute-start.27 = (f32[29,768]{1,0:T(8,128)S(1)}, f32[29,768]{1,0:T(8,128)S(1)}, u32[]{:S(2)}, u32[]{:S(2)}) collective-permute-start(f32[29,768]{1,0:T(8,128)S(1)} %add_add_fusion), channel_id=1, source_target_pairs={{0,4},{1,5},{2,6},{3,7},{4,0},{5,1},{6,2},{7,3},{8,12},{9,13},{10,... | collective-permute-start | bytes 267272 | tf_op jit(solution)/shard_map/ppermute | solution.py:20
  187.5 9.7 %collective-permute-start.26 = (f32[29,768]{1,0:T(8,128)S(1)}, f32[29,768]{1,0:T(8,128)S(1)}, u32[]{:S(2)}, u32[]{:S(2)}) collective-permute-start(f32[29,768]{1,0:T(8,128)S(1)} %add_add_fusion), channel_id=1, source_target_pairs={{0,2},{1,3},{2,0},{3,1},{4,6},{5,7},{6,4},{7,5},{8,10},{9,11},{10,... | collective-permute-start | bytes 267272 | tf_op jit(solution)/shard_map/ppermute | solution.py:20
  190.7 7.7 %collective-permute-start.21 = (bf16[2,4,24,3072]{3,2,1,0:T(8,128)(2,1)S(1)}, bf16[2,4,24,3072]{3,2,1,0:T(8,128)(2,1)S(1)}, u32[]{:S(2)}, u32[]{:S(2)}) collective-permute-start(bf16[2,4,24,3072]{3,2,1,0:T(8,128)(2,1)S(1)} %pad_maximum_fusion.3), channel_id=1, source_target_pairs={{0,1},{1,0},{2,3},{3,2},{4,5},{5,4},{6,7},{7,6},{8,9},{9,8},{10,11... | collective-permute-start | bytes 3538952 | tf_op jit(solution)/shard_map/ppermute | solution.py:20
  (56 other events, 562.3 us)

commit v2 on v1

v2 whole, which is shorter than its diff:
```python
import functools
import math

import jax
import jax.numpy as jnp
from jax import lax
from jax.experimental import pallas as pl
from jax.experimental.pallas import tpu as pltpu
from jax.sharding import PartitionSpec as P

HALF = 8
BF = jnp.bfloat16
F32 = jnp.float32


def busy(microseconds, megabytes):
    return pl.CostEstimate(
        flops=int(microseconds * 0.5e8), bytes_accessed=int(megabytes * 0.6e6), transcendentals=0
    )


def swapped(x, axis, flip):
    count = 1
    for name in (axis,) if isinstance(axis, str) else axis:
        count = count * lax.axis_size(name)
    return lax.ppermute(x, axis, [(i, i ^ flip) for i in range(count)])


def window_partner(x):
    count = lax.axis_size("seq")
    pairs = [(i, (i + 1) % count if i % 2 else (i - 1) % count) for i in range(count)]
    return lax.ppermute(x, "seq", pairs)


def edge_partner(x):
    count = lax.axis_size("seq")
    pairs = [(i, i + 1) for i in range(1, count - 1, 2)]
    return lax.ppermute(x, "seq", pairs + [(j, i) for i, j in pairs])


def with_halo(x, inner, outer, core):
    low = core == 0
    return jnp.concatenate(
        [jnp.where(low, outer, inner)[None], x, jnp.where(low, inner, outer)[None]], axis=0
    )


def tap_sum(padded, weight, slab_depth, height, grid_width, flipped):
    summed = jnp.zeros((slab_depth, height, grid_width, padded.shape[-1]), F32)
    for a in range(3):
        for b in range(3):
            for e in range(3):
                starts = (2 - a, 2 - b, 2 - e) if flipped else (a, b, e)
                part = padded[
                    starts[0] : starts[0] + slab_depth,
                    starts[1] : starts[1] + height,
                    starts[2] : starts[2] + grid_width,
                ]
                summed = summed + weight[9 * a + 3 * b + e] * part.astype(F32)
    return summed


OVER_ROWS = (((0,), (0,)), ((), ()))
OVER_LANES = (((1,), (1,)), ((), ()))


def allowed_pairs(nums, n):
    rows_shift, cols_shift, second = nums[0], nums[1], nums[2]

    def code(dim):
        t = lax.broadcasted_iota(jnp.int32, (n, n), dim)
        first_bit = jnp.where(((t >> 3) & 7) < rows_shift, 2, 0)
        return first_bit + jnp.where((t & 7) < cols_shift, second, 0)

    return jnp.where(code(0) == code(1), 1.0, 0.0).astype(F32)


def project(nums, x, mine, low, got, other, group, qkv):
    channels = x.shape[1]
    half = channels // 2
    quarter = half // 2
    low_rows, low_core = nums[3] == 0, nums[4] == 0
    x = x.astype(F32)
    x_mine = jnp.where(low_rows, x[:, :half], x[:, half:])
    x_peer = jnp.where(low_rows, x[:, half:], x[:, :half])
    x_got = jnp.where(low_core, x_peer[:, :quarter], x_peer[:, quarter:]).astype(BF)
    x_other = jnp.where(low_core, x_peer[:, quarter:], x_peer[:, :quarter]).astype(BF)
    x_mine = x_mine.astype(BF)
    for part in range(3):
        own = slice(part * channels + low, part * channels + low + group)
        far = slice(own.start + channels, own.stop + channels)
        total = jnp.dot(x_mine, mine[:, own], preferred_element_type=F32)
        total = total + jnp.dot(x_got, got[:, far], preferred_element_type=F32)
        total = total + jnp.dot(x_other, other[:, far], preferred_element_type=F32)
        qkv[part * group : (part + 1) * group, :] = total.T.astype(BF)


def attend(head_dim, allowed, scale, base, group, qkv, ba, ba_low, att, back, gs):
    def unit(raw):
        inverse = lax.rsqrt(jnp.sum(raw * raw, axis=0, keepdims=True) + 1.0)
        return inverse, (raw * inverse).astype(BF)

    def radius_back(raw, inverse, grad):
        inner = jnp.sum(raw * grad, axis=0, keepdims=True)
        return grad * inverse - raw * (inner * (inverse * inverse * inverse))

    def one_head(h):
        def rows(start):
            return pl.ds(pl.multiple_of(start + h * head_dim, head_dim), head_dim)

        s = scale[base + h]
        qf = qkv[rows(0), :].astype(F32)
        kf = qkv[rows(group), :].astype(F32)
        v = qkv[rows(2 * group), :]
        b = ba[rows(ba_low), :]
        iq, uq = unit(qf)
        ik, uk = unit(kf)
        cosine = lax.dot_general(uk, uq, OVER_ROWS, preferred_element_type=F32)
        expo = jnp.exp(cosine * s) * allowed
        prob = expo * (1.0 / jnp.sum(expo, axis=0, keepdims=True))
        weights = prob.astype(BF)
        att[rows(0), :] = jnp.dot(v, weights, preferred_element_type=F32).astype(BF)
        back_prob = lax.dot_general(v, b, OVER_ROWS, preferred_element_type=F32)
        mean = jnp.sum(prob * back_prob, axis=0, keepdims=True)
        back_score = prob * (back_prob - mean)
        gs[pl.ds(h, 1), :] = jnp.sum(back_score * cosine, axis=0, keepdims=True)
        scaled = (back_score * s).astype(BF)
        buq = jnp.dot(uk, scaled, preferred_element_type=F32)
        buk = lax.dot_general(uq, scaled, OVER_LANES, preferred_element_type=F32)
        bv = lax.dot_general(b, weights, OVER_LANES, preferred_element_type=F32)
        back[rows(0), :] = radius_back(qf, iq, buq).astype(BF)
        back[rows(group), :] = radius_back(kf, ik, buk).astype(BF)
        back[rows(2 * group), :] = bv.astype(BF)

    def body(i, carry):
        for u in range(4):
            one_head(i * 4 + u)
        return carry

    lax.fori_loop(0, group // head_dim // 4, body, 0)


def first_kernel(group, head_dim, nums, scale, xm, xg, cot, order, w_qkv, w_proj, got, other, *outs):
    send, x_rows, att, ba, gs, qkv = outs
    channels = xm.shape[1]
    half = channels // 2
    x = jnp.concatenate([xm[...], xg[...]], axis=0)
    project(nums, x, w_qkv, 0, got, other, group, qkv)
    quarter = half // 2
    dp, core = nums[3], nums[4]

    def back_rows(start, count, weight):
        value = lax.dot_general(weight, cot[...], OVER_LANES, preferred_element_type=F32)
        ba[pl.ds(pl.multiple_of(start, quarter), count), :] = value.astype(BF)

    back_rows(dp * half, half, w_proj[...])
    back_rows((1 - dp) * half + core * quarter, quarter, got[:, :channels])
    back_rows((1 - dp) * half + (1 - core) * quarter, quarter, other[:, :channels])
    allowed = allowed_pairs(nums, x.shape[0])
    attend(head_dim, allowed, scale, 0, group, qkv, ba, 0, att, send, gs)
    x_rows[...] = lax.dot_general(
        order[:half, :], x, OVER_LANES, preferred_element_type=F32
    ).astype(BF)
    send[3 * group :, :] = lax.dot_general(
        order[half:, :], x, OVER_LANES, preferred_element_type=F32
    ).astype(BF)


def second_kernel(group, head_dim, nums, scale, xm, xg, order, w_qkv, got, other, ba, att_first, *outs):
    send, att_rows, att, gs, qkv = outs
    channels = xm.shape[1]
    half = channels // 2
    low = channels - group
    x = jnp.concatenate([xm[...], xg[...]], axis=0)
    project(nums, x, w_qkv, low, got, other, group, qkv)
    allowed = allowed_pairs(nums, x.shape[0])
    attend(head_dim, allowed, scale, low // head_dim, group, qkv, ba, low, att, send, gs)

    def ordered(rows):
        total = jnp.dot(order[rows, :low], att_first[...], preferred_element_type=F32)
        total = total + jnp.dot(order[rows, low:], att[...], preferred_element_type=F32)
        return total.astype(BF)

    att_rows[...] = ordered(slice(0, half))
    send[3 * group :, :] = ordered(slice(half, channels))


def attention_call(body, name, group, head_dim, head_count, outs, operands):
    n = 2 * operands[2].shape[0]
    channels = operands[2].shape[1]
    vmem = pl.BlockSpec(memory_space=pltpu.VMEM)
    smem = pl.BlockSpec(memory_space=pltpu.SMEM)
    shapes = tuple(jax.ShapeDtypeStruct((rows, n), BF) for rows in outs)
    shapes = shapes + (jax.ShapeDtypeStruct((group // head_dim, n), F32),)
    return pl.pallas_call(
        functools.partial(body, group, head_dim),
        out_shape=shapes,
        in_specs=[smem, smem] + [vmem] * (len(operands) - 2),
        out_specs=(vmem,) * len(shapes),
        scratch_shapes=[pltpu.VMEM((3 * group, n), BF)],
        compiler_params=pltpu.CompilerParams(vmem_limit_bytes=20 * 1024 * 1024),
        cost_estimate=busy(5 + 0.5 * (group // head_dim), 8),
        name=name,
    )(*operands)


def stage_kernel(core, w_qkv, w_proj, tokens, weights, inner, outer, sems):
    rows, channels = weights.shape[0], w_proj.shape[1]
    mine = pl.ds(pl.multiple_of(core[0] * rows, rows), rows)
    copies = (
        (w_proj.at[mine, :], weights.at[:, :channels]),
        (w_qkv.at[mine, :], weights.at[:, channels:]),
        (tokens.at[0, core[0]], outer),
        (tokens.at[0, 1 - core[0]], inner),
    )
    started = [pltpu.make_async_copy(x, y, sems.at[i]) for i, (x, y) in enumerate(copies)]
    for copy in started:
        copy.start()
    for copy in started:
        copy.wait()


def stage(core, w_qkv, w_proj, tokens):
    channels = w_proj.shape[1]
    rows = w_proj.shape[0] // 2
    anywhere = pl.BlockSpec(memory_space=pl.ANY)
    vmem = pl.BlockSpec(memory_space=pltpu.VMEM)
    plane = jax.ShapeDtypeStruct(tokens.shape[2:], BF)
    return pl.pallas_call(
        stage_kernel,
        out_shape=(jax.ShapeDtypeStruct((rows, 4 * channels), BF), plane, plane),
        in_specs=[pl.BlockSpec(memory_space=pltpu.SMEM)] + [anywhere] * 3,
        out_specs=(vmem,) * 3,
        scratch_shapes=[pltpu.SemaphoreType.DMA((4,))],
        cost_estimate=busy(2.5, 4),
        name="stage",
    )(core[None].astype(jnp.int32), w_qkv, w_proj, tokens)


def back_kernel(group, nums, first, second, w_qkv, got, other, att1, att2, *outs):
    mine, send, att_mine = outs
    n = first.shape[1]
    half = n // 2
    channels = att_mine.shape[1]
    rest = channels - group
    low_rows, low_core = nums[3] == 0, nums[4] == 0
    first_t = first[: 3 * group, :].astype(F32).T.astype(BF)
    second_t = second[: 3 * rest, :].astype(F32).T.astype(BF)

    def through(pieces):
        total = None
        for left, right in pieces:
            term = lax.dot_general(left, right, OVER_LANES, preferred_element_type=F32)
            total = term if total is None else total + term
        return total

    def pieces(weight, base):
        for part in range(3):
            low = base + part * channels
            yield first_t[:, part * group : (part + 1) * group], weight[:, low : low + group]
            yield second_t[:, part * rest : (part + 1) * rest], weight[:, low + group : low + channels]

    from_mine = through(pieces(w_qkv, 0))
    from_got = through(pieces(got, channels))
    from_other = through(pieces(other, channels))
    from_peer = jnp.concatenate(
        [jnp.where(low_core, from_got, from_other), jnp.where(low_core, from_other, from_got)], axis=1
    )
    shifted = jnp.concatenate(
        [jnp.where(low_rows, from_mine, from_peer), jnp.where(low_rows, from_peer, from_mine)], axis=1
    ).astype(BF)
    mine[...] = shifted[:half]
    send[:half, :] = shifted[half:]
    for low, ref in ((0, att1), (group, att2)):
        wide = slice(low, low + ref.shape[0])
        turned = ref[...].astype(F32).T.astype(BF)
        att_mine[:, wide] = turned[:half]
        send[half:, wide] = turned[half:]


def back_through(group, operands):
    n = operands[1].shape[1]
    channels = operands[6].shape[0] + operands[7].shape[0]
    vmem = pl.BlockSpec(memory_space=pltpu.VMEM)
    smem = pl.BlockSpec(memory_space=pltpu.SMEM)
    half = jax.ShapeDtypeStruct((n // 2, channels), BF)
    return pl.pallas_call(
        functools.partial(back_kernel, group),
        out_shape=(half, jax.ShapeDtypeStruct((n, channels), BF), half),
        in_specs=[smem] + [vmem] * (len(operands) - 1),
        out_specs=(vmem,) * 3,
        compiler_params=pltpu.CompilerParams(vmem_limit_bytes=20 * 1024 * 1024),
        cost_estimate=busy(4, 8),
        name="back_through",
    )(*operands)


def after(x, *others):
    anywhere = pl.BlockSpec(memory_space=pl.ANY)

    def nothing(*refs):
        del refs

    return pl.pallas_call(
        nothing,
        out_shape=jax.ShapeDtypeStruct(x.shape, x.dtype),
        in_specs=[anywhere] * (1 + len(others)),
        out_specs=anywhere,
        input_output_aliases={0: 0},
        name="ordered",
    )(x, *others)


def pick(x, index, axis):
    return lax.dynamic_index_in_dim(x, index, axis, keepdims=False)


def tree_sum(parts):
    while len(parts) > 1:
        parts = [a + b for a, b in zip(parts[::2], parts[1::2])]
    return parts[0]


def chip_stages(chips):
    stages = []
    stride = 1
    while stride < chips:
        radix = 4 if (chips // stride) % 4 == 0 else 2
        stages.append((radix, stride))
        stride = stride * radix
    return stages


class Place:
    def __init__(self, channels):
        self.seq = lax.axis_index("seq")
        self.core = self.seq % 2
        self.rep, self.dp = lax.axis_index("rep"), lax.axis_index("dp")
        self.stages = chip_stages(lax.axis_size("seq") // 2)
        self.split = self.stages[0][0] if self.stages else 1
        self.digit = (self.seq // 2) % self.split
        self.rows = channels // (8 * self.split)
        self.channels = channels

    def row_order(self):
        p = jnp.arange(self.channels)
        inner = p % self.rows
        z = (p // self.rows) % self.split
        square = (p // (self.rows * self.split)) % 4
        pair = p // (self.rows * self.split * 4)
        rep, dp = self.rep ^ (square >> 1), self.dp ^ (square & 1)
        target = ((dp * 2 + (self.core ^ pair)) * 2 + rep) * self.split + (self.digit ^ z)
        target = target * self.rows + inner
        return (target[:, None] == jnp.arange(self.channels)[None, :]).astype(BF)


def gradient_kernel(width, has_proj, *refs):
    if has_proj:
        xm, xg, bm, bg, am, cm, cg, own, s1, s2, s3 = refs
    else:
        xm, xg, bm, bg, own, s1, s2, s3 = refs
    quarter = own.shape[0]
    tile = 384
    x_far = xg[xg.shape[0] - 4 * quarter :, :]

    def put(first, total):
        columns = slice(first, first + tile)
        own[:, columns] = total[:quarter]
        for k, ref in enumerate((s1, s2, s3)):
            ref[:, columns] = total[(k + 1) * quarter : (k + 2) * quarter].astype(BF)

    for first in range(0, width, tile):
        rows = slice(first, first + tile)
        total = lax.dot_general(xm[...], bm[rows, :], OVER_LANES, preferred_element_type=F32)
        put(first, total + lax.dot_general(x_far, bg[rows, :], OVER_LANES, preferred_element_type=F32))
    if has_proj:
        far = bg[width:, :]
        for first in range(0, cm.shape[1], tile):
            columns = slice(first, first + tile)
            total = jnp.dot(am[...], cm[:, columns], preferred_element_type=F32)
            put(width + first, total + jnp.dot(far, cg[:, columns], preferred_element_type=F32))


def chip_gradient(operands):
    rows, n = operands[0].shape
    width = operands[2].shape[0] - rows
    has_proj = len(operands) > 4
    total = width + (operands[5].shape[1] if has_proj else 0)
    vmem = pl.BlockSpec(memory_space=pltpu.VMEM)
    wire = jax.ShapeDtypeStruct((rows // 4, total), BF)
    return pl.pallas_call(
        functools.partial(gradient_kernel, width, has_proj),
        out_shape=(jax.ShapeDtypeStruct((rows // 4, total), F32), wire, wire, wire),
        in_specs=[vmem] * len(operands),
        out_specs=(vmem,) * 4,
        compiler_params=pltpu.CompilerParams(vmem_limit_bytes=16 * 1024 * 1024),
        cost_estimate=busy(1.5, 3.5),
        name="chip_gradient",
    )(*operands)


def sum_square(own, sends, place):
    got = [own] + [swapped(s, ("rep", "dp"), k + 1).astype(F32) for k, s in enumerate(sends)]
    return tree_sum(got)


def sum_chips(total, place, *others):
    parts = total.reshape(place.split, place.rows, -1)
    got = [parts[0]]
    for k in range(1, place.split):
        there = swapped(parts[k].astype(BF), "seq", 2 * k)
        got.append((after(there, *others) if others else there).astype(F32))
    total = tree_sum(got)
    for radix, stride in place.stages[1:]:
        held = total.astype(BF)
        got = [swapped(held, "seq", 2 * k * stride) if k else held for k in range(radix)]
        total = tree_sum([g.astype(F32) for g in got])
    return total.astype(BF)


def gather_blocks(block, place):
    got = [swapped(block, "seq", 2 * k) if k else block for k in range(place.split)]
    chips = jnp.concatenate(got)
    other_rep = swapped(chips, "rep", 1)
    return chips, other_rep, swapped(chips, "seq", 1), swapped(other_rep, "seq", 1)


def assemble_kernel(split, factor, group, at, *refs):
    first, second = refs[:4], refs[4:8]
    qkv, proj = refs[8], refs[9]
    rows = first[0].shape[0] // split
    third = qkv.shape[1] // 3
    rest = third - group
    for pair in range(2):
        for square in range(2):
            index = 2 * pair + square
            base = ((at[0] ^ pair) * 2 + (at[1] ^ square)) * split
            for z in range(split):
                here = slice(z * rows, (z + 1) * rows)
                there = pl.ds(pl.multiple_of((base + (at[2] ^ z)) * rows, rows), rows)
                for part in range(3):
                    low, mid = part * third, part * third + group
                    a = first[index][here, part * group : (part + 1) * group]
                    qkv[there, low:mid] = a.astype(F32) * factor
                    b = second[index][here, part * rest : (part + 1) * rest]
                    qkv[there, mid : low + third] = b.astype(F32) * factor
                proj[there, :] = second[index][here, 3 * rest :].astype(F32) * factor


def assemble(first, second, place, factor, group):
    rows = 4 * first[0].shape[0]
    channels = place.channels
    vmem = pl.BlockSpec(memory_space=pltpu.VMEM)
    smem = pl.BlockSpec(memory_space=pltpu.SMEM)
    at = jnp.stack([place.core, place.rep, place.digit]).astype(jnp.int32)
    return pl.pallas_call(
        functools.partial(assemble_kernel, place.split, factor, group),
        out_shape=(
            jax.ShapeDtypeStruct((rows, 3 * channels), F32),
            jax.ShapeDtypeStruct((rows, channels), F32),
        ),
        in_specs=[smem] + [vmem] * 8,
        out_specs=(vmem, vmem),
        compiler_params=pltpu.CompilerParams(vmem_limit_bytes=16 * 1024 * 1024),
        cost_estimate=busy(3, 7),
        name="assemble",
    )(at, *first, *second)


def sum_everywhere(x, place):
    half = x.shape[0] // 2
    low = place.core == 0
    x = jnp.where(low, x[:half], x[half:]) + swapped(
        jnp.where(low, x[half:], x[:half]), "seq", 1
    )
    x = x + swapped(x, "rep", 1)
    x = x + swapped(x, "dp", 1)
    flip = 2
    while flip < lax.axis_size("seq"):
        x = x + swapped(x, "seq", flip)
        flip = flip * 2
    got = swapped(x, "seq", 1)
    return jnp.concatenate([jnp.where(low, x, got), jnp.where(low, got, x)])


def rows_of_both(mine, got, other, place):
    half = got.shape[0]
    m0, m1 = mine[:half], mine[half:]
    p0 = jnp.where(place.core == 0, got, other)
    p1 = jnp.where(place.core == 0, other, got)
    low = place.dp == 0
    return jnp.concatenate(
        [jnp.where(low, a, b) for a, b in ((m0, p0), (m1, p1), (p0, m0), (p1, m1))]
    )


GROUP_HEADS = 16


def tap_gradient_kernel(bm, tokens, back, unit, scale, out):
    depth, height, width, lanes = bm.shape
    mixed = bm[...]
    zero = jnp.zeros((1, lanes), F32)
    for e in range(3):
        shifted = tokens[:, :, e : e + width, :].astype(F32)
        for a in range(3):
            for b in range(3):
                product = mixed * shifted[a : a + depth, b : b + height]
                row = jnp.sum(jnp.sum(product, axis=(0, 1)), axis=0, keepdims=True)
                out[9 * a + 3 * b + e : 9 * a + 3 * b + e + 1, :] = row
    gain = jnp.sum(jnp.sum(back[...].astype(F32) * unit[...], axis=(0, 1)), axis=0, keepdims=True)
    out[27:28, :] = gain
    sums = jnp.sum(scale[...], axis=1, keepdims=True)
    heads = sums.shape[0]
    same = lax.broadcasted_iota(jnp.int32, (heads, lanes), 0) == lax.broadcasted_iota(
        jnp.int32, (heads, lanes), 1
    )
    out[28:29, :] = jnp.sum(jnp.where(same, sums, 0.0), axis=0, keepdims=True)
    for row in range(29, 32):
        out[row : row + 1, :] = zero


def small_gradients(bm, padded, back, unit, scale):
    depth, height, width, channels = bm.shape
    tile = 128

    def field(x):
        return pl.BlockSpec(x.shape[:-1] + (tile,), lambda i: (0, 0, 0, i))

    return pl.pallas_call(
        tap_gradient_kernel,
        grid=(channels // tile,),
        out_shape=jax.ShapeDtypeStruct((32, channels), F32),
        in_specs=[
            field(bm),
            field(padded),
            field(back),
            field(unit),
            pl.BlockSpec(scale.shape, lambda i: (0, 0)),
        ],
        out_specs=pl.BlockSpec((32, tile), lambda i: (0, i)),
        compiler_params=pltpu.CompilerParams(vmem_limit_bytes=16 * 1024 * 1024),
        cost_estimate=busy(3.5, 3),
        name="small_gradients",
    )(bm, padded, back, unit, scale)


def per_device(tokens, cotangent, w_qkv, w_proj, conv_weight, norm_gain, head_scale, shift_offsets):
    slab = tokens[0]
    cot = cotangent[0]
    depth, height, width, channels = slab.shape
    head_count = head_scale.shape[0]
    head_dim = channels // head_count
    place = Place(channels)
    core, dp = place.core, place.dp
    rows_shift, cols_shift = shift_offsets[0], shift_offsets[1]
    positions = depth * height * width
    half = positions // 2
    columns = jnp.arange(HALF)[None, None, :, None]
    straight = (columns >= cols_shift) == (core == 1)
    group = GROUP_HEADS * head_dim

    def split_columns(field):
        low, high = field[:, :, :HALF], field[:, :, HALF:]
        return (
            jnp.where(straight, low, high).reshape(half, -1),
            jnp.where(straight, high, low).reshape(half, -1),
        )

    def join_columns(mine, theirs):
        mine = mine.reshape(depth, height, HALF, -1)
        theirs = theirs.reshape(depth, height, HALF, -1)
        return jnp.concatenate(
            [jnp.where(straight, mine, theirs), jnp.where(straight, theirs, mine)], axis=2
        )

    spatial = ((0, 0), (1, 1), (1, 1), (0, 0))
    weights_part, inner, outer = stage(core, w_qkv, w_proj, tokens)
    outer = edge_partner(outer)
    inner = swapped(inner, "seq", 1)
    weights_got = swapped(weights_part, "dp", 1)
    cot_mine, cot_theirs = split_columns(cot)
    cot_got = window_partner(cot_theirs)
    padded_tokens = jnp.pad(with_halo(slab, inner, after(outer, cot_got), core), spatial)
    cot_window = jnp.concatenate([cot_mine, cot_got])
    order = place.row_order()

    mixed_field = slab.astype(F32) + tap_sum(
        padded_tokens, conv_weight, depth, height, width, False
    )
    centred = mixed_field - jnp.mean(mixed_field, axis=-1, keepdims=True)
    inverse_std = lax.rsqrt(jnp.mean(centred * centred, axis=-1, keepdims=True) + 1e-05)
    unit_field = centred * inverse_std
    normed = (unit_field * norm_gain).astype(BF)
    x_mine, x_theirs = split_columns(normed)
    x_theirs = window_partner(x_theirs)
    weights_got = after(weights_got, x_theirs)
    weights_other = swapped(weights_got, "seq", 1)
    cot_other = swapped(cot_window, "seq", 1)
    nums = jnp.stack([rows_shift, cols_shift, 1 - core, dp, core]).astype(jnp.int32)
    half_rows = channels // 2
    send_first, x_rows, att_first, back_attended, scale_first = attention_call(
        first_kernel,
        "first_heads",
        group,
        head_dim,
        head_count,
        (3 * group + half_rows, half_rows, group, channels),
        (nums, head_scale, x_mine, x_theirs, cot_window, order, w_qkv, w_proj, weights_got, weights_other),
    )
    got_first = swapped(send_first, "seq", 1)
    own, *sends = chip_gradient((x_rows, got_first, send_first, got_first))
    rest = channels - group
    send_second, att_rows, att_second, scale_second = attention_call(
        second_kernel,
        "second_heads",
        rest,
        head_dim,
        head_count,
        (3 * rest + half_rows, half_rows, rest),
        (
            nums,
            head_scale,
            x_mine,
            x_theirs,
            order,
            w_qkv,
            weights_got,
            weights_other,
            after(back_attended, own),
            att_first,
        ),
    )
    first_total = sum_square(own, sends, place)

    got_second = swapped(send_second, "seq", 1)
    own, *sends = chip_gradient(
        (x_rows, got_first, send_second, got_second, att_rows, cot_window, cot_other)
    )
    second_total = sum_square(own, sends, place)
    first_block = sum_chips(first_total, place, own)
    second_block = sum_chips(second_total, place)
    factor = 1.0 / math.sqrt(
        lax.axis_size("rep") * lax.axis_size("dp") * lax.axis_size("seq") * positions
    )
    grad_qkv, grad_proj = assemble(
        gather_blocks(first_block, place), gather_blocks(second_block, place), place, factor, group
    )

    back_mine, window_send, att_mine = back_through(
        group,
        (
            nums,
            send_first,
            send_second,
            w_qkv,
            weights_got,
            weights_other,
            att_first,
            att_second,
        ),
    )
    window_send = after(window_partner(window_send), own, first_total)
    back_normed = join_columns(back_mine, window_send[:half])
    restored = join_columns(att_mine, window_send[half:]).reshape(positions, channels)
    full_proj = rows_of_both(
        w_proj, weights_got[:, :channels], weights_other[:, :channels], place
    )
    projected = jnp.dot(restored, full_proj, preferred_element_type=F32)
    output = (mixed_field + projected.reshape(slab.shape)).astype(BF)

    back_float = back_normed.astype(F32)
    grad_unit = back_float * norm_gain
    back_mixed = cot.astype(F32) + inverse_std * (
        grad_unit
        - jnp.mean(grad_unit, axis=-1, keepdims=True)
        - unit_field * jnp.mean(grad_unit * unit_field, axis=-1, keepdims=True)
    )
    edges = back_mixed.astype(BF)
    inner = swapped(pick(edges, 1 - core, 0), "seq", 1)
    outer = edge_partner(pick(edges, core, 0))
    padded_back = jnp.pad(
        with_halo(back_mixed, inner.astype(F32), outer.astype(F32), core), spatial
    )
    grad_tokens = (
        back_mixed + tap_sum(padded_back, conv_weight, depth, height, width, True)
    ).astype(BF)
    scale_rows = jnp.concatenate([scale_first, scale_second])
    small = small_gradients(back_mixed, padded_tokens, back_normed, unit_field, scale_rows)
    small = sum_everywhere(after(small, second_total), place) * factor
    taps = conv_weight.shape[0]
    return (
        output[None],
        grad_tokens[None],
        grad_qkv,
        grad_proj,
        small[:taps],
        small[taps],
        small[taps + 1, :head_count],
    )


def solution(mesh):
    block = P(("rep", "dp"), "seq", None, None, None)
    rows = P("dp", None)
    return jax.shard_map(
        per_device,
        mesh=mesh,
        in_specs=(block, block, rows, rows, P(), P(), P(), P()),
        out_specs=(block, block, rows, rows, P(), P(), P()),
        check_vma=False,
    )
```

time: 203 us -> 174 us (0.86)
  waiting for transfers between devices: 83 us -> 33.7 us
  Pallas kernels: 15.5 us -> 42.4 us
  starting transfers between devices: 37.5 us -> 51.9 us
  matrix products: 12.8 us -> 1.23 us
  other arithmetic: 32.8 us -> 26.1 us
  local copies, waits for them, and re-layouts: 18.9 us -> 16.2 us
    ppermute x21 -> x37, waiting for transfers between devices: 72.9 us -> 25.7 us  [swapped(): return lax.ppermute(x, axis, [(i, i ^ flip) for i in range(count)])]
    pallas_call x1 -> x16, Pallas kernels: 15.5 us -> 42.4 us  [the longest x2 22.3 us: attention_call(): pl.pallas_call(functools.partial(body, group, head_dim), out_shape=shapes...]
    ppermute x21 -> x37, starting transfers between devices: 24.5 us -> 39.9 us  [swapped(): return lax.ppermute(x, axis, [(i, i ^ flip) for i in range(count)])]
    dot_general x7 -> x1, matrix products: 12.8 us -> 1.23 us  [per_device(): projected = jnp.dot(restored, full_proj, preferred_element_type=F32)]
    unnamed x103 -> x152, local copies, waits for them, and re-layouts: 4.08 us -> 12.4 us
    concatenate x4 -> x7, other arithmetic: 10.5 us -> 3.4 us  [the longest x1 1.48 us: per_device(): cot_window = jnp.concatenate([cot_mine, cot_got])]
    reduce_sum x4 -> x1, other arithmetic: 5.22 us -> 0.22 us  [per_device(): jnp.mean(grad_unit, axis=-1, keepdims=True)]
    convert_element_type x3 -> x0, local copies, waits for them, and re-layouts: 4.39 us -> none  [the longest x1 4.08 us: scatter_sum(): other = swapped(pick(parts, 1 - core, 3).astype(BF), 'seq', 1)]
  transfers between devices with their start and end apart: 29 -> 42, of which waited for: 15 -> 11; matrix products, arithmetic and copies ran while one was open for 16% -> 18% of each run, Pallas kernels for 0% -> 13%
where the time goes in v2:
time: 174 us; the launch traced here: 173 us
  starting transfers between devices  51.9 us (30%)
  Pallas kernels  42.4 us (24%)
  waiting for transfers between devices  33.7 us (19%)
  other arithmetic  26.1 us (15%)
  local copies, waits for them, and re-layouts  16.2 us (9%)
    ppermute x37, starting transfers between devices, swapped(): return lax.ppermute(x, axis, [(i, i ^ flip) for i in range(count)])  39.9 us
    ppermute x37, waiting for transfers between devices, swapped(): return lax.ppermute(x, axis, [(i, i ^ flip) for i in range(count)])  25.7 us
    pallas_call x2, Pallas kernels, attention_call(): pl.pallas_call(functools.partial(body, group, head_dim), out_shape=shapes...  22.3 us
    unnamed x152, local copies, waits for them, and re-layouts  12.4 us
    ppermute x3, starting transfers between devices, window_partner(): return lax.ppermute(x, 'seq', pairs)  10.7 us
    ppermute x3, waiting for transfers between devices, window_partner(): return lax.ppermute(x, 'seq', pairs)  8 us
    pallas_call x2, Pallas kernels, chip_gradient(): pl.pallas_call(functools.partial(gradient_kernel, width, has_proj), out_s...  6.81 us
    pallas_call x1, Pallas kernels, back_through(): pl.pallas_call(functools.partial(back_kernel, group), out_shape=(half, ja...  4.33 us
  transfers between devices with their start and end apart: 42, of which 11 were waited for; matrix products, arithmetic and copies ran while one was open for 18% of the time, Pallas kernels for 13%

profile of v2, /device:TPU:0, one launch (start us, length us, event | category | flops | bytes accessed | tf_op | source)
XLA Modules:
  0.0 173.3 jit_solution(3200142036654611799)
XLA Ops:
  0.7 2.6 %stage.1 = (bf16[192,3072]{1,0:T(8,128)(2,1)}, bf16[8,16,768]{2,1,0:T(8,128)(2,1)}, bf16[8,16,768]{2,1,0:T(8,128)(2,1)}) custom-call(s32[1]{0:T(128)} %bitcast.1.core, bf16[384,2304]{1,0:T(8,128)(2,1)} %w_qkv.7, bf16[384,768]{1,0:T(8,128)(2,1)} %w_proj.3, bf16[1,2,8,16,768]{4,3,2,1,0:T(8,128)(2,1)} %tokens.1), custom_call_target="tpu_custom_call" | custom-call | flops 125000000 | bytes 2400000 | tf_op jit(solution)/shard_map/stage/pallas_call | solution.py:229
  6.0 4.5 %collective-permute-start.1 = (bf16[128,768]{1,0:T(8,128)(2,1)S(1)}, bf16[128,768]{1,0:T(8,128)(2,1)S(1)}, u32[]{:S(2)}, u32[]{:S(2)}) collective-permute-start(bf16[128,768]{1,0:T(8,128)(2,1)S(1)} %bitcast.52), channel_id=1, source_target_pairs={{0,7},{1,2},{2,1},{3,4},{4,3},{5,6},{6,5},{7,0},{8,15},{9,10},{10,... | collective-permute-start | bytes 589832 | tf_op jit(solution)/shard_map/ppermute | solution.py:32
  12.4 3.3 %collective-permute-done.1.refs_1_ = bf16[128,768]{1,0:T(8,128)(2,1)S(1)} collective-permute-done((bf16[128,768]{1,0:T(8,128)(2,1)S(1)}, bf16[128,768]{1,0:T(8,128)(2,1)S(1)}, u32[]{:S(2)}, u32[]{:S(2)}) %collective-permute-start.1) | collective-permute-done | bytes 196640 | tf_op jit(solution)/shard_map/ppermute | solution.py:32
  17.9 3.7 %fusion.91 = (f32[2,8,16]{2,1,0:T(8,128)S(1)}, f32[2,8,16,768]{3,2,1,0:T(8,128)S(1)}) fusion(bf16[4,10,18,768]{3,2,1,0:T(8,128)(2,1)S(1)} %select_maximum_fusion.2.tokens, f32[768]{0:T(1024)S(1)} %get-tuple-element.84, f32[768]{0:T(1024)S(1)} %get-tuple-element.85, f32[768]{0:T(1024)S(1)} %get-tuple-element.60, f32[768]{0:T(1024)S(1)} %get-tuple-element.61, ...), kind=kLoop, calls=%fused_computation.225 | loop fusion | flops 16514816 | bytes 11094016 | tf_op jit(solution)/shard_map/reduce_sum | solution.py:591
  23.9 3.4 %collective-permute-start.3 = (bf16[128,768]{1,0:T(8,128)(2,1)S(1)}, bf16[128,768]{1,0:T(8,128)(2,1)S(1)}, u32[]{:S(2)}, u32[]{:S(2)}) collective-permute-start(bf16[128,768]{1,0:T(8,128)(2,1)S(1)} %bitcast.53), channel_id=1, source_target_pairs={{0,7},{1,2},{2,1},{3,4},{4,3},{5,6},{6,5},{7,0},{8,15},{9,10},{10,... | collective-permute-start | bytes 589832 | tf_op jit(solution)/shard_map/ppermute | solution.py:32
  27.3 4.7 %collective-permute-done.3.refs_1_.xg = bf16[128,768]{1,0:T(8,128)(2,1)S(1)} collective-permute-done((bf16[128,768]{1,0:T(8,128)(2,1)S(1)}, bf16[128,768]{1,0:T(8,128)(2,1)S(1)}, u32[]{:S(2)}, u32[]{:S(2)}) %collective-permute-start.3) | collective-permute-done | bytes 196640 | tf_op jit(solution)/shard_map/ppermute | solution.py:32
  31.9 7.2 %collective-permute-done.4.refs_0_ = bf16[192,3072]{1,0:T(8,128)(2,1)} collective-permute-done((bf16[192,3072]{1,0:T(8,128)(2,1)}, bf16[192,3072]{1,0:T(8,128)(2,1)}, u32[]{:S(2)}, u32[]{:S(2)}) %collective-permute-start.4) | collective-permute-done | bytes 1179680 | tf_op jit(solution)/shard_map/ppermute | solution.py:26
  44.3 14.3 %first_heads.1 = (bf16[1920,256]{1,0:T(8,128)(2,1)}, bf16[384,256]{1,0:T(8,128)(2,1)S(1)}, bf16[512,256]{1,0:T(8,128)(2,1)S(1)}, bf16[768,256]{1,0:T(8,128)(2,1)S(1)}, f32[16,256]{1,0:T(8,128)S(1)}) custom-call(s32[5]{0:T(128)S(1)} %pad_add_fusion.nums, f32[24]{0:T(128)S(1)} %copy-done.27, bf16[128,768]{1,0:T(8,128)(2,1)S(1)} %bitcast.42, ...), custom_call_target="tpu_custom_call" | custom-call | flops 650000000 | bytes 4800000 | tf_op jit(solution)/shard_map/first_heads/pallas_call | solution.py:195
  60.6 2.3 %collective-permute-done.6.refs_1_.refs_3_ = bf16[1920,256]{1,0:T(8,128)(2,1)} collective-permute-done((bf16[1920,256]{1,0:T(8,128)(2,1)}, bf16[1920,256]{1,0:T(8,128)(2,1)}, u32[]{:S(2)}, u32[]{:S(2)}) %collective-permute-start.6) | collective-permute-done | bytes 983072 | tf_op jit(solution)/shard_map/ppermute | solution.py:26
  63.0 3.8 %chip_gradient.2 = (f32[96,1536]{1,0:T(8,128)S(1)}, bf16[96,1536]{1,0:T(8,128)(2,1)}, bf16[96,1536]{1,0:T(8,128)(2,1)}, bf16[96,1536]{1,0:T(8,128)(2,1)}) custom-call(bf16[384,256]{1,0:T(8,128)(2,1)S(1)} %get-tuple-element.37.refs_0_, bf16[1920,256]{1,0:T(8,128)(2,1)} %collective-permute-done.6.refs_1_.refs_3_, ...), custom_call_target="tpu_custom_call" | custom-call | flops 75000000 | bytes 2100000 | tf_op jit(solution)/shard_map/chip_gradient/pallas_call | solution.py:391
  70.9 2.2 %broadcast_select_fusion.5 = (bf16[192,768]{1,0:T(8,128)(2,1)}, bf16[192,768]{1,0:T(8,128)(2,1)}, bf16[192,768]{1,0:T(8,128)(2,1)}, bf16[192,768]{1,0:T(8,128)(2,1)}) fusion(pred[]{:T(512)S(6)} %eq.51, bf16[384,768]{1,0:T(8,128)(2,1)S(1)} %copy-done.7, bf16[192,3072]{1,0:T(8,128)(2,1)} %collective-permute-done.5.other, bf16[192,3072]{1,0:T(8,128)(2,1)} %ordered.9.got, ...), kind=kLoop, calls=%fused_computation.124 | loop fusion | flops 884736 | bytes 2359298 | tf_op jit(solution)/shard_map/jit(_where)/select_n | solution.py:493
  77.2 8.0 %second_heads.1 = (bf16[1152,256]{1,0:T(8,128)(2,1)S(1)}, bf16[384,256]{1,0:T(8,128)(2,1)S(1)}, bf16[256,256]{1,0:T(8,128)(2,1)S(1)}, f32[8,256]{1,0:T(8,128)S(1)}) custom-call(s32[5]{0:T(128)S(1)} %pad_add_fusion.nums, f32[24]{0:T(128)S(1)} %copy-done.27, bf16[128,768]{1,0:T(8,128)(2,1)S(1)} %bitcast.43, bf16[128,768]{1,0:T(8,128)(2,1)S(1)} %copy-done.14, ...), custom_call_target="tpu_custom_call" | custom-call | flops 450000000 | bytes 4800000 | tf_op jit(solution)/shard_map/second_heads/pallas_call | solution.py:195
  85.3 4.3 %back_through.1 = (bf16[128,768]{1,0:T(8,128)(2,1)S(1)}, bf16[256,768]{1,0:T(8,128)(2,1)}, bf16[128,768]{1,0:T(8,128)(2,1)S(1)}) custom-call(s32[5]{0:T(128)S(1)} %pad_add_fusion.nums, bf16[1920,256]{1,0:T(8,128)(2,1)} %get-tuple-element.35.refs_2_.first, bf16[1152,256]{1,0:T(8,128)(2,1)S(1)} %get-tuple-element.40.second.refs_2_, ...), custom_call_target="tpu_custom_call" | custom-call | flops 200000000 | bytes 4800000 | tf_op jit(solution)/shard_map/back_through/pallas_call | solution.py:287
  92.6 2.6 %collective-permute-start.16 = (bf16[24,1536]{1,0:T(8,128)(2,1)S(1)}, bf16[24,1536]{1,0:T(8,128)(2,1)S(1)}, u32[]{:S(2)}, u32[]{:S(2)}) collective-permute-start(bf16[24,1536]{1,0:T(8,128)(2,1)S(1)} %get-tuple-element.121), channel_id=1, source_target_pairs={{0,4},{1,5},{2,6},{3,7},{4,0},{5,1},{6,2},{7,3},{8,12},{9,13},{10,... | collective-permute-start | bytes 221192 | tf_op jit(solution)/shard_map/ppermute | solution.py:26
  95.5 2.8 %collective-permute-start.7 = (bf16[256,768]{1,0:T(8,128)(2,1)}, bf16[256,768]{1,0:T(8,128)(2,1)}, u32[]{:S(2)}, u32[]{:S(2)}) collective-permute-start(bf16[256,768]{1,0:T(8,128)(2,1)} %get-tuple-element.43), channel_id=1, source_target_pairs={{0,7},{1,2},{2,1},{3,4},{4,3},{5,6},{6,5},{7,0},{8,15},{9,10},{10,... | collective-permute-start | bytes 1179656 | tf_op jit(solution)/shard_map/ppermute | solution.py:32
  98.3 3.1 %chip_gradient.3 = (f32[96,1536]{1,0:T(8,128)S(1)}, bf16[96,1536]{1,0:T(8,128)(2,1)}, bf16[96,1536]{1,0:T(8,128)(2,1)}, bf16[96,1536]{1,0:T(8,128)(2,1)S(1)}) custom-call(bf16[384,256]{1,0:T(8,128)(2,1)S(1)} %copy-done.24, bf16[1920,256]{1,0:T(8,128)(2,1)} %collective-permute-done.6.refs_1_.refs_3_, bf16[1152,256]{1,0:T(8,128)(2,1)S(1)} %get-tuple-element.40.second.refs_2_, ...), custom_call_target="tpu_custom_call" | custom-call | flops 75000000 | bytes 2100000 | tf_op jit(solution)/shard_map/chip_gradient/pallas_call | solution.py:391
  119.5 3.3 %small_gradients.1.refs_0_ = f32[32,768]{1,0:T(8,128)S(1)} custom-call(f32[2,8,16,768]{3,2,1,0:T(8,128)S(1)} %get-tuple-element.91.bm, bf16[4,10,18,768]{3,2,1,0:T(8,128)(2,1)S(1)} %select_maximum_fusion.2.tokens, bf16[2,8,16,768]{3,2,1,0:T(8,128)(2,1)S(1)} %pad_maximum_fusion.5.back, f32[2,8,16,768]{3,2,1,0:T(8,128)S(1)} %copy-done.3, ...), custom_call_target="tpu_custom_call" | custom-call | flops 175000000 | bytes 1800000 | tf_op jit(solution)/shard_map/small_gradients/pallas_call | solution.py:530
  132.4 4.6 %collective-permute-start.27 = (bf16[24,1536]{1,0:T(8,128)(2,1)S(1)}, bf16[24,1536]{1,0:T(8,128)(2,1)S(1)}, u32[]{:S(2)}, u32[]{:S(2)}) collective-permute-start(bf16[24,1536]{1,0:T(8,128)(2,1)S(1)} %get-tuple-element.116), channel_id=1, source_target_pairs={{0,2},{1,3},{2,0},{3,1},{4,6},{5,7},{6,4},{7,5},{8,10},{9,11},{10,... | collective-permute-start | bytes 221192 | tf_op jit(solution)/shard_map/ppermute | solution.py:26
  137.1 2.4 %collective-permute-start.29 = (bf16[24,1536]{1,0:T(8,128)(2,1)S(1)}, bf16[24,1536]{1,0:T(8,128)(2,1)S(1)}, u32[]{:S(2)}, u32[]{:S(2)}) collective-permute-start(bf16[24,1536]{1,0:T(8,128)(2,1)S(1)} %get-tuple-element.117), channel_id=1, source_target_pairs={{0,6},{1,7},{2,4},{3,5},{4,2},{5,3},{6,0},{7,1},{8,14},{9,15},{10,... | collective-permute-start | bytes 221192 | tf_op jit(solution)/shard_map/ppermute | solution.py:26
  148.7 2.2 %collective-permute-start.32 = (bf16[24,1536]{1,0:T(8,128)(2,1)S(1)}, bf16[24,1536]{1,0:T(8,128)(2,1)S(1)}, u32[]{:S(2)}, u32[]{:S(2)}) collective-permute-start(bf16[24,1536]{1,0:T(8,128)(2,1)S(1)} %fusion.65), channel_id=1, source_target_pairs={{0,6},{1,7},{2,4},{3,5},{4,2},{5,3},{6,0},{7,1},{8,14},{9,15},{10,... | collective-permute-start | bytes 221192 | tf_op jit(solution)/shard_map/ppermute | solution.py:26
  151.6 3.4 %fusion.63 = bf16[1,2,8,16,768]{4,3,2,1,0:T(8,128)(2,1)} fusion(f32[2,8,16,768]{3,2,1,0:T(8,128)S(1)} %get-tuple-element.91.bm, f32[4,10,18,768]{3,2,1,0:T(8,128)S(1)} %select_maximum_fusion, f32[768]{0:T(1024)S(1)} %get-tuple-element.84, f32[768]{0:T(1024)S(1)} %get-tuple-element.85, f32[768]{0:T(1024)S(1)} %get-tuple-element.60, ...), kind=kLoop, calls=%fused_computation.116 | loop fusion | flops 11206656 | bytes 20923392 | tf_op jit(solution)/shard_map/broadcast_in_dim | solution.py:694
  155.0 3.7 %collective-permute-done.40 = f32[16,768]{1,0:T(8,128)S(1)} collective-permute-done((f32[16,768]{1,0:T(8,128)S(1)}, f32[16,768]{1,0:T(8,128)S(1)}, u32[]{:S(2)}, u32[]{:S(2)}) %collective-permute-start.40) | collective-permute-done | bytes 49184 | tf_op jit(solution)/shard_map/ppermute | solution.py:26
  161.5 7.2 %collective-permute-done.33.refs_5_ = bf16[96,1536]{1,0:T(8,128)(2,1)S(1)} collective-permute-done((bf16[96,1536]{1,0:T(8,128)(2,1)S(1)}, bf16[96,1536]{1,0:T(8,128)(2,1)S(1)}, u32[]{:S(2)}, u32[]{:S(2)}) %collective-permute-start.33) | collective-permute-done | bytes 294944 | tf_op jit(solution)/shard_map/ppermute | solution.py:26
  170.2 3.1 %assemble.1 = (f32[384,2304]{1,0:T(8,128)}, f32[384,768]{1,0:T(8,128)}) custom-call(s32[3]{0:T(128)S(1)} %pad_add_fusion.1.at, bf16[96,1536]{1,0:T(8,128)(2,1)S(1)} %pad_maximum_fusion.6.refs_0_, bf16[96,1536]{1,0:T(8,128)(2,1)S(1)} %collective-permute-done.21.refs_1_, bf16[96,1536]{1,0:T(8,128)(2,1)S(1)} %collective-permute-done.22.refs_2_, ...), custom_call_target="tpu_custom_call" | custom-call | flops 150000000 | bytes 4200000 | tf_op jit(solution)/shard_map/assemble/pallas_call | solution.py:456
  (277 shorter events, 69.1 us)
Async XLA Ops:
  6.0 9.7 %collective-permute-start.1 = (bf16[128,768]{1,0:T(8,128)(2,1)S(1)}, bf16[128,768]{1,0:T(8,128)(2,1)S(1)}, u32[]{:S(2)}, u32[]{:S(2)}) collective-permute-start(bf16[128,768]{1,0:T(8,128)(2,1)S(1)} %bitcast.52), channel_id=1, source_target_pairs={{0,7},{1,2},{2,1},{3,4},{4,3},{5,6},{6,5},{7,0},{8,15},{9,10},{10,... | collective-permute-start | bytes 589832 | tf_op jit(solution)/shard_map/ppermute | solution.py:32
  10.5 28.7 %collective-permute-start.4 = (bf16[192,3072]{1,0:T(8,128)(2,1)}, bf16[192,3072]{1,0:T(8,128)(2,1)}, u32[]{:S(2)}, u32[]{:S(2)}) collective-permute-start(bf16[192,3072]{1,0:T(8,128)(2,1)} %get-tuple-element.34), channel_id=1, source_target_pairs={{0,8},{8,0},{1,9},{9,1},{2,10},{10,2},{3,11},{11,3},{4,12},{12,4},... | collective-permute-start | bytes 3538952 | tf_op jit(solution)/shard_map/ppermute | solution.py:26
  60.3 35.2 %collective-permute-start.9 = (bf16[256,768]{1,0:T(8,128)(2,1)}, bf16[256,768]{1,0:T(8,128)(2,1)}, u32[]{:S(2)}, u32[]{:S(2)}) collective-permute-start(bf16[256,768]{1,0:T(8,128)(2,1)} %copy-done.8), channel_id=1, source_target_pairs={{0,1},{1,0},{2,3},{3,2},{4,5},{5,4},{6,7},{7,6},{8,9},{9,8},{10,11... | collective-permute-start | bytes 1179656 | tf_op jit(solution)/shard_map/ppermute | solution.py:26
  67.4 22.2 %collective-permute-start.10 = (bf16[96,1536]{1,0:T(8,128)(2,1)}, bf16[96,1536]{1,0:T(8,128)(2,1)}, u32[]{:S(2)}, u32[]{:S(2)}) collective-permute-start(bf16[96,1536]{1,0:T(8,128)(2,1)} %get-tuple-element.46), channel_id=1, source_target_pairs={{0,8},{8,0},{16,24},{24,16},{1,9},{9,1},{17,25},{25,17},{2,10},{10... | collective-permute-start | bytes 884744 | tf_op jit(solution)/shard_map/ppermute | solution.py:26
  68.9 20.7 %collective-permute-start.11 = (bf16[96,1536]{1,0:T(8,128)(2,1)}, bf16[96,1536]{1,0:T(8,128)(2,1)}, u32[]{:S(2)}, u32[]{:S(2)}) collective-permute-start(bf16[96,1536]{1,0:T(8,128)(2,1)} %get-tuple-element.47), channel_id=1, source_target_pairs={{0,16},{8,24},{16,0},{24,8},{1,17},{9,25},{17,1},{25,9},{2,18},{10... | collective-permute-start | bytes 884744 | tf_op jit(solution)/shard_map/ppermute | solution.py:26
  70.4 19.2 %collective-permute-start.12 = (bf16[96,1536]{1,0:T(8,128)(2,1)}, bf16[96,1536]{1,0:T(8,128)(2,1)}, u32[]{:S(2)}, u32[]{:S(2)}) collective-permute-start(bf16[96,1536]{1,0:T(8,128)(2,1)} %get-tuple-element.48), channel_id=1, source_target_pairs={{0,24},{8,16},{16,8},{24,0},{1,25},{9,17},{17,9},{25,1},{2,26},{10... | collective-permute-start | bytes 884744 | tf_op jit(solution)/shard_map/ppermute | solution.py:26
  85.2 13.1 %collective-permute-start.8 = (bf16[1152,256]{1,0:T(8,128)(2,1)S(1)}, bf16[1152,256]{1,0:T(8,128)(2,1)S(1)}, u32[]{:S(2)}, u32[]{:S(2)}) collective-permute-start(bf16[1152,256]{1,0:T(8,128)(2,1)S(1)} %get-tuple-element.40.second.refs_2_), channel_id=1, source_target_pairs={{0,1},{1,0},{2,3},{3,2},{4,5},{5,4},{6,7},{7,6},{8,9},{9,8},{10,11... | collective-permute-start | bytes 1769480 | tf_op jit(solution)/shard_map/ppermute | solution.py:26
  91.0 11.8 %collective-permute-start.15 = (bf16[24,1536]{1,0:T(8,128)(2,1)S(1)}, bf16[24,1536]{1,0:T(8,128)(2,1)S(1)}, u32[]{:S(2)}, u32[]{:S(2)}) collective-permute-start(bf16[24,1536]{1,0:T(8,128)(2,1)S(1)} %get-tuple-element.119), channel_id=1, source_target_pairs={{0,2},{1,3},{2,0},{3,1},{4,6},{5,7},{6,4},{7,5},{8,10},{9,11},{10,... | collective-permute-start | bytes 221192 | tf_op jit(solution)/shard_map/ppermute | solution.py:26
  92.6 10.9 %collective-permute-start.16 = (bf16[24,1536]{1,0:T(8,128)(2,1)S(1)}, bf16[24,1536]{1,0:T(8,128)(2,1)S(1)}, u32[]{:S(2)}, u32[]{:S(2)}) collective-permute-start(bf16[24,1536]{1,0:T(8,128)(2,1)S(1)} %get-tuple-element.121), channel_id=1, source_target_pairs={{0,4},{1,5},{2,6},{3,7},{4,0},{5,1},{6,2},{7,3},{8,12},{9,13},{10,... | collective-permute-start | bytes 221192 | tf_op jit(solution)/shard_map/ppermute | solution.py:26
  95.5 15.4 %collective-permute-start.7 = (bf16[256,768]{1,0:T(8,128)(2,1)}, bf16[256,768]{1,0:T(8,128)(2,1)}, u32[]{:S(2)}, u32[]{:S(2)}) collective-permute-start(bf16[256,768]{1,0:T(8,128)(2,1)} %get-tuple-element.43), channel_id=1, source_target_pairs={{0,7},{1,2},{2,1},{3,4},{4,3},{5,6},{6,5},{7,0},{8,15},{9,10},{10,... | collective-permute-start | bytes 1179656 | tf_op jit(solution)/shard_map/ppermute | solution.py:32
  106.5 11.7 %collective-permute-start.18 = (bf16[24,1536]{1,0:T(8,128)(2,1)}, bf16[24,1536]{1,0:T(8,128)(2,1)}, u32[]{:S(2)}, u32[]{:S(2)}) collective-permute-start(bf16[24,1536]{1,0:T(8,128)(2,1)} %fusion.67), channel_id=1, source_target_pairs={{0,2},{1,3},{2,0},{3,1},{4,6},{5,7},{6,4},{7,5},{8,10},{9,11},{10,... | collective-permute-start | bytes 221192 | tf_op jit(solution)/shard_map/ppermute | solution.py:26
  107.7 15.1 %collective-permute-start.19 = (bf16[24,1536]{1,0:T(8,128)(2,1)}, bf16[24,1536]{1,0:T(8,128)(2,1)}, u32[]{:S(2)}, u32[]{:S(2)}) collective-permute-start(bf16[24,1536]{1,0:T(8,128)(2,1)} %fusion.67), channel_id=1, source_target_pairs={{0,4},{1,5},{2,6},{3,7},{4,0},{5,1},{6,2},{7,3},{8,12},{9,13},{10,... | collective-permute-start | bytes 221192 | tf_op jit(solution)/shard_map/ppermute | solution.py:26
  109.2 14.4 %collective-permute-start.20 = (bf16[24,1536]{1,0:T(8,128)(2,1)}, bf16[24,1536]{1,0:T(8,128)(2,1)}, u32[]{:S(2)}, u32[]{:S(2)}) collective-permute-start(bf16[24,1536]{1,0:T(8,128)(2,1)} %fusion.67), channel_id=1, source_target_pairs={{0,6},{1,7},{2,4},{3,5},{4,2},{5,3},{6,0},{7,1},{8,14},{9,15},{10,... | collective-permute-start | bytes 221192 | tf_op jit(solution)/shard_map/ppermute | solution.py:26
  111.9 14.4 %collective-permute-start.24 = (bf16[96,1536]{1,0:T(8,128)(2,1)}, bf16[96,1536]{1,0:T(8,128)(2,1)S(1)}, u32[]{:S(2)}, u32[]{:S(2)}) collective-permute-start(bf16[96,1536]{1,0:T(8,128)(2,1)} %get-tuple-element.50), channel_id=1, source_target_pairs={{0,8},{8,0},{16,24},{24,16},{1,9},{9,1},{17,25},{25,17},{2,10},{10... | collective-permute-start | bytes 884744 | tf_op jit(solution)/shard_map/ppermute | solution.py:26
  113.5 14.4 %collective-permute-start.25 = (bf16[96,1536]{1,0:T(8,128)(2,1)}, bf16[96,1536]{1,0:T(8,128)(2,1)S(1)}, u32[]{:S(2)}, u32[]{:S(2)}) collective-permute-start(bf16[96,1536]{1,0:T(8,128)(2,1)} %get-tuple-element.51), channel_id=1, source_target_pairs={{0,16},{8,24},{16,0},{24,8},{1,17},{9,25},{17,1},{25,9},{2,18},{10... | collective-permute-start | bytes 884744 | tf_op jit(solution)/shard_map/ppermute | solution.py:26
  118.2 9.7 %collective-permute-start.26 = (bf16[96,1536]{1,0:T(8,128)(2,1)S(1)}, bf16[96,1536]{1,0:T(8,128)(2,1)S(1)}, u32[]{:S(2)}, u32[]{:S(2)}) collective-permute-start(bf16[96,1536]{1,0:T(8,128)(2,1)S(1)} %copy-done.29), channel_id=1, source_target_pairs={{0,24},{8,16},{16,8},{24,0},{1,25},{9,17},{17,9},{25,1},{2,26},{10... | collective-permute-start | bytes 884744 | tf_op jit(solution)/shard_map/ppermute | solution.py:26
  126.4 28.7 %collective-permute-start.21 = (bf16[96,1536]{1,0:T(8,128)(2,1)S(1)}, bf16[96,1536]{1,0:T(8,128)(2,1)S(1)}, u32[]{:S(2)}, u32[]{:S(2)}) collective-permute-start(bf16[96,1536]{1,0:T(8,128)(2,1)S(1)} %pad_maximum_fusion.6.refs_0_), channel_id=1, source_target_pairs={{0,16},{16,0},{1,17},{17,1},{2,18},{18,2},{3,19},{19,3},{4,20},{20... | collective-permute-start | bytes 884744 | tf_op jit(solution)/shard_map/ppermute | solution.py:26
  132.4 12.8 %collective-permute-start.27 = (bf16[24,1536]{1,0:T(8,128)(2,1)S(1)}, bf16[24,1536]{1,0:T(8,128)(2,1)S(1)}, u32[]{:S(2)}, u32[]{:S(2)}) collective-permute-start(bf16[24,1536]{1,0:T(8,128)(2,1)S(1)} %get-tuple-element.116), channel_id=1, source_target_pairs={{0,2},{1,3},{2,0},{3,1},{4,6},{5,7},{6,4},{7,5},{8,10},{9,11},{10,... | collective-permute-start | bytes 221192 | tf_op jit(solution)/shard_map/ppermute | solution.py:26
  146.4 12.3 %collective-permute-start.30 = (bf16[24,1536]{1,0:T(8,128)(2,1)S(1)}, bf16[24,1536]{1,0:T(8,128)(2,1)S(1)}, u32[]{:S(2)}, u32[]{:S(2)}) collective-permute-start(bf16[24,1536]{1,0:T(8,128)(2,1)S(1)} %fusion.65), channel_id=1, source_target_pairs={{0,2},{1,3},{2,0},{3,1},{4,6},{5,7},{6,4},{7,5},{8,10},{9,11},{10,... | collective-permute-start | bytes 221192 | tf_op jit(solution)/shard_map/ppermute | solution.py:26
  147.9 11.4 %collective-permute-start.31 = (bf16[24,1536]{1,0:T(8,128)(2,1)S(1)}, bf16[24,1536]{1,0:T(8,128)(2,1)S(1)}, u32[]{:S(2)}, u32[]{:S(2)}) collective-permute-start(bf16[24,1536]{1,0:T(8,128)(2,1)S(1)} %fusion.65), channel_id=1, source_target_pairs={{0,4},{1,5},{2,6},{3,7},{4,0},{5,1},{6,2},{7,3},{8,12},{9,13},{10,... | collective-permute-start | bytes 221192 | tf_op jit(solution)/shard_map/ppermute | solution.py:26
  148.7 10.6 %collective-permute-start.32 = (bf16[24,1536]{1,0:T(8,128)(2,1)S(1)}, bf16[24,1536]{1,0:T(8,128)(2,1)S(1)}, u32[]{:S(2)}, u32[]{:S(2)}) collective-permute-start(bf16[24,1536]{1,0:T(8,128)(2,1)S(1)} %fusion.65), channel_id=1, source_target_pairs={{0,6},{1,7},{2,4},{3,5},{4,2},{5,3},{6,0},{7,1},{8,14},{9,15},{10,... | collective-permute-start | bytes 221192 | tf_op jit(solution)/shard_map/ppermute | solution.py:26
  155.0 14.7 %collective-permute-start.22 = (bf16[96,1536]{1,0:T(8,128)(2,1)S(1)}, bf16[96,1536]{1,0:T(8,128)(2,1)S(1)}, u32[]{:S(2)}, u32[]{:S(2)}) collective-permute-start(bf16[96,1536]{1,0:T(8,128)(2,1)S(1)} %pad_maximum_fusion.6.refs_0_), channel_id=1, source_target_pairs={{0,1},{1,0},{2,3},{3,2},{4,5},{5,4},{6,7},{7,6},{8,9},{9,8},{10,11... | collective-permute-start | bytes 884744 | tf_op jit(solution)/shard_map/ppermute | solution.py:26
  158.7 11.1 %collective-permute-start.23 = (bf16[96,1536]{1,0:T(8,128)(2,1)S(1)}, bf16[96,1536]{1,0:T(8,128)(2,1)S(1)}, u32[]{:S(2)}, u32[]{:S(2)}) collective-permute-start(bf16[96,1536]{1,0:T(8,128)(2,1)S(1)} %collective-permute-done.21.refs_1_), channel_id=1, source_target_pairs={{0,1},{1,0},{2,3},{3,2},{4,5},{5,4},{6,7},{7,6},{8,9},{9,8},{10,11... | collective-permute-start | bytes 884744 | tf_op jit(solution)/shard_map/ppermute | solution.py:26
  159.3 9.3 %collective-permute-start.33 = (bf16[96,1536]{1,0:T(8,128)(2,1)S(1)}, bf16[96,1536]{1,0:T(8,128)(2,1)S(1)}, u32[]{:S(2)}, u32[]{:S(2)}) collective-permute-start(bf16[96,1536]{1,0:T(8,128)(2,1)S(1)} %pad_maximum_fusion.7.refs_4_), channel_id=1, source_target_pairs={{0,16},{16,0},{1,17},{17,1},{2,18},{18,2},{3,19},{19,3},{4,20},{20... | collective-permute-start | bytes 884744 | tf_op jit(solution)/shard_map/ppermute | solution.py:26
  (94 other events, 681.6 us)

commit v3 on v2

--- a/solution.py
+++ b/solution.py
@@ -9,13 +9,14 @@
 from jax.sharding import PartitionSpec as P
 
 HALF = 8
+LOG2_E = math.log2(math.e)
 BF = jnp.bfloat16
 F32 = jnp.float32
 
 
 def busy(microseconds, megabytes):
     return pl.CostEstimate(
-        flops=int(microseconds * 0.5e8), bytes_accessed=int(megabytes * 0.6e6), transcendentals=0
+        flops=int(microseconds * 0.5e7), bytes_accessed=int(megabytes * 0.1e6), transcendentals=0
     )
 
 
@@ -116,15 +117,15 @@
         iq, uq = unit(qf)
         ik, uk = unit(kf)
         cosine = lax.dot_general(uk, uq, OVER_ROWS, preferred_element_type=F32)
-        expo = jnp.exp(cosine * s) * allowed
-        prob = expo * (1.0 / jnp.sum(expo, axis=0, keepdims=True))
-        weights = prob.astype(BF)
+        back_prob = lax.dot_general(v, b, OVER_ROWS, preferred_element_type=F32)
+        expo = jnp.exp2(cosine * (s * LOG2_E)) * allowed
+        inverse = 1.0 / jnp.sum(expo, axis=0, keepdims=True)
+        weights = (expo * inverse).astype(BF)
         att[rows(0), :] = jnp.dot(v, weights, preferred_element_type=F32).astype(BF)
-        back_prob = lax.dot_general(v, b, OVER_ROWS, preferred_element_type=F32)
-        mean = jnp.sum(prob * back_prob, axis=0, keepdims=True)
-        back_score = prob * (back_prob - mean)
-        gs[pl.ds(h, 1), :] = jnp.sum(back_score * cosine, axis=0, keepdims=True)
-        scaled = (back_score * s).astype(BF)
+        mean = jnp.sum(expo * back_prob, axis=0, keepdims=True) * inverse
+        scaled = expo * (inverse * s) * (back_prob - mean)
+        gs[pl.ds(h, 1), :] = jnp.sum(scaled * cosine, axis=0, keepdims=True) * (1.0 / s)
+        scaled = scaled.astype(BF)
         buq = jnp.dot(uk, scaled, preferred_element_type=F32)
         buk = lax.dot_general(uq, scaled, OVER_LANES, preferred_element_type=F32)
         bv = lax.dot_general(b, weights, OVER_LANES, preferred_element_type=F32)
@@ -133,11 +134,11 @@
         back[rows(2 * group), :] = bv.astype(BF)
 
     def body(i, carry):
-        for u in range(4):
-            one_head(i * 4 + u)
+        for u in range(8):
+            one_head(i * 8 + u)
         return carry
 
-    lax.fori_loop(0, group // head_dim // 4, body, 0)
+    lax.fori_loop(0, group // head_dim // 8, body, 0)
 
 
 def first_kernel(group, head_dim, nums, scale, xm, xg, cot, order, w_qkv, w_proj, got, other, *outs):
@@ -198,7 +199,7 @@
         in_specs=[smem, smem] + [vmem] * (len(operands) - 2),
         out_specs=(vmem,) * len(shapes),
         scratch_shapes=[pltpu.VMEM((3 * group, n), BF)],
-        compiler_params=pltpu.CompilerParams(vmem_limit_bytes=20 * 1024 * 1024),
+        compiler_params=pltpu.CompilerParams(vmem_limit_bytes=60 * 1024 * 1024),
         cost_estimate=busy(5 + 0.5 * (group // head_dim), 8),
         name=name,
     )(*operands)
@@ -289,7 +290,7 @@
         out_shape=(half, jax.ShapeDtypeStruct((n, channels), BF), half),
         in_specs=[smem] + [vmem] * (len(operands) - 1),
         out_specs=(vmem,) * 3,
-        compiler_params=pltpu.CompilerParams(vmem_limit_bytes=20 * 1024 * 1024),
+        compiler_params=pltpu.CompilerParams(vmem_limit_bytes=60 * 1024 * 1024),
         cost_estimate=busy(4, 8),
         name="back_through",
     )(*operands)
@@ -393,7 +394,7 @@
         out_shape=(jax.ShapeDtypeStruct((rows // 4, total), F32), wire, wire, wire),
         in_specs=[vmem] * len(operands),
         out_specs=(vmem,) * 4,
-        compiler_params=pltpu.CompilerParams(vmem_limit_bytes=16 * 1024 * 1024),
+        compiler_params=pltpu.CompilerParams(vmem_limit_bytes=60 * 1024 * 1024),
         cost_estimate=busy(1.5, 3.5),
         name="chip_gradient",
     )(*operands)
@@ -418,8 +419,10 @@
     return total.astype(BF)
 
 
-def gather_blocks(block, place):
+def gather_blocks(block, place, *others):
     got = [swapped(block, "seq", 2 * k) if k else block for k in range(place.split)]
+    if others:
+        got[-1] = after(got[-1], *others)
     chips = jnp.concatenate(got)
     other_rep = swapped(chips, "rep", 1)
     return chips, other_rep, swapped(chips, "seq", 1), swapped(other_rep, "seq", 1)
@@ -461,26 +464,29 @@
         ),
         in_specs=[smem] + [vmem] * 8,
         out_specs=(vmem, vmem),
-        compiler_params=pltpu.CompilerParams(vmem_limit_bytes=16 * 1024 * 1024),
+        compiler_params=pltpu.CompilerParams(vmem_limit_bytes=60 * 1024 * 1024),
         cost_estimate=busy(3, 7),
         name="assemble",
     )(at, *first, *second)
 
 
-def sum_everywhere(x, place):
+def sum_steps(x, place):
     half = x.shape[0] // 2
     low = place.core == 0
     x = jnp.where(low, x[:half], x[half:]) + swapped(
         jnp.where(low, x[half:], x[:half]), "seq", 1
     )
     x = x + swapped(x, "rep", 1)
+    yield x
     x = x + swapped(x, "dp", 1)
+    yield x
     flip = 2
     while flip < lax.axis_size("seq"):
         x = x + swapped(x, "seq", flip)
+        yield x
         flip = flip * 2
     got = swapped(x, "seq", 1)
-    return jnp.concatenate([jnp.where(low, x, got), jnp.where(low, got, x)])
+    yield jnp.concatenate([jnp.where(low, x, got), jnp.where(low, got, x)])
 
 
 def rows_of_both(mine, got, other, place):
@@ -497,52 +503,87 @@
 GROUP_HEADS = 16
 
 
-def tap_gradient_kernel(bm, tokens, back, unit, scale, out):
-    depth, height, width, lanes = bm.shape
-    mixed = bm[...]
-    zero = jnp.zeros((1, lanes), F32)
-    for e in range(3):
-        shifted = tokens[:, :, e : e + width, :].astype(F32)
-        for a in range(3):
-            for b in range(3):
-                product = mixed * shifted[a : a + depth, b : b + height]
-                row = jnp.sum(jnp.sum(product, axis=(0, 1)), axis=0, keepdims=True)
-                out[9 * a + 3 * b + e : 9 * a + 3 * b + e + 1, :] = row
-    gain = jnp.sum(jnp.sum(back[...].astype(F32) * unit[...], axis=(0, 1)), axis=0, keepdims=True)
-    out[27:28, :] = gain
+def into_field(nums, mine, theirs):
+    count = mine.shape[0] // HALF
+    mine = mine.astype(F32).reshape(count, HALF, -1)
+    theirs = theirs.astype(F32).reshape(count, HALF, -1)
+    column = lax.broadcasted_iota(jnp.int32, mine.shape, 1)
+    low = (column >= nums[1]).astype(jnp.int32) == nums[4]
+    return jnp.concatenate([jnp.where(low, mine, theirs), jnp.where(low, theirs, mine)], axis=1)
+
+
+def field_kernel(*refs):
+    nums, back, att, got, mixed, unit, inverse, cot, padded, gain, scale = refs[:11]
+    w_mine, w_got, w_other = refs[11:14]
+    bm, inner, outer, out, small = refs[14:]
+    depth, height, width, channels = mixed.shape
+    half = back.shape[0]
+    rows = depth * height
+    restored = into_field(nums, att[...], got[half:, :]).reshape(rows * width, channels)
+    low_rows, low_core = nums[3] == 0, nums[4] == 0
+    side, part = channels // 2, channels // 4
+    r_mine = jnp.where(low_rows, restored[:, :side], restored[:, side:]).astype(BF)
+    r_peer = jnp.where(low_rows, restored[:, side:], restored[:, :side])
+    r_got = jnp.where(low_core, r_peer[:, :part], r_peer[:, part:]).astype(BF)
+    r_other = jnp.where(low_core, r_peer[:, part:], r_peer[:, :part]).astype(BF)
+    projected = jnp.dot(r_mine, w_mine[...], preferred_element_type=F32)
+    projected = projected + jnp.dot(r_got, w_got[:, :channels], preferred_element_type=F32)
+    projected = projected + jnp.dot(r_other, w_other[:, :channels], preferred_element_type=F32)
+    out[...] = (mixed[...] + projected.reshape(mixed.shape)).astype(BF)
+
+    normed = into_field(nums, back[...], got[:half, :])
+    field = unit[...].reshape(rows, width, channels)
+    small[27:28, :] = jnp.sum(jnp.sum(normed * field, axis=0), axis=0, keepdims=True)
+    grad = normed * gain[...].reshape(1, 1, channels)
+    mean = jnp.mean(grad, axis=-1, keepdims=True)
+    slope = jnp.mean(grad * field, axis=-1, keepdims=True)
+    std = inverse[...].reshape(rows, width, 1)
+    value = cot[...].astype(F32).reshape(rows, width, channels) + std * (grad - mean - field * slope)
+    bm[...] = value.reshape(mixed.shape)
+    first, last = value[:height].astype(BF), value[rows - height :].astype(BF)
+    inner[...] = jnp.where(low_core, last.astype(F32), first.astype(F32)).astype(BF)
+    outer[...] = jnp.where(low_core, first.astype(F32), last.astype(F32)).astype(BF)
+
+    tile = 128
+    for start in range(0, channels, tile):
+        lanes = slice(start, start + tile)
+        mixed_back = bm[:, :, :, lanes]
+        for e in range(3):
+            shifted = padded[:, :, e : e + width, lanes].astype(F32)
+            for a in range(3):
+                for b in range(3):
+                    product = mixed_back * shifted[a : a + depth, b : b + height]
+                    row = jnp.sum(jnp.sum(product, axis=(0, 1)), axis=0, keepdims=True)
+                    small[9 * a + 3 * b + e : 9 * a + 3 * b + e + 1, lanes] = row
     sums = jnp.sum(scale[...], axis=1, keepdims=True)
     heads = sums.shape[0]
-    same = lax.broadcasted_iota(jnp.int32, (heads, lanes), 0) == lax.broadcasted_iota(
-        jnp.int32, (heads, lanes), 1
-    )
-    out[28:29, :] = jnp.sum(jnp.where(same, sums, 0.0), axis=0, keepdims=True)
-    for row in range(29, 32):
-        out[row : row + 1, :] = zero
-
-
-def small_gradients(bm, padded, back, unit, scale):
-    depth, height, width, channels = bm.shape
-    tile = 128
-
-    def field(x):
-        return pl.BlockSpec(x.shape[:-1] + (tile,), lambda i: (0, 0, 0, i))
-
+    same = lax.broadcasted_iota(jnp.int32, (heads, channels), 0) == lax.broadcasted_iota(
+        jnp.int32, (heads, channels), 1
+    )
+    small[28:29, :] = jnp.sum(jnp.where(same, sums, 0.0), axis=0, keepdims=True)
+    small[29:32, :] = jnp.zeros((3, channels), F32)
+
+
+def field_back(operands):
+    mixed = operands[4]
+    vmem = pl.BlockSpec(memory_space=pltpu.VMEM)
+    smem = pl.BlockSpec(memory_space=pltpu.SMEM)
+    plane = jax.ShapeDtypeStruct(mixed.shape[1:], BF)
     return pl.pallas_call(
-        tap_gradient_kernel,
-        grid=(channels // tile,),
-        out_shape=jax.ShapeDtypeStruct((32, channels), F32),
-        in_specs=[
-            field(bm),
-            field(padded),
-            field(back),
-            field(unit),
-            pl.BlockSpec(scale.shape, lambda i: (0, 0)),
-        ],
-        out_specs=pl.BlockSpec((32, tile), lambda i: (0, i)),
-        compiler_params=pltpu.CompilerParams(vmem_limit_bytes=16 * 1024 * 1024),
-        cost_estimate=busy(3.5, 3),
-        name="small_gradients",
-    )(bm, padded, back, unit, scale)
+        field_kernel,
+        out_shape=(
+            jax.ShapeDtypeStruct(mixed.shape, F32),
+            plane,
+            plane,
+            jax.ShapeDtypeStruct(mixed.shape, BF),
+            jax.ShapeDtypeStruct((32, mixed.shape[-1]), F32),
+        ),
+        in_specs=[smem] + [vmem] * (len(operands) - 1),
+        out_specs=(vmem,) * 5,
+        compiler_params=pltpu.CompilerParams(vmem_limit_bytes=60 * 1024 * 1024),
+        cost_estimate=busy(1, 2),
+        name="field_back",
+    )(*operands)
 
 
 def per_device(tokens, cotangent, w_qkv, w_proj, conv_weight, norm_gain, head_scale, shift_offsets):
@@ -631,22 +672,9 @@
             att_first,
         ),
     )
-    first_total = sum_square(own, sends, place)
+    first_own, first_sends = own, sends
 
     got_second = swapped(send_second, "seq", 1)
-    own, *sends = chip_gradient(
-        (x_rows, got_first, send_second, got_second, att_rows, cot_window, cot_other)
-    )
-    second_total = sum_square(own, sends, place)
-    first_block = sum_chips(first_total, place, own)
-    second_block = sum_chips(second_total, place)
-    factor = 1.0 / math.sqrt(
-        lax.axis_size("rep") * lax.axis_size("dp") * lax.axis_size("seq") * positions
-    )
-    grad_qkv, grad_proj = assemble(
-        gather_blocks(first_block, place), gather_blocks(second_block, place), place, factor, group
-    )
-
     back_mine, window_send, att_mine = back_through(
         group,
         (
@@ -660,34 +688,62 @@
             att_second,
         ),
     )
-    window_send = after(window_partner(window_send), own, first_total)
-    back_normed = join_columns(back_mine, window_send[:half])
-    restored = join_columns(att_mine, window_send[half:]).reshape(positions, channels)
-    full_proj = rows_of_both(
-        w_proj, weights_got[:, :channels], weights_other[:, :channels], place
-    )
-    projected = jnp.dot(restored, full_proj, preferred_element_type=F32)
-    output = (mixed_field + projected.reshape(slab.shape)).astype(BF)
-
-    back_float = back_normed.astype(F32)
-    grad_unit = back_float * norm_gain
-    back_mixed = cot.astype(F32) + inverse_std * (
-        grad_unit
-        - jnp.mean(grad_unit, axis=-1, keepdims=True)
-        - unit_field * jnp.mean(grad_unit * unit_field, axis=-1, keepdims=True)
-    )
-    edges = back_mixed.astype(BF)
-    inner = swapped(pick(edges, 1 - core, 0), "seq", 1)
-    outer = edge_partner(pick(edges, core, 0))
+    first_total = sum_square(first_own, first_sends, place)
+    own, *sends = chip_gradient(
+        (
+            after(x_rows, back_mine, first_total),
+            got_first,
+            send_second,
+            got_second,
+            att_rows,
+            cot_window,
+            cot_other,
+        )
+    )
+    window_got = after(window_partner(window_send), own)
+    scale_rows = jnp.concatenate([scale_first, scale_second])
+    back_mixed, inner, outer, output, small = field_back(
+        (
+            nums,
+            back_mine,
+            att_mine,
+            window_got,
+            mixed_field,
+            unit_field,
+            inverse_std,
+            cot,
+            padded_tokens,
+            norm_gain[None],
+            scale_rows,
+            w_proj,
+            weights_got,
+            weights_other,
+        )
+    )
+    second_total = sum_square(after(own, small), sends, place)
+    first_block = sum_chips(first_total, place, second_total)
+    steps = sum_steps(after(small, second_total), place)
+    small = next(steps)
+    small = next(steps)
+    second_block = sum_chips(second_total, place)
+    small = next(steps)
+    factor = 1.0 / math.sqrt(
+        lax.axis_size("rep") * lax.axis_size("dp") * lax.axis_size("seq") * positions
+    )
+    grad_qkv, grad_proj = assemble(
+        gather_blocks(first_block, place), gather_blocks(second_block, place, small), place, factor, group
+    )
+    inner = swapped(after(inner, second_total), "seq", 1)
+    outer = edge_partner(after(outer, second_total))
     padded_back = jnp.pad(
         with_halo(back_mixed, inner.astype(F32), outer.astype(F32), core), spatial
     )
     grad_tokens = (
         back_mixed + tap_sum(padded_back, conv_weight, depth, height, width, True)
     ).astype(BF)
-    scale_rows = jnp.concatenate([scale_first, scale_second])
-    small = small_gradients(back_mixed, padded_tokens, back_normed, unit_field, scale_rows)
-    small = sum_everywhere(after(small, second_total), place) * factor
+    for small in steps:
+        pass
+    small = small * factor
     taps = conv_weight.shape[0]
     return (
         output[None],

time: 174 us -> 164 us (0.943)
  Pallas kernels: 42.4 us -> 48.4 us
  starting transfers between devices: 51.9 us -> 46.6 us
  local copies, waits for them, and re-layouts: 16.2 us -> 11.1 us
  other arithmetic: 26.1 us -> 24.1 us
    ppermute x37, starting transfers between devices: 39.9 us -> 34.2 us  [swapped(): return lax.ppermute(x, axis, [(i, i ^ flip) for i in range(count)])]
    unnamed x152 -> x72, local copies, waits for them, and re-layouts: 12.4 us -> 7.05 us
    pallas_call x1, Pallas kernels: 3.34 us -> 7.71 us  [field_back(): pl.pallas_call(field_kernel, out_shape=(jax.ShapeDtypeStruct(mixed.shape,...]
    ppermute x37, waiting for transfers between devices: 25.7 us -> 23.4 us  [swapped(): return lax.ppermute(x, axis, [(i, i ^ flip) for i in range(count)])]
  transfers between devices with their start and end apart: 42 -> 42, of which waited for: 11 -> 12; matrix products, arithmetic and copies ran while one was open for 18% -> 17% of each run, Pallas kernels for 13% -> 15%
where the time goes in v3:
time: 164 us
  Pallas kernels  48.4 us (30%)
  starting transfers between devices  46.6 us (28%)
  waiting for transfers between devices  32.3 us (20%)
  other arithmetic  24.1 us (15%)
  local copies, waits for them, and re-layouts  11.1 us (7%)
    ppermute x37, starting transfers between devices, swapped(): return lax.ppermute(x, axis, [(i, i ^ flip) for i in range(count)])  34.2 us
    ppermute x37, waiting for transfers between devices, swapped(): return lax.ppermute(x, axis, [(i, i ^ flip) for i in range(count)])  23.4 us
    pallas_call x2, Pallas kernels, attention_call(): pl.pallas_call(functools.partial(body, group, head_dim), out_shape=shapes...  20.9 us
    ppermute x3, starting transfers between devices, window_partner(): return lax.ppermute(x, 'seq', pairs)  11 us
    ppermute x3, waiting for transfers between devices, window_partner(): return lax.ppermute(x, 'seq', pairs)  8.92 us
    pallas_call x2, Pallas kernels, chip_gradient(): pl.pallas_call(functools.partial(gradient_kernel, width, has_proj), out_s...  7.83 us
    pallas_call x1, Pallas kernels, field_back(): pl.pallas_call(field_kernel, out_shape=(jax.ShapeDtypeStruct(mixed.shape,...  7.71 us
    unnamed x72, local copies, waits for them, and re-layouts  7.05 us
  transfers between devices with their start and end apart: 42, of which 12 were waited for; matrix products, arithmetic and copies ran while one was open for 17% of the time, Pallas kernels for 15%

profile of v3, /device:TPU:0, one launch (start us, length us, event | category | flops | bytes accessed | tf_op | source)
XLA Modules:
  0.0 163.7 jit_solution(17075036421611537183)
XLA Ops:
  0.7 2.6 %stage.1 = (bf16[192,3072]{1,0:T(8,128)(2,1)}, bf16[8,16,768]{2,1,0:T(8,128)(2,1)}, bf16[8,16,768]{2,1,0:T(8,128)(2,1)}) custom-call(s32[1]{0:T(128)} %bitcast.2.core, bf16[384,2304]{1,0:T(8,128)(2,1)} %w_qkv.7, bf16[384,768]{1,0:T(8,128)(2,1)} %refs_11_.1, bf16[1,2,8,16,768]{4,3,2,1,0:T(8,128)(2,1)} %tokens.1), custom_call_target="tpu_custom_call" | custom-call | flops 12500000 | bytes 400000 | tf_op jit(solution)/shard_map/stage/pallas_call | solution.py:230
  6.0 4.6 %collective-permute-start.1 = (bf16[128,768]{1,0:T(8,128)(2,1)S(1)}, bf16[128,768]{1,0:T(8,128)(2,1)S(1)}, u32[]{:S(2)}, u32[]{:S(2)}) collective-permute-start(bf16[128,768]{1,0:T(8,128)(2,1)S(1)} %bitcast.35), channel_id=1, source_target_pairs={{0,7},{1,2},{2,1},{3,4},{4,3},{5,6},{6,5},{7,0},{8,15},{9,10},{10,... | collective-permute-start | bytes 589832 | tf_op jit(solution)/shard_map/ppermute | solution.py:33
  12.3 3.5 %collective-permute-done.1.refs_1_ = bf16[128,768]{1,0:T(8,128)(2,1)S(1)} collective-permute-done((bf16[128,768]{1,0:T(8,128)(2,1)S(1)}, bf16[128,768]{1,0:T(8,128)(2,1)S(1)}, u32[]{:S(2)}, u32[]{:S(2)}) %collective-permute-start.1) | collective-permute-done | bytes 196640 | tf_op jit(solution)/shard_map/ppermute | solution.py:33
  18.0 3.7 %fusion.78 = (f32[2,8,16]{2,1,0:T(8,128)S(1)}, f32[2,8,16,768]{3,2,1,0:T(8,128)S(1)}) fusion(bf16[4,10,18,768]{3,2,1,0:T(8,128)(2,1)S(1)} %select_maximum_fusion.2.refs_8_, f32[768]{0:T(1024)S(1)} %get-tuple-element.92, f32[768]{0:T(1024)S(1)} %get-tuple-element.93, f32[768]{0:T(1024)S(1)} %get-tuple-element.68, f32[768]{0:T(1024)S(1)} %get-tuple-element.69, ...), kind=kLoop, calls=%fused_computation.192 | loop fusion | flops 16514816 | bytes 11094016 | tf_op jit(solution)/shard_map/reduce_sum | solution.py:632
  23.8 3.3 %collective-permute-start.3 = (bf16[128,768]{1,0:T(8,128)(2,1)S(1)}, bf16[128,768]{1,0:T(8,128)(2,1)S(1)}, u32[]{:S(2)}, u32[]{:S(2)}) collective-permute-start(bf16[128,768]{1,0:T(8,128)(2,1)S(1)} %bitcast.36), channel_id=1, source_target_pairs={{0,7},{1,2},{2,1},{3,4},{4,3},{5,6},{6,5},{7,0},{8,15},{9,10},{10,... | collective-permute-start | bytes 589832 | tf_op jit(solution)/shard_map/ppermute | solution.py:33
  27.1 4.9 %collective-permute-done.3.refs_1_.xg = bf16[128,768]{1,0:T(8,128)(2,1)S(1)} collective-permute-done((bf16[128,768]{1,0:T(8,128)(2,1)S(1)}, bf16[128,768]{1,0:T(8,128)(2,1)S(1)}, u32[]{:S(2)}, u32[]{:S(2)}) %collective-permute-start.3) | collective-permute-done | bytes 196640 | tf_op jit(solution)/shard_map/ppermute | solution.py:33
  32.1 7.0 %collective-permute-done.4.refs_0_ = bf16[192,3072]{1,0:T(8,128)(2,1)S(1)} collective-permute-done((bf16[192,3072]{1,0:T(8,128)(2,1)}, bf16[192,3072]{1,0:T(8,128)(2,1)S(1)}, u32[]{:S(2)}, u32[]{:S(2)}) %collective-permute-start.4) | collective-permute-done | bytes 1179680 | tf_op jit(solution)/shard_map/ppermute | solution.py:27
  44.2 12.8 %first_heads.1 = (bf16[1920,256]{1,0:T(8,128)(2,1)}, bf16[384,256]{1,0:T(8,128)(2,1)}, bf16[512,256]{1,0:T(8,128)(2,1)}, bf16[768,256]{1,0:T(8,128)(2,1)}, f32[16,256]{1,0:T(8,128)}) custom-call(s32[5]{0:T(128)} %pad_add_fusion.nums.refs_0_, f32[24]{0:T(128)} %scale.3, bf16[128,768]{1,0:T(8,128)(2,1)} %bitcast.30, bf16[128,768]{1,0:T(8,128)(2,1)} %copy-done.9, ...), custom_call_target="tpu_custom_call" | custom-call | flops 65000000 | bytes 800000 | tf_op jit(solution)/shard_map/first_heads/pallas_call | solution.py:196
  57.2 2.6 %collective-permute-done.6.refs_1_.refs_3_ = bf16[1920,256]{1,0:T(8,128)(2,1)S(1)} collective-permute-done((bf16[1920,256]{1,0:T(8,128)(2,1)}, bf16[1920,256]{1,0:T(8,128)(2,1)S(1)}, u32[]{:S(2)}, u32[]{:S(2)}) %collective-permute-start.6) | collective-permute-done | bytes 983072 | tf_op jit(solution)/shard_map/ppermute | solution.py:27
  60.8 3.9 %chip_gradient.2 = (f32[96,1536]{1,0:T(8,128)}, bf16[96,1536]{1,0:T(8,128)(2,1)}, bf16[96,1536]{1,0:T(8,128)(2,1)}, bf16[96,1536]{1,0:T(8,128)(2,1)}) custom-call(bf16[384,256]{1,0:T(8,128)(2,1)} %get-tuple-element.42.refs_0_, bf16[1920,256]{1,0:T(8,128)(2,1)} %copy-done.4, bf16[1920,256]{1,0:T(8,128)(2,1)} %get-tuple-element.40.refs_2_.first, ...), custom_call_target="tpu_custom_call" | custom-call | flops 7500000 | bytes 350000 | tf_op jit(solution)/shard_map/chip_gradient/pallas_call | solution.py:392
  64.7 2.4 %collective-permute-start.10 = (bf16[96,1536]{1,0:T(8,128)(2,1)}, bf16[96,1536]{1,0:T(8,128)(2,1)S(1)}, u32[]{:S(2)}, u32[]{:S(2)}) collective-permute-start(bf16[96,1536]{1,0:T(8,128)(2,1)} %get-tuple-element.52), channel_id=1, source_target_pairs={{0,24},{8,16},{16,8},{24,0},{1,25},{9,17},{17,9},{25,1},{2,26},{10... | collective-permute-start | bytes 884744 | tf_op jit(solution)/shard_map/ppermute | solution.py:27
  70.3 8.2 %second_heads.1 = (bf16[1152,256]{1,0:T(8,128)(2,1)}, bf16[384,256]{1,0:T(8,128)(2,1)}, bf16[256,256]{1,0:T(8,128)(2,1)}, f32[8,256]{1,0:T(8,128)}) custom-call(s32[5]{0:T(128)} %pad_add_fusion.nums.refs_0_, f32[24]{0:T(128)} %scale.3, bf16[128,768]{1,0:T(8,128)(2,1)} %bitcast.31, bf16[128,768]{1,0:T(8,128)(2,1)} %copy-done.9, ...), custom_call_target="tpu_custom_call" | custom-call | flops 45000000 | bytes 800000 | tf_op jit(solution)/shard_map/second_heads/pallas_call | solution.py:196
  78.9 5.2 %back_through.1 = (bf16[128,768]{1,0:T(8,128)(2,1)}, bf16[256,768]{1,0:T(8,128)(2,1)}, bf16[128,768]{1,0:T(8,128)(2,1)}) custom-call(s32[5]{0:T(128)} %pad_add_fusion.nums.refs_0_, bf16[1920,256]{1,0:T(8,128)(2,1)} %get-tuple-element.40.refs_2_.first, bf16[1152,256]{1,0:T(8,128)(2,1)} %get-tuple-element.45.second.refs_2_, bf16[384,2304]{1,0:T(8,128)(2,1)} %w_qkv.7, ...), custom_call_target="tpu_custom_call" | custom-call | flops 20000000 | bytes 800000 | tf_op jit(solution)/shard_map/back_through/pallas_call | solution.py:288
  84.7 3.2 %collective-permute-start.7 = (bf16[256,768]{1,0:T(8,128)(2,1)}, bf16[256,768]{1,0:T(8,128)(2,1)S(1)}, u32[]{:S(2)}, u32[]{:S(2)}) collective-permute-start(bf16[256,768]{1,0:T(8,128)(2,1)} %get-tuple-element.49), channel_id=1, source_target_pairs={{0,7},{1,2},{2,1},{3,4},{4,3},{5,6},{6,5},{7,0},{8,15},{9,10},{10,... | collective-permute-start | bytes 1179656 | tf_op jit(solution)/shard_map/ppermute | solution.py:33
  89.8 3.9 %chip_gradient.3 = (f32[96,1536]{1,0:T(8,128)}, bf16[96,1536]{1,0:T(8,128)(2,1)}, bf16[96,1536]{1,0:T(8,128)(2,1)}, bf16[96,1536]{1,0:T(8,128)(2,1)}) custom-call(bf16[384,256]{1,0:T(8,128)(2,1)} %ordered.16.refs_0_, bf16[1920,256]{1,0:T(8,128)(2,1)} %copy-done.4, bf16[1152,256]{1,0:T(8,128)(2,1)} %get-tuple-element.45.second.refs_2_, ...), custom_call_target="tpu_custom_call" | custom-call | flops 7500000 | bytes 350000 | tf_op jit(solution)/shard_map/chip_gradient/pallas_call | solution.py:392
  98.9 7.7 %field_back.1 = (f32[2,8,16,768]{3,2,1,0:T(8,128)}, bf16[8,16,768]{2,1,0:T(8,128)(2,1)}, bf16[8,16,768]{2,1,0:T(8,128)(2,1)}, bf16[2,8,16,768]{3,2,1,0:T(8,128)(2,1)}, f32[32,768]{1,0:T(8,128)}) custom-call(s32[5]{0:T(128)} %pad_add_fusion.nums.refs_0_, bf16[128,768]{1,0:T(8,128)(2,1)} %get-tuple-element.47.refs_1_, ...), custom_call_target="tpu_custom_call" | custom-call | flops 5000000 | bytes 200000 | tf_op jit(solution)/shard_map/field_back/pallas_call | solution.py:572
  106.6 2.9 %collective-permute-start.20 = (bf16[24,1536]{1,0:T(8,128)(2,1)S(1)}, bf16[24,1536]{1,0:T(8,128)(2,1)S(1)}, u32[]{:S(2)}, u32[]{:S(2)}) collective-permute-start(bf16[24,1536]{1,0:T(8,128)(2,1)S(1)} %get-tuple-element.114), channel_id=1, source_target_pairs={{0,6},{1,7},{2,4},{3,5},{4,2},{5,3},{6,0},{7,1},{8,14},{9,15},{10,... | collective-permute-start | bytes 221192 | tf_op jit(solution)/shard_map/ppermute | solution.py:27
  114.9 2.3 %collective-permute-start.29 = (bf16[24,1536]{1,0:T(8,128)(2,1)S(1)}, bf16[24,1536]{1,0:T(8,128)(2,1)S(1)}, u32[]{:S(2)}, u32[]{:S(2)}) collective-permute-start(bf16[24,1536]{1,0:T(8,128)(2,1)S(1)} %get-tuple-element.111), channel_id=1, source_target_pairs={{0,6},{1,7},{2,4},{3,5},{4,2},{5,3},{6,0},{7,1},{8,14},{9,15},{10,... | collective-permute-start | bytes 221192 | tf_op jit(solution)/shard_map/ppermute | solution.py:27
  123.5 2.3 %collective-permute-start.23 = (bf16[24,1536]{1,0:T(8,128)(2,1)S(1)}, bf16[24,1536]{1,0:T(8,128)(2,1)S(1)}, u32[]{:S(2)}, u32[]{:S(2)}) collective-permute-start(bf16[24,1536]{1,0:T(8,128)(2,1)S(1)} %fusion.55), channel_id=1, source_target_pairs={{0,6},{1,7},{2,4},{3,5},{4,2},{5,3},{6,0},{7,1},{8,14},{9,15},{10,... | collective-permute-start | bytes 221192 | tf_op jit(solution)/shard_map/ppermute | solution.py:27
  130.6 2.9 %collective-permute-start.32 = (bf16[24,1536]{1,0:T(8,128)(2,1)S(1)}, bf16[24,1536]{1,0:T(8,128)(2,1)S(1)}, u32[]{:S(2)}, u32[]{:S(2)}) collective-permute-start(bf16[24,1536]{1,0:T(8,128)(2,1)S(1)} %fusion.53), channel_id=1, source_target_pairs={{0,6},{1,7},{2,4},{3,5},{4,2},{5,3},{6,0},{7,1},{8,14},{9,15},{10,... | collective-permute-start | bytes 221192 | tf_op jit(solution)/shard_map/ppermute | solution.py:27
  136.5 3.9 %collective-permute-done.36 = f32[16,768]{1,0:T(8,128)S(1)} collective-permute-done((f32[16,768]{1,0:T(8,128)S(1)}, f32[16,768]{1,0:T(8,128)S(1)}, u32[]{:S(2)}, u32[]{:S(2)}) %collective-permute-start.36) | collective-permute-done | bytes 49184 | tf_op jit(solution)/shard_map/ppermute | solution.py:27
  148.4 3.4 %fusion.51 = bf16[1,2,8,16,768]{4,3,2,1,0:T(8,128)(2,1)} fusion(f32[2,8,16,768]{3,2,1,0:T(8,128)S(1)} %copy-done.7, f32[4,10,18,768]{3,2,1,0:T(8,128)S(1)} %select_maximum_fusion, f32[768]{0:T(1024)S(1)} %get-tuple-element.92, f32[768]{0:T(1024)S(1)} %get-tuple-element.93, f32[768]{0:T(1024)S(1)} %get-tuple-element.68, f32[768]{0:T(1024)S(1)} %get-tuple-element.69, ...), kind=kLoop, calls=%fused_computation.98 | loop fusion | flops 11206656 | bytes 20923392 | tf_op jit(solution)/shard_map/broadcast_in_dim | solution.py:750
  152.4 4.3 %collective-permute-done.37.refs_5_ = bf16[96,1536]{1,0:T(8,128)(2,1)S(1)} collective-permute-done((bf16[96,1536]{1,0:T(8,128)(2,1)S(1)}, bf16[96,1536]{1,0:T(8,128)(2,1)S(1)}, u32[]{:S(2)}, u32[]{:S(2)}) %collective-permute-start.37) | collective-permute-done | bytes 294944 | tf_op jit(solution)/shard_map/ppermute | solution.py:27
  159.5 4.1 %assemble.1 = (f32[384,2304]{1,0:T(8,128)}, f32[384,768]{1,0:T(8,128)}) custom-call(s32[3]{0:T(128)} %pad_add_fusion.1.at, bf16[96,1536]{1,0:T(8,128)(2,1)} %copy-done.12, bf16[96,1536]{1,0:T(8,128)(2,1)} %copy-done.20, bf16[96,1536]{1,0:T(8,128)(2,1)} %copy-done.21, bf16[96,1536]{1,0:T(8,128)(2,1)} %copy-done.24, bf16[96,1536]{1,0:T(8,128)(2,1)} %copy-done.13, ...), custom_call_target="tpu_custom_call" | custom-call | flops 15000000 | bytes 700000 | tf_op jit(solution)/shard_map/assemble/pallas_call | solution.py:459
  (195 shorter events, 57.1 us)
Async XLA Ops:
  10.5 28.6 %collective-permute-start.4 = (bf16[192,3072]{1,0:T(8,128)(2,1)}, bf16[192,3072]{1,0:T(8,128)(2,1)S(1)}, u32[]{:S(2)}, u32[]{:S(2)}) collective-permute-start(bf16[192,3072]{1,0:T(8,128)(2,1)} %get-tuple-element.39), channel_id=1, source_target_pairs={{0,8},{8,0},{1,9},{9,1},{2,10},{10,2},{3,11},{11,3},{4,12},{12,4},... | collective-permute-start | bytes 3538952 | tf_op jit(solution)/shard_map/ppermute | solution.py:27
  64.7 20.0 %collective-permute-start.10 = (bf16[96,1536]{1,0:T(8,128)(2,1)}, bf16[96,1536]{1,0:T(8,128)(2,1)S(1)}, u32[]{:S(2)}, u32[]{:S(2)}) collective-permute-start(bf16[96,1536]{1,0:T(8,128)(2,1)} %get-tuple-element.52), channel_id=1, source_target_pairs={{0,24},{8,16},{16,8},{24,0},{1,25},{9,17},{17,9},{25,1},{2,26},{10... | collective-permute-start | bytes 884744 | tf_op jit(solution)/shard_map/ppermute | solution.py:27
  67.1 20.8 %collective-permute-start.8 = (bf16[96,1536]{1,0:T(8,128)(2,1)}, bf16[96,1536]{1,0:T(8,128)(2,1)S(1)}, u32[]{:S(2)}, u32[]{:S(2)}) collective-permute-start(bf16[96,1536]{1,0:T(8,128)(2,1)} %get-tuple-element.50), channel_id=1, source_target_pairs={{0,8},{8,0},{16,24},{24,16},{1,9},{9,1},{17,25},{25,17},{2,10},{10... | collective-permute-start | bytes 884744 | tf_op jit(solution)/shard_map/ppermute | solution.py:27
  67.7 20.3 %collective-permute-start.9 = (bf16[96,1536]{1,0:T(8,128)(2,1)}, bf16[96,1536]{1,0:T(8,128)(2,1)S(1)}, u32[]{:S(2)}, u32[]{:S(2)}) collective-permute-start(bf16[96,1536]{1,0:T(8,128)(2,1)} %get-tuple-element.51), channel_id=1, source_target_pairs={{0,16},{8,24},{16,0},{24,8},{1,17},{9,25},{17,1},{25,9},{2,18},{10... | collective-permute-start | bytes 884744 | tf_op jit(solution)/shard_map/ppermute | solution.py:27
  69.4 19.5 %collective-permute-start.12 = (bf16[256,768]{1,0:T(8,128)(2,1)S(1)}, bf16[256,768]{1,0:T(8,128)(2,1)S(1)}, u32[]{:S(2)}, u32[]{:S(2)}) collective-permute-start(bf16[256,768]{1,0:T(8,128)(2,1)S(1)} %copy-done.6), channel_id=1, source_target_pairs={{0,1},{1,0},{2,3},{3,2},{4,5},{5,4},{6,7},{7,6},{8,9},{9,8},{10,11... | collective-permute-start | bytes 1179656 | tf_op jit(solution)/shard_map/ppermute | solution.py:27
  78.4 10.5 %collective-permute-start.11 = (bf16[1152,256]{1,0:T(8,128)(2,1)}, bf16[1152,256]{1,0:T(8,128)(2,1)S(1)}, u32[]{:S(2)}, u32[]{:S(2)}) collective-permute-start(bf16[1152,256]{1,0:T(8,128)(2,1)} %get-tuple-element.45.second.refs_2_), channel_id=1, source_target_pairs={{0,1},{1,0},{2,3},{3,2},{4,5},{5,4},{6,7},{7,6},{8,9},{9,8},{10,11... | collective-permute-start | bytes 1769480 | tf_op jit(solution)/shard_map/ppermute | solution.py:27
  84.7 13.1 %collective-permute-start.7 = (bf16[256,768]{1,0:T(8,128)(2,1)}, bf16[256,768]{1,0:T(8,128)(2,1)S(1)}, u32[]{:S(2)}, u32[]{:S(2)}) collective-permute-start(bf16[256,768]{1,0:T(8,128)(2,1)} %get-tuple-element.49), channel_id=1, source_target_pairs={{0,7},{1,2},{2,1},{3,4},{4,3},{5,6},{6,5},{7,0},{8,15},{9,10},{10,... | collective-permute-start | bytes 1179656 | tf_op jit(solution)/shard_map/ppermute | solution.py:33
  93.8 12.9 %collective-permute-start.13 = (bf16[96,1536]{1,0:T(8,128)(2,1)}, bf16[96,1536]{1,0:T(8,128)(2,1)S(1)}, u32[]{:S(2)}, u32[]{:S(2)}) collective-permute-start(bf16[96,1536]{1,0:T(8,128)(2,1)} %get-tuple-element.61), channel_id=1, source_target_pairs={{0,8},{8,0},{16,24},{24,16},{1,9},{9,1},{17,25},{25,17},{2,10},{10... | collective-permute-start | bytes 884744 | tf_op jit(solution)/shard_map/ppermute | solution.py:27
  95.3 14.2 %collective-permute-start.14 = (bf16[96,1536]{1,0:T(8,128)(2,1)}, bf16[96,1536]{1,0:T(8,128)(2,1)S(1)}, u32[]{:S(2)}, u32[]{:S(2)}) collective-permute-start(bf16[96,1536]{1,0:T(8,128)(2,1)} %get-tuple-element.62), channel_id=1, source_target_pairs={{0,16},{8,24},{16,0},{24,8},{1,17},{9,25},{17,1},{25,9},{2,18},{10... | collective-permute-start | bytes 884744 | tf_op jit(solution)/shard_map/ppermute | solution.py:27
  96.8 12.8 %collective-permute-start.15 = (bf16[96,1536]{1,0:T(8,128)(2,1)}, bf16[96,1536]{1,0:T(8,128)(2,1)S(1)}, u32[]{:S(2)}, u32[]{:S(2)}) collective-permute-start(bf16[96,1536]{1,0:T(8,128)(2,1)} %get-tuple-element.63), channel_id=1, source_target_pairs={{0,24},{8,16},{16,8},{24,0},{1,25},{9,17},{17,9},{25,1},{2,26},{10... | collective-permute-start | bytes 884744 | tf_op jit(solution)/shard_map/ppermute | solution.py:27
  97.3 15.9 %collective-permute-start.18 = (bf16[24,1536]{1,0:T(8,128)(2,1)S(1)}, bf16[24,1536]{1,0:T(8,128)(2,1)S(1)}, u32[]{:S(2)}, u32[]{:S(2)}) collective-permute-start(bf16[24,1536]{1,0:T(8,128)(2,1)S(1)} %get-tuple-element.113), channel_id=1, source_target_pairs={{0,2},{1,3},{2,0},{3,1},{4,6},{5,7},{6,4},{7,5},{8,10},{9,11},{10,... | collective-permute-start | bytes 221192 | tf_op jit(solution)/shard_map/ppermute | solution.py:27
  97.9 17.0 %collective-permute-start.19 = (bf16[24,1536]{1,0:T(8,128)(2,1)S(1)}, bf16[24,1536]{1,0:T(8,128)(2,1)S(1)}, u32[]{:S(2)}, u32[]{:S(2)}) collective-permute-start(bf16[24,1536]{1,0:T(8,128)(2,1)S(1)} %get-tuple-element.115), channel_id=1, source_target_pairs={{0,4},{1,5},{2,6},{3,7},{4,0},{5,1},{6,2},{7,3},{8,12},{9,13},{10,... | collective-permute-start | bytes 221192 | tf_op jit(solution)/shard_map/ppermute | solution.py:27
  106.6 10.5 %collective-permute-start.20 = (bf16[24,1536]{1,0:T(8,128)(2,1)S(1)}, bf16[24,1536]{1,0:T(8,128)(2,1)S(1)}, u32[]{:S(2)}, u32[]{:S(2)}) collective-permute-start(bf16[24,1536]{1,0:T(8,128)(2,1)S(1)} %get-tuple-element.114), channel_id=1, source_target_pairs={{0,6},{1,7},{2,4},{3,5},{4,2},{5,3},{6,0},{7,1},{8,14},{9,15},{10,... | collective-permute-start | bytes 221192 | tf_op jit(solution)/shard_map/ppermute | solution.py:27
  112.4 11.1 %collective-permute-start.27 = (bf16[24,1536]{1,0:T(8,128)(2,1)S(1)}, bf16[24,1536]{1,0:T(8,128)(2,1)S(1)}, u32[]{:S(2)}, u32[]{:S(2)}) collective-permute-start(bf16[24,1536]{1,0:T(8,128)(2,1)S(1)} %get-tuple-element.110), channel_id=1, source_target_pairs={{0,2},{1,3},{2,0},{3,1},{4,6},{5,7},{6,4},{7,5},{8,10},{9,11},{10,... | collective-permute-start | bytes 221192 | tf_op jit(solution)/shard_map/ppermute | solution.py:27
  113.1 12.7 %collective-permute-start.28 = (bf16[24,1536]{1,0:T(8,128)(2,1)S(1)}, bf16[24,1536]{1,0:T(8,128)(2,1)S(1)}, u32[]{:S(2)}, u32[]{:S(2)}) collective-permute-start(bf16[24,1536]{1,0:T(8,128)(2,1)S(1)} %get-tuple-element.112), channel_id=1, source_target_pairs={{0,4},{1,5},{2,6},{3,7},{4,0},{5,1},{6,2},{7,3},{8,12},{9,13},{10,... | collective-permute-start | bytes 221192 | tf_op jit(solution)/shard_map/ppermute | solution.py:27
  114.9 11.6 %collective-permute-start.29 = (bf16[24,1536]{1,0:T(8,128)(2,1)S(1)}, bf16[24,1536]{1,0:T(8,128)(2,1)S(1)}, u32[]{:S(2)}, u32[]{:S(2)}) collective-permute-start(bf16[24,1536]{1,0:T(8,128)(2,1)S(1)} %get-tuple-element.111), channel_id=1, source_target_pairs={{0,6},{1,7},{2,4},{3,5},{4,2},{5,3},{6,0},{7,1},{8,14},{9,15},{10,... | collective-permute-start | bytes 221192 | tf_op jit(solution)/shard_map/ppermute | solution.py:27
  121.3 12.3 %collective-permute-start.21 = (bf16[24,1536]{1,0:T(8,128)(2,1)S(1)}, bf16[24,1536]{1,0:T(8,128)(2,1)S(1)}, u32[]{:S(2)}, u32[]{:S(2)}) collective-permute-start(bf16[24,1536]{1,0:T(8,128)(2,1)S(1)} %fusion.55), channel_id=1, source_target_pairs={{0,2},{1,3},{2,0},{3,1},{4,6},{5,7},{6,4},{7,5},{8,10},{9,11},{10,... | collective-permute-start | bytes 221192 | tf_op jit(solution)/shard_map/ppermute | solution.py:27
  122.8 10.8 %collective-permute-start.22 = (bf16[24,1536]{1,0:T(8,128)(2,1)S(1)}, bf16[24,1536]{1,0:T(8,128)(2,1)S(1)}, u32[]{:S(2)}, u32[]{:S(2)}) collective-permute-start(bf16[24,1536]{1,0:T(8,128)(2,1)S(1)} %fusion.55), channel_id=1, source_target_pairs={{0,4},{1,5},{2,6},{3,7},{4,0},{5,1},{6,2},{7,3},{8,12},{9,13},{10,... | collective-permute-start | bytes 221192 | tf_op jit(solution)/shard_map/ppermute | solution.py:27
  123.5 11.6 %collective-permute-start.23 = (bf16[24,1536]{1,0:T(8,128)(2,1)S(1)}, bf16[24,1536]{1,0:T(8,128)(2,1)S(1)}, u32[]{:S(2)}, u32[]{:S(2)}) collective-permute-start(bf16[24,1536]{1,0:T(8,128)(2,1)S(1)} %fusion.55), channel_id=1, source_target_pairs={{0,6},{1,7},{2,4},{3,5},{4,2},{5,3},{6,0},{7,1},{8,14},{9,15},{10,... | collective-permute-start | bytes 221192 | tf_op jit(solution)/shard_map/ppermute | solution.py:27
  125.8 19.1 %collective-permute-start.16 = (bf16[8,16,768]{2,1,0:T(8,128)(2,1)}, bf16[8,16,768]{2,1,0:T(8,128)(2,1)S(1)}, u32[]{:S(2)}, u32[]{:S(2)}) collective-permute-start(bf16[8,16,768]{2,1,0:T(8,128)(2,1)} %ordered.19), channel_id=1, source_target_pairs={{1,2},{3,4},{5,6},{2,1},{4,3},{6,5},{9,10},{11,12},{13,14},{10,9},... | collective-permute-start | bytes 589832 | tf_op jit(solution)/shard_map/ppermute | solution.py:39
  140.9 11.0 %collective-permute-start.24 = (bf16[96,1536]{1,0:T(8,128)(2,1)S(1)}, bf16[96,1536]{1,0:T(8,128)(2,1)S(1)}, u32[]{:S(2)}, u32[]{:S(2)}) collective-permute-start(bf16[96,1536]{1,0:T(8,128)(2,1)S(1)} %pad_maximum_fusion.5.refs_0_), channel_id=1, source_target_pairs={{0,16},{16,0},{1,17},{17,1},{2,18},{18,2},{3,19},{19,3},{4,20},{20... | collective-permute-start | bytes 884744 | tf_op jit(solution)/shard_map/ppermute | solution.py:27
  141.6 16.3 %collective-permute-start.25 = (bf16[96,1536]{1,0:T(8,128)(2,1)S(1)}, bf16[96,1536]{1,0:T(8,128)(2,1)S(1)}, u32[]{:S(2)}, u32[]{:S(2)}) collective-permute-start(bf16[96,1536]{1,0:T(8,128)(2,1)S(1)} %pad_maximum_fusion.5.refs_0_), channel_id=1, source_target_pairs={{0,1},{1,0},{2,3},{3,2},{4,5},{5,4},{6,7},{7,6},{8,9},{9,8},{10,11... | collective-permute-start | bytes 884744 | tf_op jit(solution)/shard_map/ppermute | solution.py:27
  144.9 11.8 %collective-permute-start.37 = (bf16[96,1536]{1,0:T(8,128)(2,1)S(1)}, bf16[96,1536]{1,0:T(8,128)(2,1)S(1)}, u32[]{:S(2)}, u32[]{:S(2)}) collective-permute-start(bf16[96,1536]{1,0:T(8,128)(2,1)S(1)} %pad_maximum_fusion.6.refs_4_), channel_id=1, source_target_pairs={{0,16},{16,0},{1,17},{17,1},{2,18},{18,2},{3,19},{19,3},{4,20},{20... | collective-permute-start | bytes 884744 | tf_op jit(solution)/shard_map/ppermute | solution.py:27
  146.1 11.8 %collective-permute-start.38 = (bf16[96,1536]{1,0:T(8,128)(2,1)S(1)}, bf16[96,1536]{1,0:T(8,128)(2,1)S(1)}, u32[]{:S(2)}, u32[]{:S(2)}) collective-permute-start(bf16[96,1536]{1,0:T(8,128)(2,1)S(1)} %pad_maximum_fusion.6.refs_4_), channel_id=1, source_target_pairs={{0,1},{1,0},{2,3},{3,2},{4,5},{5,4},{6,7},{7,6},{8,9},{9,8},{10,11... | collective-permute-start | bytes 884744 | tf_op jit(solution)/shard_map/ppermute | solution.py:27
  (54 other events, 330.9 us)

commit v4 on v3

--- a/solution.py
+++ b/solution.py
@@ -76,7 +76,7 @@
     return jnp.where(code(0) == code(1), 1.0, 0.0).astype(F32)
 
 
-def project(nums, x, mine, low, got, other, group, qkv):
+def project(nums, x, mine, got, other, group, qkv):
     channels = x.shape[1]
     half = channels // 2
     quarter = half // 2
@@ -88,11 +88,9 @@
     x_other = jnp.where(low_core, x_peer[:, quarter:], x_peer[:, :quarter]).astype(BF)
     x_mine = x_mine.astype(BF)
     for part in range(3):
-        own = slice(part * channels + low, part * channels + low + group)
-        far = slice(own.start + channels, own.stop + channels)
-        total = jnp.dot(x_mine, mine[:, own], preferred_element_type=F32)
-        total = total + jnp.dot(x_got, got[:, far], preferred_element_type=F32)
-        total = total + jnp.dot(x_other, other[:, far], preferred_element_type=F32)
+        total = jnp.dot(x_mine, mine(part), preferred_element_type=F32)
+        total = total + jnp.dot(x_got, got(part), preferred_element_type=F32)
+        total = total + jnp.dot(x_other, other(part), preferred_element_type=F32)
         qkv[part * group : (part + 1) * group, :] = total.T.astype(BF)
 
 
@@ -133,20 +131,28 @@
         back[rows(group), :] = radius_back(kf, ik, buk).astype(BF)
         back[rows(2 * group), :] = bv.astype(BF)
 
+    count = group // head_dim
+    unrolled = math.gcd(count, 10) if count > 8 else count
+
     def body(i, carry):
-        for u in range(8):
-            one_head(i * 8 + u)
+        for u in range(unrolled):
+            one_head(i * unrolled + u)
         return carry
 
-    lax.fori_loop(0, group // head_dim // 8, body, 0)
-
-
-def first_kernel(group, head_dim, nums, scale, xm, xg, cot, order, w_qkv, w_proj, got, other, *outs):
-    send, x_rows, att, ba, gs, qkv = outs
+    lax.fori_loop(0, count // unrolled, body, 0)
+
+
+def first_kernel(group, head_dim, nums, scale, xm, xg, cot, w_qkv, w_proj, got, other, *outs):
+    send, att, ba, gs, qkv = outs
     channels = xm.shape[1]
     half = channels // 2
     x = jnp.concatenate([xm[...], xg[...]], axis=0)
-    project(nums, x, w_qkv, 0, got, other, group, qkv)
+
+    def columns(ref, base):
+        return lambda part: ref[:, base + part * channels : base + part * channels + group]
+
+    far = (columns(got, channels), columns(other, channels))
+    project(nums, x, columns(w_qkv, 0), *far, group, qkv)
     quarter = half // 2
     dp, core = nums[3], nums[4]
 
@@ -159,21 +165,16 @@
     back_rows((1 - dp) * half + (1 - core) * quarter, quarter, other[:, :channels])
     allowed = allowed_pairs(nums, x.shape[0])
     attend(head_dim, allowed, scale, 0, group, qkv, ba, 0, att, send, gs)
-    x_rows[...] = lax.dot_general(
-        order[:half, :], x, OVER_LANES, preferred_element_type=F32
-    ).astype(BF)
-    send[3 * group :, :] = lax.dot_general(
-        order[half:, :], x, OVER_LANES, preferred_element_type=F32
-    ).astype(BF)
-
-
-def second_kernel(group, head_dim, nums, scale, xm, xg, order, w_qkv, got, other, ba, att_first, *outs):
-    send, att_rows, att, gs, qkv = outs
+
+
+def second_kernel(group, head_dim, nums, scale, xm, xg, order, ba, att_first, *refs):
+    weights, (send, att_rows, att, gs, qkv) = refs[:9], refs[9:]
     channels = xm.shape[1]
     half = channels // 2
     low = channels - group
     x = jnp.concatenate([xm[...], xg[...]], axis=0)
-    project(nums, x, w_qkv, low, got, other, group, qkv)
+    mine, got, other = [lambda part, refs=weights[i : i + 3]: refs[part][...] for i in (0, 3, 6)]
+    project(nums, x, mine, got, other, group, qkv)
     allowed = allowed_pairs(nums, x.shape[0])
     attend(head_dim, allowed, scale, low // head_dim, group, qkv, ba, low, att, send, gs)
 
@@ -186,20 +187,25 @@
     send[3 * group :, :] = ordered(slice(half, channels))
 
 
-def attention_call(body, name, group, head_dim, head_count, outs, operands):
+def attention_call(body, name, group, head_dim, head_count, outs, operands, columns=()):
     n = 2 * operands[2].shape[0]
     channels = operands[2].shape[1]
     vmem = pl.BlockSpec(memory_space=pltpu.VMEM)
     smem = pl.BlockSpec(memory_space=pltpu.SMEM)
+    tail = operands[len(operands) - len(columns) :]
+    blocks = [
+        pl.BlockSpec((x.shape[0], wide), lambda i, at=at: (0, at)) for x, (wide, at) in zip(tail, columns)
+    ]
     shapes = tuple(jax.ShapeDtypeStruct((rows, n), BF) for rows in outs)
     shapes = shapes + (jax.ShapeDtypeStruct((group // head_dim, n), F32),)
     return pl.pallas_call(
         functools.partial(body, group, head_dim),
+        grid=(1,),
         out_shape=shapes,
-        in_specs=[smem, smem] + [vmem] * (len(operands) - 2),
+        in_specs=[smem, smem] + [vmem] * (len(operands) - 2 - len(columns)) + blocks,
         out_specs=(vmem,) * len(shapes),
         scratch_shapes=[pltpu.VMEM((3 * group, n), BF)],
-        compiler_params=pltpu.CompilerParams(vmem_limit_bytes=60 * 1024 * 1024),
+        compiler_params=pltpu.CompilerParams(vmem_limit_bytes=(60 if columns else 24) * 1024 * 1024),
         cost_estimate=busy(5 + 0.5 * (group // head_dim), 8),
         name=name,
     )(*operands)
@@ -362,7 +368,7 @@
         xm, xg, bm, bg, own, s1, s2, s3 = refs
     quarter = own.shape[0]
     tile = 384
-    x_far = xg[xg.shape[0] - 4 * quarter :, :]
+    x_far = xg[...]
 
     def put(first, total):
         columns = slice(first, first + tile)
@@ -382,9 +388,9 @@
             put(width + first, total + jnp.dot(far, cg[:, columns], preferred_element_type=F32))
 
 
-def chip_gradient(operands):
+def chip_gradient(group, operands):
     rows, n = operands[0].shape
-    width = operands[2].shape[0] - rows
+    width = 3 * group
     has_proj = len(operands) > 4
     total = width + (operands[5].shape[1] if has_proj else 0)
     vmem = pl.BlockSpec(memory_space=pltpu.VMEM)
@@ -394,7 +400,7 @@
         out_shape=(jax.ShapeDtypeStruct((rows // 4, total), F32), wire, wire, wire),
         in_specs=[vmem] * len(operands),
         out_specs=(vmem,) * 4,
-        compiler_params=pltpu.CompilerParams(vmem_limit_bytes=60 * 1024 * 1024),
+        compiler_params=pltpu.CompilerParams(vmem_limit_bytes=12 * 1024 * 1024),
         cost_estimate=busy(1.5, 3.5),
         name="chip_gradient",
     )(*operands)
@@ -410,7 +416,7 @@
     got = [parts[0]]
     for k in range(1, place.split):
         there = swapped(parts[k].astype(BF), "seq", 2 * k)
-        got.append((after(there, *others) if others else there).astype(F32))
+        got.append((after(there, *others) if others and k == 1 else there).astype(F32))
     total = tree_sum(got)
     for radix, stride in place.stages[1:]:
         held = total.astype(BF)
@@ -437,10 +443,10 @@
     for pair in range(2):
         for square in range(2):
             index = 2 * pair + square
-            base = ((at[0] ^ pair) * 2 + (at[1] ^ square)) * split
+            base = ((at[4] ^ pair) * 2 + (at[5] ^ square)) * split
             for z in range(split):
                 here = slice(z * rows, (z + 1) * rows)
-                there = pl.ds(pl.multiple_of((base + (at[2] ^ z)) * rows, rows), rows)
+                there = pl.ds(pl.multiple_of((base + (at[6] ^ z)) * rows, rows), rows)
                 for part in range(3):
                     low, mid = part * third, part * third + group
                     a = first[index][here, part * group : (part + 1) * group]
@@ -450,12 +456,11 @@
                 proj[there, :] = second[index][here, 3 * rest :].astype(F32) * factor
 
 
-def assemble(first, second, place, factor, group):
+def assemble(nums, first, second, place, factor, group):
     rows = 4 * first[0].shape[0]
     channels = place.channels
     vmem = pl.BlockSpec(memory_space=pltpu.VMEM)
     smem = pl.BlockSpec(memory_space=pltpu.SMEM)
-    at = jnp.stack([place.core, place.rep, place.digit]).astype(jnp.int32)
     return pl.pallas_call(
         functools.partial(assemble_kernel, place.split, factor, group),
         out_shape=(
@@ -464,10 +469,10 @@
         ),
         in_specs=[smem] + [vmem] * 8,
         out_specs=(vmem, vmem),
-        compiler_params=pltpu.CompilerParams(vmem_limit_bytes=60 * 1024 * 1024),
+        compiler_params=pltpu.CompilerParams(vmem_limit_bytes=16 * 1024 * 1024),
         cost_estimate=busy(3, 7),
         name="assemble",
-    )(at, *first, *second)
+    )(nums, *first, *second)
 
 
 def sum_steps(x, place):
@@ -500,7 +505,7 @@
     )
 
 
-GROUP_HEADS = 16
+GROUP_HEADS = 20
 
 
 def into_field(nums, mine, theirs):
@@ -513,9 +518,9 @@
 
 
 def field_kernel(*refs):
-    nums, back, att, got, mixed, unit, inverse, cot, padded, gain, scale = refs[:11]
-    w_mine, w_got, w_other = refs[11:14]
-    bm, inner, outer, out, small = refs[14:]
+    nums, back, att, got, mixed, cot, padded, gain, scale1, scale2 = refs[:10]
+    w_mine, w_got, w_other = refs[10:13]
+    bm, inner, outer, out, small = refs[13:]
     depth, height, width, channels = mixed.shape
     half = back.shape[0]
     rows = depth * height
@@ -527,17 +532,19 @@
     r_got = jnp.where(low_core, r_peer[:, :part], r_peer[:, part:]).astype(BF)
     r_other = jnp.where(low_core, r_peer[:, part:], r_peer[:, :part]).astype(BF)
     projected = jnp.dot(r_mine, w_mine[...], preferred_element_type=F32)
-    projected = projected + jnp.dot(r_got, w_got[:, :channels], preferred_element_type=F32)
-    projected = projected + jnp.dot(r_other, w_other[:, :channels], preferred_element_type=F32)
+    projected = projected + jnp.dot(r_got, w_got[...], preferred_element_type=F32)
+    projected = projected + jnp.dot(r_other, w_other[...], preferred_element_type=F32)
     out[...] = (mixed[...] + projected.reshape(mixed.shape)).astype(BF)
 
     normed = into_field(nums, back[...], got[:half, :])
-    field = unit[...].reshape(rows, width, channels)
+    field = mixed[...].reshape(rows, width, channels)
+    field = field - jnp.mean(field, axis=-1, keepdims=True)
+    std = lax.rsqrt(jnp.mean(field * field, axis=-1, keepdims=True) + 1e-05)
+    field = field * std
     small[27:28, :] = jnp.sum(jnp.sum(normed * field, axis=0), axis=0, keepdims=True)
     grad = normed * gain[...].reshape(1, 1, channels)
     mean = jnp.mean(grad, axis=-1, keepdims=True)
     slope = jnp.mean(grad * field, axis=-1, keepdims=True)
-    std = inverse[...].reshape(rows, width, 1)
     value = cot[...].astype(F32).reshape(rows, width, channels) + std * (grad - mean - field * slope)
     bm[...] = value.reshape(mixed.shape)
     first, last = value[:height].astype(BF), value[rows - height :].astype(BF)
@@ -555,7 +562,8 @@
                     product = mixed_back * shifted[a : a + depth, b : b + height]
                     row = jnp.sum(jnp.sum(product, axis=(0, 1)), axis=0, keepdims=True)
                     small[9 * a + 3 * b + e : 9 * a + 3 * b + e + 1, lanes] = row
-    sums = jnp.sum(scale[...], axis=1, keepdims=True)
+    sums = jnp.concatenate([scale1[...], scale2[...]], axis=0)
+    sums = jnp.sum(sums, axis=1, keepdims=True)
     heads = sums.shape[0]
     same = lax.broadcasted_iota(jnp.int32, (heads, channels), 0) == lax.broadcasted_iota(
         jnp.int32, (heads, channels), 1
@@ -566,11 +574,14 @@
 
 def field_back(operands):
     mixed = operands[4]
+    channels = mixed.shape[-1]
+    first_columns = pl.BlockSpec((operands[-1].shape[0], channels), lambda i: (0, 0))
     vmem = pl.BlockSpec(memory_space=pltpu.VMEM)
     smem = pl.BlockSpec(memory_space=pltpu.SMEM)
     plane = jax.ShapeDtypeStruct(mixed.shape[1:], BF)
     return pl.pallas_call(
         field_kernel,
+        grid=(1,),
         out_shape=(
             jax.ShapeDtypeStruct(mixed.shape, F32),
             plane,
@@ -578,7 +589,7 @@
             jax.ShapeDtypeStruct(mixed.shape, BF),
             jax.ShapeDtypeStruct((32, mixed.shape[-1]), F32),
         ),
-        in_specs=[smem] + [vmem] * (len(operands) - 1),
+        in_specs=[smem] + [vmem] * (len(operands) - 3) + [first_columns] * 2,
         out_specs=(vmem,) * 5,
         compiler_params=pltpu.CompilerParams(vmem_limit_bytes=60 * 1024 * 1024),
         cost_estimate=busy(1, 2),
@@ -624,7 +635,7 @@
     cot_got = window_partner(cot_theirs)
     padded_tokens = jnp.pad(with_halo(slab, inner, after(outer, cot_got), core), spatial)
     cot_window = jnp.concatenate([cot_mine, cot_got])
-    order = place.row_order()
+    order = after(place.row_order(), cot_got)
 
     mixed_field = slab.astype(F32) + tap_sum(
         padded_tokens, conv_weight, depth, height, width, False
@@ -635,23 +646,34 @@
     normed = (unit_field * norm_gain).astype(BF)
     x_mine, x_theirs = split_columns(normed)
     x_theirs = window_partner(x_theirs)
-    weights_got = after(weights_got, x_theirs)
+    x_rows = jnp.einsum(
+        "pc,tc->pt",
+        order,
+        jnp.concatenate([x_mine, x_theirs]),
+        preferred_element_type=F32,
+    ).astype(BF)
+    x_other = swapped(x_rows[channels // 2 :], "seq", 1)
+    x_rows = x_rows[: channels // 2]
+    weights_got = after(weights_got, x_other)
     weights_other = swapped(weights_got, "seq", 1)
     cot_other = swapped(cot_window, "seq", 1)
-    nums = jnp.stack([rows_shift, cols_shift, 1 - core, dp, core]).astype(jnp.int32)
+    nums = jnp.stack(
+        [rows_shift, cols_shift, 1 - core, dp, core, place.rep, place.digit]
+    ).astype(jnp.int32)
     half_rows = channels // 2
-    send_first, x_rows, att_first, back_attended, scale_first = attention_call(
+    send_first, att_first, back_attended, scale_first = attention_call(
         first_kernel,
         "first_heads",
         group,
         head_dim,
         head_count,
-        (3 * group + half_rows, half_rows, group, channels),
-        (nums, head_scale, x_mine, x_theirs, cot_window, order, w_qkv, w_proj, weights_got, weights_other),
+        (3 * group, group, channels),
+        (nums, head_scale, x_mine, x_theirs, cot_window, w_qkv, w_proj, weights_got, weights_other),
     )
     got_first = swapped(send_first, "seq", 1)
-    own, *sends = chip_gradient((x_rows, got_first, send_first, got_first))
+    own, *sends = chip_gradient(group, (x_rows, x_other, send_first, got_first))
     rest = channels - group
+    parts = [part * channels + group for part in range(3)]
     send_second, att_rows, att_second, scale_second = attention_call(
         second_kernel,
         "second_heads",
@@ -665,12 +687,14 @@
             x_mine,
             x_theirs,
             order,
-            w_qkv,
-            weights_got,
-            weights_other,
             after(back_attended, own),
             att_first,
+            *[w_qkv] * 3,
+            *[weights_got] * 3,
+            *[weights_other] * 3,
         ),
+        [(rest, base // rest) for base in parts]
+        + [(rest, (base + channels) // rest) for base in parts] * 2,
     )
     first_own, first_sends = own, sends
 
@@ -690,9 +714,10 @@
     )
     first_total = sum_square(first_own, first_sends, place)
     own, *sends = chip_gradient(
+        rest,
         (
             after(x_rows, back_mine, first_total),
-            got_first,
+            x_other,
             send_second,
             got_second,
             att_rows,
@@ -701,7 +726,6 @@
         )
     )
     window_got = after(window_partner(window_send), own)
-    scale_rows = jnp.concatenate([scale_first, scale_second])
     back_mixed, inner, outer, output, small = field_back(
         (
             nums,
@@ -709,12 +733,11 @@
             att_mine,
             window_got,
             mixed_field,
-            unit_field,
-            inverse_std,
             cot,
             padded_tokens,
-            norm_gain[None],
-            scale_rows,
+            norm_gain,
+            scale_first,
+            scale_second,
             w_proj,
             weights_got,
             weights_other,
@@ -731,7 +754,7 @@
         lax.axis_size("rep") * lax.axis_size("dp") * lax.axis_size("seq") * positions
     )
     grad_qkv, grad_proj = assemble(
-        gather_blocks(first_block, place), gather_blocks(second_block, place, small), place, factor, group
+        nums, gather_blocks(first_block, place), gather_blocks(second_block, place, small), place, factor, group
     )
     inner = swapped(after(inner, second_total), "seq", 1)
     outer = edge_partner(after(outer, second_total))

time: 164 us -> 157 us (0.957)
  Pallas kernels: 48.4 us -> 38.6 us
  waiting for transfers between devices: 32.3 us -> 25.9 us
  starting transfers between devices: 46.6 us -> 50 us
  local copies, waits for them, and re-layouts: 11.1 us -> 13.6 us
  matrix products: 0 us -> 1.99 us
    pallas_call x3, Pallas kernels: 28.6 us -> 23.4 us  [the longest x2 16.5 us: attention_call(): pl.pallas_call(functools.partial(body, group, head_dim), grid=(1,), out_s...]
    ppermute x37 -> x38, waiting for transfers between devices: 23.4 us -> 19 us  [swapped(): return lax.ppermute(x, axis, [(i, i ^ flip) for i in range(count)])]
    pallas_call x2, Pallas kernels: 7.83 us -> 3.99 us  [chip_gradient(): pl.pallas_call(functools.partial(gradient_kernel, width, has_proj), out_s...]
    ppermute x37 -> x38, starting transfers between devices: 34.2 us -> 37.8 us  [swapped(): return lax.ppermute(x, axis, [(i, i ^ flip) for i in range(count)])]
    unnamed x72 -> x172, local copies, waits for them, and re-layouts: 7.05 us -> 9.51 us
    dot_general x0 -> x1, matrix products: none -> 1.99 us  [per_device(): jnp.einsum('pc,tc->pt', order, jnp.concatenate([x_mine, x_theirs]), prefe...]
    ppermute x3, waiting for transfers between devices: 8.92 us -> 6.93 us  [window_partner(): return lax.ppermute(x, 'seq', pairs)]
    another operation x4 -> x2, other arithmetic: 4.28 us -> 4.11 us
  transfers between devices with their start and end apart: 42 -> 43, of which waited for: 12 -> 11; matrix products, arithmetic and copies ran while one was open for 17% -> 19% of each run, Pallas kernels for 15% -> 12%
where the time goes in v4:
time: 157 us; the launch traced here: 156 us
  starting transfers between devices  50 us (32%)
  Pallas kernels  38.6 us (25%)
  waiting for transfers between devices  25.9 us (16%)
  other arithmetic  24 us (15%)
  local copies, waits for them, and re-layouts  13.6 us (9%)
  matrix products  1.99 us (1%)
  between operations  1.96 us (1%)
    ppermute x38, starting transfers between devices, swapped(): return lax.ppermute(x, axis, [(i, i ^ flip) for i in range(count)])  37.8 us
    ppermute x38, waiting for transfers between devices, swapped(): return lax.ppermute(x, axis, [(i, i ^ flip) for i in range(count)])  19 us
    pallas_call x2, Pallas kernels, attention_call(): pl.pallas_call(functools.partial(body, group, head_dim), grid=(1,), out_s...  16.5 us
    ppermute x3, starting transfers between devices, window_partner(): return lax.ppermute(x, 'seq', pairs)  10.9 us
    unnamed x172, local copies, waits for them, and re-layouts  9.51 us
    ppermute x3, waiting for transfers between devices, window_partner(): return lax.ppermute(x, 'seq', pairs)  6.93 us
    pallas_call x1, Pallas kernels, field_back(): pl.pallas_call(field_kernel, grid=(1,), out_shape=(jax.ShapeDtypeStruct(m...  6.91 us
    pallas_call x1, Pallas kernels, back_through(): pl.pallas_call(functools.partial(back_kernel, group), out_shape=(half, ja...  5.48 us
  transfers between devices with their start and end apart: 43, of which 11 were waited for; matrix products, arithmetic and copies ran while one was open for 19% of the time, Pallas kernels for 12%

profile of v4, /device:TPU:0, one launch (start us, length us, event | category | flops | bytes accessed | tf_op | source)
XLA Modules:
  0.0 156.0 jit_solution(13727911763047028529)
XLA Ops:
  0.7 2.6 %stage.1 = (bf16[192,3072]{1,0:T(8,128)(2,1)}, bf16[8,16,768]{2,1,0:T(8,128)(2,1)}, bf16[8,16,768]{2,1,0:T(8,128)(2,1)}) custom-call(s32[1]{0:T(128)} %bitcast.2.core, bf16[384,2304]{1,0:T(8,128)(2,1)} %w_qkv.5, bf16[384,768]{1,0:T(8,128)(2,1)} %refs_10_.1, bf16[1,2,8,16,768]{4,3,2,1,0:T(8,128)(2,1)} %tokens.1), custom_call_target="tpu_custom_call" | custom-call | flops 12500000 | bytes 400000 | tf_op jit(solution)/shard_map/stage/pallas_call | solution.py:236
  6.6 4.5 %collective-permute-start.1 = (bf16[128,768]{1,0:T(8,128)(2,1)S(1)}, bf16[128,768]{1,0:T(8,128)(2,1)S(1)}, u32[]{:S(2)}, u32[]{:S(2)}) collective-permute-start(bf16[128,768]{1,0:T(8,128)(2,1)S(1)} %bitcast.35), channel_id=1, source_target_pairs={{0,7},{1,2},{2,1},{3,4},{4,3},{5,6},{6,5},{7,0},{8,15},{9,10},{10,... | collective-permute-start | bytes 589832 | tf_op jit(solution)/shard_map/ppermute | solution.py:33
  13.2 3.1 %collective-permute-done.1.refs_1_ = bf16[128,768]{1,0:T(8,128)(2,1)S(1)} collective-permute-done((bf16[128,768]{1,0:T(8,128)(2,1)S(1)}, bf16[128,768]{1,0:T(8,128)(2,1)S(1)}, u32[]{:S(2)}, u32[]{:S(2)}) %collective-permute-start.1) | collective-permute-done | bytes 196640 | tf_op jit(solution)/shard_map/ppermute | solution.py:33
  18.5 3.7 %fusion.81 = (f32[2,8,16]{2,1,0:T(8,128)S(1)}, f32[2,8,16,768]{3,2,1,0:T(8,128)S(1)}) fusion(bf16[4,10,18,768]{3,2,1,0:T(8,128)(2,1)S(1)} %select_maximum_fusion.2.refs_6_, f32[768]{0:T(1024)S(1)} %get-tuple-element.90, f32[768]{0:T(1024)S(1)} %get-tuple-element.91, f32[768]{0:T(1024)S(1)} %get-tuple-element.66, f32[768]{0:T(1024)S(1)} %get-tuple-element.67, ...), kind=kLoop, calls=%fused_computation.192 | loop fusion | flops 16514816 | bytes 11094016 | tf_op jit(solution)/shard_map/reduce_sum | solution.py:643
  23.5 3.1 %collective-permute-start.3 = (bf16[128,768]{1,0:T(8,128)(2,1)S(1)}, bf16[128,768]{1,0:T(8,128)(2,1)S(1)}, u32[]{:S(2)}, u32[]{:S(2)}) collective-permute-start(bf16[128,768]{1,0:T(8,128)(2,1)S(1)} %bitcast.36), channel_id=1, source_target_pairs={{0,7},{1,2},{2,1},{3,4},{4,3},{5,6},{6,5},{7,0},{8,15},{9,10},{10,... | collective-permute-start | bytes 589832 | tf_op jit(solution)/shard_map/ppermute | solution.py:33
  28.1 3.8 %collective-permute-done.3.xg = bf16[128,768]{1,0:T(8,128)(2,1)S(1)} collective-permute-done((bf16[128,768]{1,0:T(8,128)(2,1)S(1)}, bf16[128,768]{1,0:T(8,128)(2,1)S(1)}, u32[]{:S(2)}, u32[]{:S(2)}) %collective-permute-start.3) | collective-permute-done | bytes 196640 | tf_op jit(solution)/shard_map/ppermute | solution.py:33
  36.9 2.8 %collective-permute-done.4.refs_0_ = bf16[192,3072]{1,0:T(8,128)(2,1)S(1)} collective-permute-done((bf16[192,3072]{1,0:T(8,128)(2,1)}, bf16[192,3072]{1,0:T(8,128)(2,1)S(1)}, u32[]{:S(2)}, u32[]{:S(2)}) %collective-permute-start.4) | collective-permute-done | bytes 1179680 | tf_op jit(solution)/shard_map/ppermute | solution.py:27
  46.9 11.3 %first_heads.1 = (bf16[1920,256]{1,0:T(8,128)(2,1)S(1)}, bf16[640,256]{1,0:T(8,128)(2,1)S(1)}, bf16[768,256]{1,0:T(8,128)(2,1)S(1)}, f32[20,256]{1,0:T(8,128)S(1)}) custom-call(s32[7]{0:T(128)S(1)} %stack.23.nums.refs_0_.at, f32[24]{0:T(128)S(1)} %copy-done.21, bf16[128,768]{1,0:T(8,128)(2,1)S(1)} %bitcast.29, bf16[128,768]{1,0:T(8,128)(2,1)S(1)} %copy-done.16, ...), custom_call_target="tpu_custom_call" | custom-call | flops 75000000 | bytes 800000 | tf_op jit(solution)/shard_map/first_heads/pallas_call | solution.py:201
  58.5 2.4 %collective-permute-done.7.refs_3_ = bf16[1920,256]{1,0:T(8,128)(2,1)S(1)} collective-permute-done((bf16[1920,256]{1,0:T(8,128)(2,1)S(1)}, bf16[1920,256]{1,0:T(8,128)(2,1)S(1)}, u32[]{:S(2)}, u32[]{:S(2)}) %collective-permute-start.7) | collective-permute-done | bytes 983072 | tf_op jit(solution)/shard_map/ppermute | solution.py:27
  64.0 2.5 %collective-permute-start.11 = (bf16[96,1920]{1,0:T(8,128)(2,1)S(1)}, bf16[96,1920]{1,0:T(8,128)(2,1)}, u32[]{:S(2)}, u32[]{:S(2)}) collective-permute-start(bf16[96,1920]{1,0:T(8,128)(2,1)S(1)} %get-tuple-element.50), channel_id=1, source_target_pairs={{0,24},{8,16},{16,8},{24,0},{1,25},{9,17},{17,9},{25,1},{2,26},{10... | collective-permute-start | bytes 1105928 | tf_op jit(solution)/shard_map/ppermute | solution.py:27
  67.5 5.2 %second_heads.1 = (bf16[768,256]{1,0:T(8,128)(2,1)}, bf16[384,256]{1,0:T(8,128)(2,1)}, bf16[128,256]{1,0:T(8,128)(2,1)}, f32[4,256]{1,0:T(4,128)}) custom-call(s32[7]{0:T(128)} %copy-done.19, f32[24]{0:T(128)} %scale.3, bf16[128,768]{1,0:T(8,128)(2,1)} %bitcast.28, bf16[128,768]{1,0:T(8,128)(2,1)} %copy-done.15, bf16[768,768]{1,0:T(8,128)(2,1)} %ordered.13.order, ...), custom_call_target="tpu_custom_call" | custom-call | flops 35000000 | bytes 800000 | tf_op jit(solution)/shard_map/second_heads/pallas_call | solution.py:201
  73.2 5.5 %back_through.1 = (bf16[128,768]{1,0:T(8,128)(2,1)}, bf16[256,768]{1,0:T(8,128)(2,1)}, bf16[128,768]{1,0:T(8,128)(2,1)}) custom-call(s32[7]{0:T(128)} %copy-done.19, bf16[1920,256]{1,0:T(8,128)(2,1)} %copy-done.6, bf16[768,256]{1,0:T(8,128)(2,1)} %get-tuple-element.43.second.refs_2_, bf16[384,2304]{1,0:T(8,128)(2,1)} %w_qkv.5, ...), custom_call_target="tpu_custom_call" | custom-call | flops 20000000 | bytes 800000 | tf_op jit(solution)/shard_map/back_through/pallas_call | solution.py:294
  78.7 3.2 %collective-permute-start.8 = (bf16[256,768]{1,0:T(8,128)(2,1)}, bf16[256,768]{1,0:T(8,128)(2,1)S(1)}, u32[]{:S(2)}, u32[]{:S(2)}) collective-permute-start(bf16[256,768]{1,0:T(8,128)(2,1)} %get-tuple-element.47), channel_id=1, source_target_pairs={{0,7},{1,2},{2,1},{3,4},{4,3},{5,6},{6,5},{7,0},{8,15},{9,10},{10,... | collective-permute-start | bytes 1179656 | tf_op jit(solution)/shard_map/ppermute | solution.py:33
  83.6 2.2 %fusion.80 = (bf16[96,1920]{1,0:T(8,128)(2,1)S(1)}, f32[96,1920]{1,0:T(8,128)}) fusion(bf16[96,1920]{1,0:T(8,128)(2,1)} %collective-permute-done.11, bf16[96,1920]{1,0:T(8,128)(2,1)} %collective-permute-done.10, f32[96,1920]{1,0:T(8,128)S(1)} %copy-done.10, bf16[96,1920]{1,0:T(8,128)(2,1)} %collective-permute-done.9), kind=kLoop, calls=%fused_computation.191 | loop fusion | flops 1290240 | bytes 2949120 | tf_op jit(solution)/shard_map/convert.5
  89.5 2.4 %collective-permute-start.16 = (bf16[96,1152]{1,0:T(8,128)(2,1)S(1)}, bf16[96,1152]{1,0:T(8,128)(2,1)S(1)}, u32[]{:S(2)}, u32[]{:S(2)}) collective-permute-start(bf16[96,1152]{1,0:T(8,128)(2,1)S(1)} %get-tuple-element.61), channel_id=1, source_target_pairs={{0,24},{8,16},{16,8},{24,0},{1,25},{9,17},{17,9},{25,1},{2,26},{10... | collective-permute-start | bytes 663560 | tf_op jit(solution)/shard_map/ppermute | solution.py:27
  93.0 3.6 %collective-permute-start.21 = (bf16[24,1920]{1,0:T(8,128)(2,1)S(1)}, bf16[24,1920]{1,0:T(8,128)(2,1)S(1)}, u32[]{:S(2)}, u32[]{:S(2)}) collective-permute-start(bf16[24,1920]{1,0:T(8,128)(2,1)S(1)} %get-tuple-element.109), channel_id=1, source_target_pairs={{0,6},{1,7},{2,4},{3,5},{4,2},{5,3},{6,0},{7,1},{8,14},{9,15},{10,... | collective-permute-start | bytes 276488 | tf_op jit(solution)/shard_map/ppermute | solution.py:27
  97.3 6.9 %field_back.1 = (f32[2,8,16,768]{3,2,1,0:T(8,128)}, bf16[8,16,768]{2,1,0:T(8,128)(2,1)}, bf16[8,16,768]{2,1,0:T(8,128)(2,1)}, bf16[2,8,16,768]{3,2,1,0:T(8,128)(2,1)}, f32[32,768]{1,0:T(8,128)}) custom-call(s32[7]{0:T(128)} %copy-done.19, bf16[128,768]{1,0:T(8,128)(2,1)} %get-tuple-element.45.refs_1_, bf16[128,768]{1,0:T(8,128)(2,1)} %get-tuple-element.46.refs_2_, ...), custom_call_target="tpu_custom_call" | custom-call | flops 5000000 | bytes 200000 | tf_op jit(solution)/shard_map/field_back/pallas_call | solution.py:582
  107.2 3.6 %collective-permute-start.30 = (bf16[24,1152]{1,0:T(8,128)(2,1)S(1)}, bf16[24,1152]{1,0:T(8,128)(2,1)S(1)}, u32[]{:S(2)}, u32[]{:S(2)}) collective-permute-start(bf16[24,1152]{1,0:T(8,128)(2,1)S(1)} %get-tuple-element.112), channel_id=1, source_target_pairs={{0,6},{1,7},{2,4},{3,5},{4,2},{5,3},{6,0},{7,1},{8,14},{9,15},{10,... | collective-permute-start | bytes 165896 | tf_op jit(solution)/shard_map/ppermute | solution.py:27
  115.2 3.6 %collective-permute-start.24 = (bf16[24,1920]{1,0:T(8,128)(2,1)S(1)}, bf16[24,1920]{1,0:T(8,128)(2,1)S(1)}, u32[]{:S(2)}, u32[]{:S(2)}) collective-permute-start(bf16[24,1920]{1,0:T(8,128)(2,1)S(1)} %fusion.56), channel_id=1, source_target_pairs={{0,6},{1,7},{2,4},{3,5},{4,2},{5,3},{6,0},{7,1},{8,14},{9,15},{10,... | collective-permute-start | bytes 276488 | tf_op jit(solution)/shard_map/ppermute | solution.py:27
  125.1 2.3 %collective-permute-start.33 = (bf16[24,1152]{1,0:T(8,128)(2,1)S(1)}, bf16[24,1152]{1,0:T(8,128)(2,1)S(1)}, u32[]{:S(2)}, u32[]{:S(2)}) collective-permute-start(bf16[24,1152]{1,0:T(8,128)(2,1)S(1)} %fusion.58), channel_id=1, source_target_pairs={{0,6},{1,7},{2,4},{3,5},{4,2},{5,3},{6,0},{7,1},{8,14},{9,15},{10,... | collective-permute-start | bytes 165896 | tf_op jit(solution)/shard_map/ppermute | solution.py:27
  129.9 3.8 %collective-permute-done.37 = f32[16,768]{1,0:T(8,128)S(1)} collective-permute-done((f32[16,768]{1,0:T(8,128)S(1)}, f32[16,768]{1,0:T(8,128)S(1)}, u32[]{:S(2)}, u32[]{:S(2)}) %collective-permute-start.37) | collective-permute-done | bytes 49184 | tf_op jit(solution)/shard_map/ppermute | solution.py:27
  142.7 3.7 %collective-permute-done.41 = f32[16,768]{1,0:T(8,128)S(1)} collective-permute-done((f32[16,768]{1,0:T(8,128)}, f32[16,768]{1,0:T(8,128)S(1)}, u32[]{:S(2)}, u32[]{:S(2)}) %collective-permute-start.41) | collective-permute-done | bytes 49184 | tf_op jit(solution)/shard_map/ppermute | solution.py:27
  146.8 3.4 %fusion.54 = bf16[1,2,8,16,768]{4,3,2,1,0:T(8,128)(2,1)} fusion(f32[2,8,16,768]{3,2,1,0:T(8,128)S(1)} %copy-done.25, f32[4,10,18,768]{3,2,1,0:T(8,128)S(1)} %select_maximum_fusion, f32[768]{0:T(1024)S(1)} %copy-done.44, f32[768]{0:T(1024)S(1)} %copy-done.46, f32[768]{0:T(1024)S(1)} %copy-done.50, f32[768]{0:T(1024)S(1)} %copy-done.52, ...), kind=kLoop, calls=%fused_computation.101 | loop fusion | flops 11206656 | bytes 20923392 | tf_op jit(solution)/shard_map/broadcast_in_dim | solution.py:773
  152.9 3.1 %assemble.1 = (f32[384,2304]{1,0:T(8,128)}, f32[384,768]{1,0:T(8,128)}) custom-call(s32[7]{0:T(128)S(1)} %copy-done.20, bf16[96,1920]{1,0:T(8,128)(2,1)S(1)} %pad_maximum_fusion.5.refs_0_, bf16[96,1920]{1,0:T(8,128)(2,1)S(1)} %collective-permute-done.25.refs_1_, bf16[96,1920]{1,0:T(8,128)(2,1)S(1)} %collective-permute-done.26.refs_2_, ...), custom_call_target="tpu_custom_call" | custom-call | flops 15000000 | bytes 700000 | tf_op jit(solution)/shard_map/assemble/pallas_call | solution.py:464
  (294 shorter events, 61.6 us)
Async XLA Ops:
  3.3 9.9 %collective-permute-start = (bf16[8,16,768]{2,1,0:T(8,128)(2,1)}, bf16[8,16,768]{2,1,0:T(8,128)(2,1)S(1)}, u32[]{:S(2)}, u32[]{:S(2)}) collective-permute-start(bf16[8,16,768]{2,1,0:T(8,128)(2,1)} %get-tuple-element.36), channel_id=1, source_target_pairs={{1,2},{3,4},{5,6},{2,1},{4,3},{6,5},{9,10},{11,12},{13,14},{10,9},... | collective-permute-start | bytes 589832 | tf_op jit(solution)/shard_map/ppermute | solution.py:39
  11.1 28.6 %collective-permute-start.4 = (bf16[192,3072]{1,0:T(8,128)(2,1)}, bf16[192,3072]{1,0:T(8,128)(2,1)S(1)}, u32[]{:S(2)}, u32[]{:S(2)}) collective-permute-start(bf16[192,3072]{1,0:T(8,128)(2,1)} %get-tuple-element.38), channel_id=1, source_target_pairs={{0,8},{8,0},{1,9},{9,1},{2,10},{10,2},{3,11},{11,3},{4,12},{12,4},... | collective-permute-start | bytes 3538952 | tf_op jit(solution)/shard_map/ppermute | solution.py:27
  64.0 14.8 %collective-permute-start.11 = (bf16[96,1920]{1,0:T(8,128)(2,1)S(1)}, bf16[96,1920]{1,0:T(8,128)(2,1)}, u32[]{:S(2)}, u32[]{:S(2)}) collective-permute-start(bf16[96,1920]{1,0:T(8,128)(2,1)S(1)} %get-tuple-element.50), channel_id=1, source_target_pairs={{0,24},{8,16},{16,8},{24,0},{1,25},{9,17},{17,9},{25,1},{2,26},{10... | collective-permute-start | bytes 1105928 | tf_op jit(solution)/shard_map/ppermute | solution.py:27
  66.4 17.2 %collective-permute-start.10 = (bf16[96,1920]{1,0:T(8,128)(2,1)S(1)}, bf16[96,1920]{1,0:T(8,128)(2,1)}, u32[]{:S(2)}, u32[]{:S(2)}) collective-permute-start(bf16[96,1920]{1,0:T(8,128)(2,1)S(1)} %get-tuple-element.49), channel_id=1, source_target_pairs={{0,16},{8,24},{16,0},{24,8},{1,17},{9,25},{17,1},{25,9},{2,18},{10... | collective-permute-start | bytes 1105928 | tf_op jit(solution)/shard_map/ppermute | solution.py:27
  67.0 16.6 %collective-permute-start.9 = (bf16[96,1920]{1,0:T(8,128)(2,1)S(1)}, bf16[96,1920]{1,0:T(8,128)(2,1)}, u32[]{:S(2)}, u32[]{:S(2)}) collective-permute-start(bf16[96,1920]{1,0:T(8,128)(2,1)S(1)} %get-tuple-element.48), channel_id=1, source_target_pairs={{0,8},{8,0},{16,24},{24,16},{1,9},{9,1},{17,25},{25,17},{2,10},{10... | collective-permute-start | bytes 1105928 | tf_op jit(solution)/shard_map/ppermute | solution.py:27
  67.5 18.4 %collective-permute-start.13 = (bf16[256,768]{1,0:T(8,128)(2,1)}, bf16[256,768]{1,0:T(8,128)(2,1)S(1)}, u32[]{:S(2)}, u32[]{:S(2)}) collective-permute-start(bf16[256,768]{1,0:T(8,128)(2,1)} %pad_maximum_fusion.4.cot.refs_5_), channel_id=1, source_target_pairs={{0,1},{1,0},{2,3},{3,2},{4,5},{5,4},{6,7},{7,6},{8,9},{9,8},{10,11... | collective-permute-start | bytes 1179656 | tf_op jit(solution)/shard_map/ppermute | solution.py:27
  72.7 13.2 %collective-permute-start.12 = (bf16[768,256]{1,0:T(8,128)(2,1)}, bf16[768,256]{1,0:T(8,128)(2,1)S(1)}, u32[]{:S(2)}, u32[]{:S(2)}) collective-permute-start(bf16[768,256]{1,0:T(8,128)(2,1)} %get-tuple-element.43.second.refs_2_), channel_id=1, source_target_pairs={{0,1},{1,0},{2,3},{3,2},{4,5},{5,4},{6,7},{7,6},{8,9},{9,8},{10,11... | collective-permute-start | bytes 1179656 | tf_op jit(solution)/shard_map/ppermute | solution.py:27
  78.7 17.9 %collective-permute-start.8 = (bf16[256,768]{1,0:T(8,128)(2,1)}, bf16[256,768]{1,0:T(8,128)(2,1)S(1)}, u32[]{:S(2)}, u32[]{:S(2)}) collective-permute-start(bf16[256,768]{1,0:T(8,128)(2,1)} %get-tuple-element.47), channel_id=1, source_target_pairs={{0,7},{1,2},{2,1},{3,4},{4,3},{5,6},{6,5},{7,0},{8,15},{9,10},{10,... | collective-permute-start | bytes 1179656 | tf_op jit(solution)/shard_map/ppermute | solution.py:33
  89.5 14.8 %collective-permute-start.16 = (bf16[96,1152]{1,0:T(8,128)(2,1)S(1)}, bf16[96,1152]{1,0:T(8,128)(2,1)S(1)}, u32[]{:S(2)}, u32[]{:S(2)}) collective-permute-start(bf16[96,1152]{1,0:T(8,128)(2,1)S(1)} %get-tuple-element.61), channel_id=1, source_target_pairs={{0,24},{8,16},{16,8},{24,0},{1,25},{9,17},{17,9},{25,1},{2,26},{10... | collective-permute-start | bytes 663560 | tf_op jit(solution)/shard_map/ppermute | solution.py:27
  91.8 12.6 %collective-permute-start.15 = (bf16[96,1152]{1,0:T(8,128)(2,1)S(1)}, bf16[96,1152]{1,0:T(8,128)(2,1)S(1)}, u32[]{:S(2)}, u32[]{:S(2)}) collective-permute-start(bf16[96,1152]{1,0:T(8,128)(2,1)S(1)} %get-tuple-element.60), channel_id=1, source_target_pairs={{0,16},{8,24},{16,0},{24,8},{1,17},{9,25},{17,1},{25,9},{2,18},{10... | collective-permute-start | bytes 663560 | tf_op jit(solution)/shard_map/ppermute | solution.py:27
  92.3 12.1 %collective-permute-start.14 = (bf16[96,1152]{1,0:T(8,128)(2,1)S(1)}, bf16[96,1152]{1,0:T(8,128)(2,1)S(1)}, u32[]{:S(2)}, u32[]{:S(2)}) collective-permute-start(bf16[96,1152]{1,0:T(8,128)(2,1)S(1)} %get-tuple-element.59), channel_id=1, source_target_pairs={{0,8},{8,0},{16,24},{24,16},{1,9},{9,1},{17,25},{25,17},{2,10},{10... | collective-permute-start | bytes 663560 | tf_op jit(solution)/shard_map/ppermute | solution.py:27
  93.0 19.6 %collective-permute-start.21 = (bf16[24,1920]{1,0:T(8,128)(2,1)S(1)}, bf16[24,1920]{1,0:T(8,128)(2,1)S(1)}, u32[]{:S(2)}, u32[]{:S(2)}) collective-permute-start(bf16[24,1920]{1,0:T(8,128)(2,1)S(1)} %get-tuple-element.109), channel_id=1, source_target_pairs={{0,6},{1,7},{2,4},{3,5},{4,2},{5,3},{6,0},{7,1},{8,14},{9,15},{10,... | collective-permute-start | bytes 276488 | tf_op jit(solution)/shard_map/ppermute | solution.py:27
  96.6 17.5 %collective-permute-start.20 = (bf16[24,1920]{1,0:T(8,128)(2,1)S(1)}, bf16[24,1920]{1,0:T(8,128)(2,1)S(1)}, u32[]{:S(2)}, u32[]{:S(2)}) collective-permute-start(bf16[24,1920]{1,0:T(8,128)(2,1)S(1)} %get-tuple-element.110), channel_id=1, source_target_pairs={{0,4},{1,5},{2,6},{3,7},{4,0},{5,1},{6,2},{7,3},{8,12},{9,13},{10,... | collective-permute-start | bytes 276488 | tf_op jit(solution)/shard_map/ppermute | solution.py:27
  107.2 11.7 %collective-permute-start.30 = (bf16[24,1152]{1,0:T(8,128)(2,1)S(1)}, bf16[24,1152]{1,0:T(8,128)(2,1)S(1)}, u32[]{:S(2)}, u32[]{:S(2)}) collective-permute-start(bf16[24,1152]{1,0:T(8,128)(2,1)S(1)} %get-tuple-element.112), channel_id=1, source_target_pairs={{0,6},{1,7},{2,4},{3,5},{4,2},{5,3},{6,0},{7,1},{8,14},{9,15},{10,... | collective-permute-start | bytes 165896 | tf_op jit(solution)/shard_map/ppermute | solution.py:27
  110.8 10.1 %collective-permute-start.29 = (bf16[24,1152]{1,0:T(8,128)(2,1)S(1)}, bf16[24,1152]{1,0:T(8,128)(2,1)S(1)}, u32[]{:S(2)}, u32[]{:S(2)}) collective-permute-start(bf16[24,1152]{1,0:T(8,128)(2,1)S(1)} %get-tuple-element.113), channel_id=1, source_target_pairs={{0,4},{1,5},{2,6},{3,7},{4,0},{5,1},{6,2},{7,3},{8,12},{9,13},{10,... | collective-permute-start | bytes 165896 | tf_op jit(solution)/shard_map/ppermute | solution.py:27
  115.2 12.3 %collective-permute-start.24 = (bf16[24,1920]{1,0:T(8,128)(2,1)S(1)}, bf16[24,1920]{1,0:T(8,128)(2,1)S(1)}, u32[]{:S(2)}, u32[]{:S(2)}) collective-permute-start(bf16[24,1920]{1,0:T(8,128)(2,1)S(1)} %fusion.56), channel_id=1, source_target_pairs={{0,6},{1,7},{2,4},{3,5},{4,2},{5,3},{6,0},{7,1},{8,14},{9,15},{10,... | collective-permute-start | bytes 276488 | tf_op jit(solution)/shard_map/ppermute | solution.py:27
  118.9 10.7 %collective-permute-start.22 = (bf16[24,1920]{1,0:T(8,128)(2,1)S(1)}, bf16[24,1920]{1,0:T(8,128)(2,1)S(1)}, u32[]{:S(2)}, u32[]{:S(2)}) collective-permute-start(bf16[24,1920]{1,0:T(8,128)(2,1)S(1)} %fusion.56), channel_id=1, source_target_pairs={{0,2},{1,3},{2,0},{3,1},{4,6},{5,7},{6,4},{7,5},{8,10},{9,11},{10,... | collective-permute-start | bytes 276488 | tf_op jit(solution)/shard_map/ppermute | solution.py:27
  120.9 19.3 %collective-permute-start.18 = (bf16[8,16,768]{2,1,0:T(8,128)(2,1)}, bf16[8,16,768]{2,1,0:T(8,128)(2,1)S(1)}, u32[]{:S(2)}, u32[]{:S(2)}) collective-permute-start(bf16[8,16,768]{2,1,0:T(8,128)(2,1)} %ordered.20), channel_id=1, source_target_pairs={{0,1},{1,0},{2,3},{3,2},{4,5},{5,4},{6,7},{7,6},{8,9},{9,8},{10,11... | collective-permute-start | bytes 589832 | tf_op jit(solution)/shard_map/ppermute | solution.py:27
  125.1 10.0 %collective-permute-start.33 = (bf16[24,1152]{1,0:T(8,128)(2,1)S(1)}, bf16[24,1152]{1,0:T(8,128)(2,1)S(1)}, u32[]{:S(2)}, u32[]{:S(2)}) collective-permute-start(bf16[24,1152]{1,0:T(8,128)(2,1)S(1)} %fusion.58), channel_id=1, source_target_pairs={{0,6},{1,7},{2,4},{3,5},{4,2},{5,3},{6,0},{7,1},{8,14},{9,15},{10,... | collective-permute-start | bytes 165896 | tf_op jit(solution)/shard_map/ppermute | solution.py:27
  127.5 10.6 %collective-permute-start.31 = (bf16[24,1152]{1,0:T(8,128)(2,1)S(1)}, bf16[24,1152]{1,0:T(8,128)(2,1)S(1)}, u32[]{:S(2)}, u32[]{:S(2)}) collective-permute-start(bf16[24,1152]{1,0:T(8,128)(2,1)S(1)} %fusion.58), channel_id=1, source_target_pairs={{0,2},{1,3},{2,0},{3,1},{4,6},{5,7},{6,4},{7,5},{8,10},{9,11},{10,... | collective-permute-start | bytes 165896 | tf_op jit(solution)/shard_map/ppermute | solution.py:27
  135.0 15.2 %collective-permute-start.25 = (bf16[96,1920]{1,0:T(8,128)(2,1)S(1)}, bf16[96,1920]{1,0:T(8,128)(2,1)S(1)}, u32[]{:S(2)}, u32[]{:S(2)}) collective-permute-start(bf16[96,1920]{1,0:T(8,128)(2,1)S(1)} %pad_maximum_fusion.5.refs_0_), channel_id=1, source_target_pairs={{0,16},{16,0},{1,17},{17,1},{2,18},{18,2},{3,19},{19,3},{4,20},{20... | collective-permute-start | bytes 1105928 | tf_op jit(solution)/shard_map/ppermute | solution.py:27
  136.5 15.6 %collective-permute-start.26 = (bf16[96,1920]{1,0:T(8,128)(2,1)S(1)}, bf16[96,1920]{1,0:T(8,128)(2,1)S(1)}, u32[]{:S(2)}, u32[]{:S(2)}) collective-permute-start(bf16[96,1920]{1,0:T(8,128)(2,1)S(1)} %pad_maximum_fusion.5.refs_0_), channel_id=1, source_target_pairs={{0,1},{1,0},{2,3},{3,2},{4,5},{5,4},{6,7},{7,6},{8,9},{9,8},{10,11... | collective-permute-start | bytes 1105928 | tf_op jit(solution)/shard_map/ppermute | solution.py:27
  139.2 12.3 %collective-permute-start.38 = (bf16[96,1152]{1,0:T(8,128)(2,1)S(1)}, bf16[96,1152]{1,0:T(8,128)(2,1)S(1)}, u32[]{:S(2)}, u32[]{:S(2)}) collective-permute-start(bf16[96,1152]{1,0:T(8,128)(2,1)S(1)} %pad_maximum_fusion.6.refs_4_), channel_id=1, source_target_pairs={{0,16},{16,0},{1,17},{17,1},{2,18},{18,2},{3,19},{19,3},{4,20},{20... | collective-permute-start | bytes 663560 | tf_op jit(solution)/shard_map/ppermute | solution.py:27
  140.2 11.8 %collective-permute-start.39 = (bf16[96,1152]{1,0:T(8,128)(2,1)S(1)}, bf16[96,1152]{1,0:T(8,128)(2,1)S(1)}, u32[]{:S(2)}, u32[]{:S(2)}) collective-permute-start(bf16[96,1152]{1,0:T(8,128)(2,1)S(1)} %pad_maximum_fusion.6.refs_4_), channel_id=1, source_target_pairs={{0,1},{1,0},{2,3},{3,2},{4,5},{5,4},{6,7},{7,6},{8,9},{9,8},{10,11... | collective-permute-start | bytes 663560 | tf_op jit(solution)/shard_map/ppermute | solution.py:27
  (105 other events, 878.7 us)

commit v5 on v4

--- a/solution.py
+++ b/solution.py
@@ -132,7 +132,7 @@
         back[rows(2 * group), :] = bv.astype(BF)
 
     count = group // head_dim
-    unrolled = math.gcd(count, 10) if count > 8 else count
+    unrolled = next(u for u in (10, 8, 4, 2, 1) if count % u == 0)
 
     def body(i, carry):
         for u in range(unrolled):
@@ -168,13 +168,17 @@
 
 
 def second_kernel(group, head_dim, nums, scale, xm, xg, order, ba, att_first, *refs):
-    weights, (send, att_rows, att, gs, qkv) = refs[:9], refs[9:]
+    send_first, w_qkv, got, other, send, att_rows, mine, window, att_mine, gs, qkv, att = refs
     channels = xm.shape[1]
     half = channels // 2
     low = channels - group
     x = jnp.concatenate([xm[...], xg[...]], axis=0)
-    mine, got, other = [lambda part, refs=weights[i : i + 3]: refs[part][...] for i in (0, 3, 6)]
-    project(nums, x, mine, got, other, group, qkv)
+
+    def columns(ref, base):
+        return lambda part: ref[:, base + part * channels : base + part * channels + group]
+
+    far = (columns(got, channels + low), columns(other, channels + low))
+    project(nums, x, columns(w_qkv, low), *far, group, qkv)
     allowed = allowed_pairs(nums, x.shape[0])
     attend(head_dim, allowed, scale, low // head_dim, group, qkv, ba, low, att, send, gs)
 
@@ -185,27 +189,22 @@
 
     att_rows[...] = ordered(slice(0, half))
     send[3 * group :, :] = ordered(slice(half, channels))
-
-
-def attention_call(body, name, group, head_dim, head_count, outs, operands, columns=()):
+    back_through(low, nums, send_first, send, w_qkv, got, other, att_first, att, mine, window, att_mine)
+
+
+def attention_call(body, name, group, head_dim, outs, operands, megabytes, scratch=()):
     n = 2 * operands[2].shape[0]
-    channels = operands[2].shape[1]
     vmem = pl.BlockSpec(memory_space=pltpu.VMEM)
     smem = pl.BlockSpec(memory_space=pltpu.SMEM)
-    tail = operands[len(operands) - len(columns) :]
-    blocks = [
-        pl.BlockSpec((x.shape[0], wide), lambda i, at=at: (0, at)) for x, (wide, at) in zip(tail, columns)
-    ]
-    shapes = tuple(jax.ShapeDtypeStruct((rows, n), BF) for rows in outs)
+    shapes = tuple(jax.ShapeDtypeStruct(shape, BF) for shape in outs)
     shapes = shapes + (jax.ShapeDtypeStruct((group // head_dim, n), F32),)
     return pl.pallas_call(
         functools.partial(body, group, head_dim),
-        grid=(1,),
         out_shape=shapes,
-        in_specs=[smem, smem] + [vmem] * (len(operands) - 2 - len(columns)) + blocks,
+        in_specs=[smem, smem] + [vmem] * (len(operands) - 2),
         out_specs=(vmem,) * len(shapes),
-        scratch_shapes=[pltpu.VMEM((3 * group, n), BF)],
-        compiler_params=pltpu.CompilerParams(vmem_limit_bytes=(60 if columns else 24) * 1024 * 1024),
+        scratch_shapes=[pltpu.VMEM((rows, n), BF) for rows in (3 * group, *scratch)],
+        compiler_params=pltpu.CompilerParams(vmem_limit_bytes=megabytes * 1024 * 1024),
         cost_estimate=busy(5 + 0.5 * (group // head_dim), 8),
         name=name,
     )(*operands)
@@ -244,38 +243,35 @@
     )(core[None].astype(jnp.int32), w_qkv, w_proj, tokens)
 
 
-def back_kernel(group, nums, first, second, w_qkv, got, other, att1, att2, *outs):
-    mine, send, att_mine = outs
+def back_through(group, nums, first, second, w_qkv, got, other, att1, att2, mine, send, att_mine):
     n = first.shape[1]
     half = n // 2
     channels = att_mine.shape[1]
     rest = channels - group
     low_rows, low_core = nums[3] == 0, nums[4] == 0
-    first_t = first[: 3 * group, :].astype(F32).T.astype(BF)
-    second_t = second[: 3 * rest, :].astype(F32).T.astype(BF)
-
-    def through(pieces):
+
+    def through(weight, base):
         total = None
-        for left, right in pieces:
-            term = lax.dot_general(left, right, OVER_LANES, preferred_element_type=F32)
-            total = term if total is None else total + term
-        return total
-
-    def pieces(weight, base):
         for part in range(3):
             low = base + part * channels
-            yield first_t[:, part * group : (part + 1) * group], weight[:, low : low + group]
-            yield second_t[:, part * rest : (part + 1) * rest], weight[:, low + group : low + channels]
-
-    from_mine = through(pieces(w_qkv, 0))
-    from_got = through(pieces(got, channels))
-    from_other = through(pieces(other, channels))
+            for columns, rows, ref in (
+                (slice(low, low + group), slice(part * group, (part + 1) * group), first),
+                (slice(low + group, low + channels), slice(part * rest, (part + 1) * rest), second),
+            ):
+                term = jnp.dot(weight[:, columns], ref[rows, :], preferred_element_type=F32)
+                total = term if total is None else total + term
+        return total
+
+    from_mine = through(w_qkv, 0)
+    from_got = through(got, channels)
+    from_other = through(other, channels)
     from_peer = jnp.concatenate(
-        [jnp.where(low_core, from_got, from_other), jnp.where(low_core, from_other, from_got)], axis=1
+        [jnp.where(low_core, from_got, from_other), jnp.where(low_core, from_other, from_got)]
     )
     shifted = jnp.concatenate(
-        [jnp.where(low_rows, from_mine, from_peer), jnp.where(low_rows, from_peer, from_mine)], axis=1
-    ).astype(BF)
+        [jnp.where(low_rows, from_mine, from_peer), jnp.where(low_rows, from_peer, from_mine)]
+    )
+    shifted = shifted.T.astype(BF)
     mine[...] = shifted[:half]
     send[:half, :] = shifted[half:]
     for low, ref in ((0, att1), (group, att2)):
@@ -283,23 +279,6 @@
         turned = ref[...].astype(F32).T.astype(BF)
         att_mine[:, wide] = turned[:half]
         send[half:, wide] = turned[half:]
-
-
-def back_through(group, operands):
-    n = operands[1].shape[1]
-    channels = operands[6].shape[0] + operands[7].shape[0]
-    vmem = pl.BlockSpec(memory_space=pltpu.VMEM)
-    smem = pl.BlockSpec(memory_space=pltpu.SMEM)
-    half = jax.ShapeDtypeStruct((n // 2, channels), BF)
-    return pl.pallas_call(
-        functools.partial(back_kernel, group),
-        out_shape=(half, jax.ShapeDtypeStruct((n, channels), BF), half),
-        in_specs=[smem] + [vmem] * (len(operands) - 1),
-        out_specs=(vmem,) * 3,
-        compiler_params=pltpu.CompilerParams(vmem_limit_bytes=60 * 1024 * 1024),
-        cost_estimate=busy(4, 8),
-        name="back_through",
-    )(*operands)
 
 
 def after(x, *others):
@@ -505,7 +484,60 @@
     )
 
 
-GROUP_HEADS = 20
+GROUP_HEADS = 16
+
+
+def shifted_fields(before, slab, behind, lanes):
+    planes = jnp.concatenate([before[:, :, lanes][None], slab[0, :, :, :, lanes], behind[:, :, lanes][None]])
+    planes = planes.astype(F32)
+    row = jnp.zeros_like(planes[:, :1])
+    planes = jnp.concatenate([row, planes, row], axis=1)
+    column = jnp.zeros_like(planes[:, :, :1])
+    width = planes.shape[2]
+    yield jnp.concatenate([column, planes[:, :, : width - 1]], axis=2)
+    yield planes
+    yield jnp.concatenate([planes[:, :, 1:], column], axis=2)
+
+
+def field_forward_kernel(nums, slab, before, behind, weight, gain, mixed, mine, theirs):
+    depth, height, width, channels = mixed.shape
+    tile = 128
+    for start in range(0, channels, tile):
+        lanes = slice(start, start + tile)
+        total = slab[0, :, :, :, lanes].astype(F32)
+        for e, shifted in enumerate(shifted_fields(before, slab, behind, lanes)):
+            for a in range(3):
+                for b in range(3):
+                    t = 9 * a + 3 * b + e
+                    factor = weight[t : t + 1, lanes].reshape(1, 1, 1, tile)
+                    total = total + factor * shifted[a : a + depth, b : b + height]
+        mixed[:, :, :, lanes] = total
+    rows = depth * height
+    field = mixed[...].reshape(rows, width, channels)
+    field = field - jnp.mean(field, axis=-1, keepdims=True)
+    std = lax.rsqrt(jnp.mean(field * field, axis=-1, keepdims=True) + 1e-05)
+    field = field * std * gain[...].reshape(1, 1, channels)
+    low, high = field[:, :HALF], field[:, HALF:]
+    column = lax.broadcasted_iota(jnp.int32, low.shape, 1)
+    straight = (column >= nums[1]).astype(jnp.int32) == nums[4]
+    mine[...] = jnp.where(straight, low, high).reshape(rows * HALF, channels).astype(BF)
+    theirs[...] = jnp.where(straight, high, low).reshape(rows * HALF, channels).astype(BF)
+
+
+def field_forward(operands):
+    shape = operands[1].shape[1:]
+    vmem = pl.BlockSpec(memory_space=pltpu.VMEM)
+    smem = pl.BlockSpec(memory_space=pltpu.SMEM)
+    half = jax.ShapeDtypeStruct((shape[0] * shape[1] * HALF, shape[3]), BF)
+    return pl.pallas_call(
+        field_forward_kernel,
+        out_shape=(jax.ShapeDtypeStruct(shape, F32), half, half),
+        in_specs=[smem] + [vmem] * (len(operands) - 1),
+        out_specs=(vmem,) * 3,
+        compiler_params=pltpu.CompilerParams(vmem_limit_bytes=24 * 1024 * 1024),
+        cost_estimate=busy(1, 2),
+        name="field_forward",
+    )(*operands)
 
 
 def into_field(nums, mine, theirs):
@@ -518,9 +550,9 @@
 
 
 def field_kernel(*refs):
-    nums, back, att, got, mixed, cot, padded, gain, scale1, scale2 = refs[:10]
-    w_mine, w_got, w_other = refs[10:13]
-    bm, inner, outer, out, small = refs[13:]
+    nums, back, att, got, mixed, cot, slab, before, behind, gain, scale1, scale2 = refs[:12]
+    w_mine, w_got, w_other = refs[12:15]
+    bm, inner, outer, out, small = refs[15:]
     depth, height, width, channels = mixed.shape
     half = back.shape[0]
     rows = depth * height
@@ -555,8 +587,7 @@
     for start in range(0, channels, tile):
         lanes = slice(start, start + tile)
         mixed_back = bm[:, :, :, lanes]
-        for e in range(3):
-            shifted = padded[:, :, e : e + width, lanes].astype(F32)
+        for e, shifted in enumerate(shifted_fields(before, slab, behind, lanes)):
             for a in range(3):
                 for b in range(3):
                     product = mixed_back * shifted[a : a + depth, b : b + height]
@@ -633,18 +664,17 @@
     weights_got = swapped(weights_part, "dp", 1)
     cot_mine, cot_theirs = split_columns(cot)
     cot_got = window_partner(cot_theirs)
-    padded_tokens = jnp.pad(with_halo(slab, inner, after(outer, cot_got), core), spatial)
+    outer = after(outer, cot_got)
+    before, behind = jnp.where(core == 0, outer, inner), jnp.where(core == 0, inner, outer)
     cot_window = jnp.concatenate([cot_mine, cot_got])
     order = after(place.row_order(), cot_got)
 
-    mixed_field = slab.astype(F32) + tap_sum(
-        padded_tokens, conv_weight, depth, height, width, False
-    )
-    centred = mixed_field - jnp.mean(mixed_field, axis=-1, keepdims=True)
-    inverse_std = lax.rsqrt(jnp.mean(centred * centred, axis=-1, keepdims=True) + 1e-05)
-    unit_field = centred * inverse_std
-    normed = (unit_field * norm_gain).astype(BF)
-    x_mine, x_theirs = split_columns(normed)
+    nums = jnp.stack(
+        [rows_shift, cols_shift, 1 - core, dp, core, place.rep, place.digit]
+    ).astype(jnp.int32)
+    mixed_field, x_mine, x_theirs = field_forward(
+        (nums, tokens, before, behind, conv_weight, norm_gain)
+    )
     x_theirs = window_partner(x_theirs)
     x_rows = jnp.einsum(
         "pc,tc->pt",
@@ -657,30 +687,32 @@
     weights_got = after(weights_got, x_other)
     weights_other = swapped(weights_got, "seq", 1)
     cot_other = swapped(cot_window, "seq", 1)
-    nums = jnp.stack(
-        [rows_shift, cols_shift, 1 - core, dp, core, place.rep, place.digit]
-    ).astype(jnp.int32)
     half_rows = channels // 2
+    n = 2 * half
     send_first, att_first, back_attended, scale_first = attention_call(
         first_kernel,
         "first_heads",
         group,
         head_dim,
-        head_count,
-        (3 * group, group, channels),
+        ((3 * group, n), (group, n), (channels, n)),
         (nums, head_scale, x_mine, x_theirs, cot_window, w_qkv, w_proj, weights_got, weights_other),
+        24,
     )
     got_first = swapped(send_first, "seq", 1)
     own, *sends = chip_gradient(group, (x_rows, x_other, send_first, got_first))
     rest = channels - group
-    parts = [part * channels + group for part in range(3)]
-    send_second, att_rows, att_second, scale_second = attention_call(
+    send_second, att_rows, back_mine, window_send, att_mine, scale_second = attention_call(
         second_kernel,
         "second_heads",
         rest,
         head_dim,
-        head_count,
-        (3 * rest + half_rows, half_rows, rest),
+        (
+            (3 * rest + half_rows, n),
+            (half_rows, n),
+            (half, channels),
+            (n, channels),
+            (half, channels),
+        ),
         (
             nums,
             head_scale,
@@ -689,29 +721,16 @@
             order,
             after(back_attended, own),
             att_first,
-            *[w_qkv] * 3,
-            *[weights_got] * 3,
-            *[weights_other] * 3,
-        ),
-        [(rest, base // rest) for base in parts]
-        + [(rest, (base + channels) // rest) for base in parts] * 2,
-    )
-    first_own, first_sends = own, sends
-
-    got_second = swapped(send_second, "seq", 1)
-    back_mine, window_send, att_mine = back_through(
-        group,
-        (
-            nums,
             send_first,
-            send_second,
             w_qkv,
             weights_got,
             weights_other,
-            att_first,
-            att_second,
         ),
-    )
+        60,
+        (rest,),
+    )
+    first_own, first_sends = own, sends
+    got_second = swapped(send_second, "seq", 1)
     first_total = sum_square(first_own, first_sends, place)
     own, *sends = chip_gradient(
         rest,
@@ -734,7 +753,9 @@
             window_got,
             mixed_field,
             cot,
-            padded_tokens,
+            tokens,
+            before,
+            behind,
             norm_gain,
             scale_first,
             scale_second,

time: 157 us -> 154 us (0.981)
  waiting for transfers between devices: 25.9 us -> 31.2 us
  other arithmetic: 24 us -> 18.9 us
    ppermute x38, waiting for transfers between devices: 19 us -> 28.2 us  [swapped(): return lax.ppermute(x, axis, [(i, i ^ flip) for i in range(count)])]
    reduce_sum x2 -> x0, other arithmetic: 3.92 us -> none  [the longest x1 3.7 us: per_device(): centred = mixed_field - jnp.mean(mixed_field, axis=-1, keepdims=True)]
    ppermute x3, waiting for transfers between devices: 6.93 us -> 3.03 us  [window_partner(): return lax.ppermute(x, 'seq', pairs)]
    unnamed x172 -> x76, local copies, waits for them, and re-layouts: 9.51 us -> 8.13 us
  transfers between devices with their start and end apart: 43 -> 43, of which waited for: 11 -> 12; matrix products, arithmetic and copies ran while one was open for 19% -> 14% of each run, Pallas kernels for 12% -> 15%
where the time goes in v5:
time: 154 us; the launch traced here: 153 us
  starting transfers between devices  49.8 us (32%)
  Pallas kernels  37.6 us (24%)
  waiting for transfers between devices  31.2 us (20%)
  other arithmetic  18.9 us (12%)
  local copies, waits for them, and re-layouts  12.5 us (8%)
  matrix products  1.99 us (1%)
    ppermute x38, starting transfers between devices, swapped(): return lax.ppermute(x, axis, [(i, i ^ flip) for i in range(count)])  37.2 us
    ppermute x38, waiting for transfers between devices, swapped(): return lax.ppermute(x, axis, [(i, i ^ flip) for i in range(count)])  28.2 us
    pallas_call x2, Pallas kernels, attention_call(): pl.pallas_call(functools.partial(body, group, head_dim), out_shape=shapes...  18.8 us
    ppermute x3, starting transfers between devices, window_partner(): return lax.ppermute(x, 'seq', pairs)  11 us
    unnamed x76, local copies, waits for them, and re-layouts  8.13 us
    pallas_call x1, Pallas kernels, field_back(): pl.pallas_call(field_kernel, grid=(1,), out_shape=(jax.ShapeDtypeStruct(m...  5.91 us
    pallas_call x2, Pallas kernels, chip_gradient(): pl.pallas_call(functools.partial(gradient_kernel, width, has_proj), out_s...  4.54 us
    another operation x2, other arithmetic  4.1 us
  transfers between devices with their start and end apart: 43, of which 12 were waited for; matrix products, arithmetic and copies ran while one was open for 14% of the time, Pallas kernels for 15%

profile of v5, /device:TPU:0, one launch (start us, length us, event | category | flops | bytes accessed | tf_op | source)
XLA Modules:
  0.0 153.3 jit_solution(5309851045886347328)
XLA Ops:
  4.4 4.5 %collective-permute-start.1 = (bf16[128,768]{1,0:T(8,128)(2,1)S(1)}, bf16[128,768]{1,0:T(8,128)(2,1)S(1)}, u32[]{:S(2)}, u32[]{:S(2)}) collective-permute-start(bf16[128,768]{1,0:T(8,128)(2,1)S(1)} %bitcast.23), channel_id=1, source_target_pairs={{0,7},{1,2},{2,1},{3,4},{4,3},{5,6},{6,5},{7,0},{8,15},{9,10},{10,... | collective-permute-start | bytes 589832 | tf_op jit(solution)/shard_map/ppermute | solution.py:33
  8.9 2.5 %stage.1 = (bf16[192,3072]{1,0:T(8,128)(2,1)}, bf16[8,16,768]{2,1,0:T(8,128)(2,1)}, bf16[8,16,768]{2,1,0:T(8,128)(2,1)}) custom-call(s32[1]{0:T(128)} %bitcast.2.core, bf16[384,2304]{1,0:T(8,128)(2,1)} %refs_1_.1, bf16[384,768]{1,0:T(8,128)(2,1)} %refs_12_.1, bf16[1,2,8,16,768]{4,3,2,1,0:T(8,128)(2,1)} %refs_6_.1), custom_call_target="tpu_custom_call" | custom-call | flops 12500000 | bytes 400000 | tf_op jit(solution)/shard_map/stage/pallas_call | solution.py:235
  16.3 2.8 %field_forward.1 = (f32[2,8,16,768]{3,2,1,0:T(8,128)S(1)}, bf16[128,768]{1,0:T(8,128)(2,1)S(1)}, bf16[128,768]{1,0:T(8,128)(2,1)S(1)}) custom-call(s32[7]{0:T(128)S(1)} %stack.23.nums.refs_0_.at, bf16[1,2,8,16,768]{4,3,2,1,0:T(8,128)(2,1)S(1)} %copy-done.8, bf16[8,16,768]{2,1,0:T(8,128)(2,1)S(1)} %get-tuple-element.107.before.refs_7_, ...), custom_call_target="tpu_custom_call" | custom-call | flops 5000000 | bytes 200000 | tf_op jit(solution)/shard_map/field_forward/pallas_call | solution.py:532
  20.0 3.3 %collective-permute-start.3 = (bf16[128,768]{1,0:T(8,128)(2,1)S(1)}, bf16[128,768]{1,0:T(8,128)(2,1)}, u32[]{:S(2)}, u32[]{:S(2)}) collective-permute-start(bf16[128,768]{1,0:T(8,128)(2,1)S(1)} %get-tuple-element.41), channel_id=1, source_target_pairs={{0,7},{1,2},{2,1},{3,4},{4,3},{5,6},{6,5},{7,0},{8,15},{9,10},{10,... | collective-permute-start | bytes 589832 | tf_op jit(solution)/shard_map/ppermute | solution.py:33
  24.6 3.0 %collective-permute-done.3.xg = bf16[128,768]{1,0:T(8,128)(2,1)} collective-permute-done((bf16[128,768]{1,0:T(8,128)(2,1)S(1)}, bf16[128,768]{1,0:T(8,128)(2,1)}, u32[]{:S(2)}, u32[]{:S(2)}) %collective-permute-start.3) | collective-permute-done | bytes 196640 | tf_op jit(solution)/shard_map/ppermute | solution.py:33
  27.6 2.0 %convolution_convert_fusion = bf16[768,256]{1,0:T(8,128)(2,1)S(1)} fusion(bf16[768,768]{1,0:T(8,128)(2,1)} %ordered.13.order, bf16[128,768]{1,0:T(8,128)(2,1)} %collective-permute-done.3.xg, bf16[128,768]{1,0:T(8,128)(2,1)} %copy-done.18), kind=kOutput, calls=%fused_computation.11 | convolution fusion | flops 302972928 | bytes 1966080 | tf_op jit(solution)/shard_map/pc,tc->pt/dot_general | solution.py:679
  33.0 7.8 %collective-permute-done.4.refs_0_ = bf16[192,3072]{1,0:T(8,128)(2,1)S(1)} collective-permute-done((bf16[192,3072]{1,0:T(8,128)(2,1)}, bf16[192,3072]{1,0:T(8,128)(2,1)S(1)}, u32[]{:S(2)}, u32[]{:S(2)}) %collective-permute-start.4) | collective-permute-done | bytes 1179680 | tf_op jit(solution)/shard_map/ppermute | solution.py:27
  42.9 2.0 %collective-permute-done.6.other.refs_3_.refs_14_ = bf16[192,3072]{1,0:T(8,128)(2,1)S(1)} collective-permute-done((bf16[192,3072]{1,0:T(8,128)(2,1)}, bf16[192,3072]{1,0:T(8,128)(2,1)S(1)}, u32[]{:S(2)}, u32[]{:S(2)}) %collective-permute-start.6) | collective-permute-done | bytes 1179680 | tf_op jit(solution)/shard_map/ppermute | solution.py:27
  47.1 9.4 %first_heads.1 = (bf16[1536,256]{1,0:T(8,128)(2,1)S(1)}, bf16[512,256]{1,0:T(8,128)(2,1)S(1)}, bf16[768,256]{1,0:T(8,128)(2,1)S(1)}, f32[16,256]{1,0:T(8,128)S(1)}) custom-call(s32[7]{0:T(128)S(1)} %stack.23.nums.refs_0_.at, f32[24]{0:T(128)S(1)} %copy-done.29, bf16[128,768]{1,0:T(8,128)(2,1)S(1)} %copy-done.19, bf16[128,768]{1,0:T(8,128)(2,1)} %collective-permute-done.3.xg, ...), custom_call_target="tpu_custom_call" | custom-call | flops 65000000 | bytes 800000 | tf_op jit(solution)/shard_map/first_heads/pallas_call | solution.py:201
  56.7 2.2 %collective-permute-done.7.refs_3_ = bf16[1536,256]{1,0:T(8,128)(2,1)S(1)} collective-permute-done((bf16[1536,256]{1,0:T(8,128)(2,1)S(1)}, bf16[1536,256]{1,0:T(8,128)(2,1)S(1)}, u32[]{:S(2)}, u32[]{:S(2)}) %collective-permute-start.7) | collective-permute-done | bytes 786464 | tf_op jit(solution)/shard_map/ppermute | solution.py:27
  58.9 2.6 %chip_gradient.2 = (f32[96,1536]{1,0:T(8,128)S(1)}, bf16[96,1536]{1,0:T(8,128)(2,1)S(1)}, bf16[96,1536]{1,0:T(8,128)(2,1)}, bf16[96,1536]{1,0:T(8,128)(2,1)S(1)}) custom-call(bf16[384,256]{1,0:T(8,128)(2,1)S(1)} %copy-done.9, bf16[384,256]{1,0:T(8,128)(2,1)} %collective-permute-done.5.refs_1_, bf16[1536,256]{1,0:T(8,128)(2,1)S(1)} %get-tuple-element.44.refs_2_.refs_0_, ...), custom_call_target="tpu_custom_call" | custom-call | flops 7500000 | bytes 350000 | tf_op jit(solution)/shard_map/chip_gradient/pallas_call | solution.py:377
  66.0 9.4 %second_heads.1 = (bf16[1152,256]{1,0:T(8,128)(2,1)}, bf16[384,256]{1,0:T(8,128)(2,1)}, bf16[128,768]{1,0:T(8,128)(2,1)}, bf16[256,768]{1,0:T(8,128)(2,1)}, bf16[128,768]{1,0:T(8,128)(2,1)}, /*index=5*/f32[8,256]{1,0:T(8,128)}) custom-call(s32[7]{0:T(128)} %copy-done.25, f32[24]{0:T(128)} %scale.3, bf16[128,768]{1,0:T(8,128)(2,1)} %copy-done.18, ...), custom_call_target="tpu_custom_call" | custom-call | flops 45000000 | bytes 800000 | tf_op jit(solution)/shard_map/second_heads/pallas_call | solution.py:201
  77.2 3.2 %collective-permute-start.8 = (bf16[256,768]{1,0:T(8,128)(2,1)}, bf16[256,768]{1,0:T(8,128)(2,1)}, u32[]{:S(2)}, u32[]{:S(2)}) collective-permute-start(bf16[256,768]{1,0:T(8,128)(2,1)} %get-tuple-element.49), channel_id=1, source_target_pairs={{0,7},{1,2},{2,1},{3,4},{4,3},{5,6},{6,5},{7,0},{8,15},{9,10},{10,... | collective-permute-start | bytes 1179656 | tf_op jit(solution)/shard_map/ppermute | solution.py:33
  80.4 2.1 %fusion.65 = (bf16[96,1536]{1,0:T(8,128)(2,1)S(1)}, f32[96,1536]{1,0:T(8,128)}) fusion(bf16[96,1536]{1,0:T(8,128)(2,1)} %collective-permute-done.11, bf16[96,1536]{1,0:T(8,128)(2,1)} %collective-permute-done.10, f32[96,1536]{1,0:T(8,128)S(1)} %copy-done.13, bf16[96,1536]{1,0:T(8,128)(2,1)} %collective-permute-done.9), kind=kLoop, calls=%fused_computation.164 | loop fusion | flops 1032192 | bytes 2359296 | tf_op jit(solution)/shard_map/convert.5
  83.5 1.9 %chip_gradient.3 = (f32[96,1536]{1,0:T(8,128)S(1)}, bf16[96,1536]{1,0:T(8,128)(2,1)S(1)}, bf16[96,1536]{1,0:T(8,128)(2,1)S(1)}, bf16[96,1536]{1,0:T(8,128)(2,1)S(1)}) custom-call(bf16[384,256]{1,0:T(8,128)(2,1)S(1)} %copy-done.10, bf16[384,256]{1,0:T(8,128)(2,1)} %collective-permute-done.5.refs_1_, bf16[1152,256]{1,0:T(8,128)(2,1)S(1)} %copy-done.20, ...), custom_call_target="tpu_custom_call" | custom-call | flops 7500000 | bytes 350000 | tf_op jit(solution)/shard_map/chip_gradient/pallas_call | solution.py:377
  91.1 2.6 %collective-permute-start.20 = (bf16[24,1536]{1,0:T(8,128)(2,1)S(1)}, bf16[24,1536]{1,0:T(8,128)(2,1)S(1)}, u32[]{:S(2)}, u32[]{:S(2)}) collective-permute-start(bf16[24,1536]{1,0:T(8,128)(2,1)S(1)} %get-tuple-element.113), channel_id=1, source_target_pairs={{0,4},{1,5},{2,6},{3,7},{4,0},{5,1},{6,2},{7,3},{8,12},{9,13},{10,... | collective-permute-start | bytes 221192 | tf_op jit(solution)/shard_map/ppermute | solution.py:27
  93.7 5.9 %field_back.1 = (f32[2,8,16,768]{3,2,1,0:T(8,128)}, bf16[8,16,768]{2,1,0:T(8,128)(2,1)}, bf16[8,16,768]{2,1,0:T(8,128)(2,1)}, bf16[2,8,16,768]{3,2,1,0:T(8,128)(2,1)}, f32[32,768]{1,0:T(8,128)}) custom-call(s32[7]{0:T(128)} %copy-done.25, bf16[128,768]{1,0:T(8,128)(2,1)} %get-tuple-element.47.refs_1_, bf16[128,768]{1,0:T(8,128)(2,1)} %get-tuple-element.48.refs_2_, ...), custom_call_target="tpu_custom_call" | custom-call | flops 5000000 | bytes 200000 | tf_op jit(solution)/shard_map/field_back/pallas_call | solution.py:613
  101.0 2.0 %fusion.64 = (bf16[96,1536]{1,0:T(8,128)(2,1)S(1)}, f32[96,1536]{1,0:T(8,128)}) fusion(bf16[96,1536]{1,0:T(8,128)(2,1)S(1)} %collective-permute-done.16, bf16[96,1536]{1,0:T(8,128)(2,1)S(1)} %collective-permute-done.15, f32[96,1536]{1,0:T(8,128)} %ordered.18, bf16[96,1536]{1,0:T(8,128)(2,1)S(1)} %collective-permute-done.14), kind=kLoop, calls=%fused_computation.163 | loop fusion | flops 1032192 | bytes 2359296 | tf_op jit(solution)/shard_map/convert.2
  105.5 2.0 %collective-permute-start.29 = (bf16[24,1536]{1,0:T(8,128)(2,1)S(1)}, bf16[24,1536]{1,0:T(8,128)(2,1)S(1)}, u32[]{:S(2)}, u32[]{:S(2)}) collective-permute-start(bf16[24,1536]{1,0:T(8,128)(2,1)S(1)} %get-tuple-element.110), channel_id=1, source_target_pairs={{0,4},{1,5},{2,6},{3,7},{4,0},{5,1},{6,2},{7,3},{8,12},{9,13},{10,... | collective-permute-start | bytes 221192 | tf_op jit(solution)/shard_map/ppermute | solution.py:27
  121.7 4.0 %collective-permute-start.33 = (bf16[24,1536]{1,0:T(8,128)(2,1)S(1)}, bf16[24,1536]{1,0:T(8,128)(2,1)S(1)}, u32[]{:S(2)}, u32[]{:S(2)}) collective-permute-start(bf16[24,1536]{1,0:T(8,128)(2,1)S(1)} %fusion.41), channel_id=1, source_target_pairs={{0,6},{1,7},{2,4},{3,5},{4,2},{5,3},{6,0},{7,1},{8,14},{9,15},{10,... | collective-permute-start | bytes 221192 | tf_op jit(solution)/shard_map/ppermute | solution.py:27
  127.9 4.3 %collective-permute-done.37 = f32[16,768]{1,0:T(8,128)S(1)} collective-permute-done((f32[16,768]{1,0:T(8,128)S(1)}, f32[16,768]{1,0:T(8,128)S(1)}, u32[]{:S(2)}, u32[]{:S(2)}) %collective-permute-start.37) | collective-permute-done | bytes 49184 | tf_op jit(solution)/shard_map/ppermute | solution.py:27
  140.0 3.4 %fusion.39 = bf16[1,2,8,16,768]{4,3,2,1,0:T(8,128)(2,1)} fusion(f32[2,8,16,768]{3,2,1,0:T(8,128)S(1)} %copy-done.30, f32[4,10,18,768]{3,2,1,0:T(8,128)S(1)} %select_maximum_fusion, f32[768]{0:T(1024)S(1)} %get-tuple-element.94, f32[768]{0:T(1024)S(1)} %get-tuple-element.95, f32[768]{0:T(1024)S(1)} %get-tuple-element.70, f32[768]{0:T(1024)S(1)} %get-tuple-element.71, ...), kind=kLoop, calls=%fused_computation.78 | loop fusion | flops 11206656 | bytes 20923392 | tf_op jit(solution)/shard_map/broadcast_in_dim | solution.py:794
  143.9 4.7 %collective-permute-done.38.refs_5_ = bf16[96,1536]{1,0:T(8,128)(2,1)S(1)} collective-permute-done((bf16[96,1536]{1,0:T(8,128)(2,1)S(1)}, bf16[96,1536]{1,0:T(8,128)(2,1)S(1)}, u32[]{:S(2)}, u32[]{:S(2)}) %collective-permute-start.38) | collective-permute-done | bytes 294944 | tf_op jit(solution)/shard_map/ppermute | solution.py:27
  150.2 3.1 %assemble.1 = (f32[384,2304]{1,0:T(8,128)}, f32[384,768]{1,0:T(8,128)}) custom-call(s32[7]{0:T(128)S(1)} %copy-done.26, bf16[96,1536]{1,0:T(8,128)(2,1)S(1)} %pad_maximum_fusion.3.refs_0_, bf16[96,1536]{1,0:T(8,128)(2,1)S(1)} %collective-permute-done.25.refs_1_, bf16[96,1536]{1,0:T(8,128)(2,1)S(1)} %collective-permute-done.26.refs_2_, ...), custom_call_target="tpu_custom_call" | custom-call | flops 15000000 | bytes 700000 | tf_op jit(solution)/shard_map/assemble/pallas_call | solution.py:443
  (191 shorter events, 61.3 us)
Async XLA Ops:
  4.4 9.5 %collective-permute-start.1 = (bf16[128,768]{1,0:T(8,128)(2,1)S(1)}, bf16[128,768]{1,0:T(8,128)(2,1)S(1)}, u32[]{:S(2)}, u32[]{:S(2)}) collective-permute-start(bf16[128,768]{1,0:T(8,128)(2,1)S(1)} %bitcast.23), channel_id=1, source_target_pairs={{0,7},{1,2},{2,1},{3,4},{4,3},{5,6},{6,5},{7,0},{8,15},{9,10},{10,... | collective-permute-start | bytes 589832 | tf_op jit(solution)/shard_map/ppermute | solution.py:33
  12.2 28.6 %collective-permute-start.4 = (bf16[192,3072]{1,0:T(8,128)(2,1)}, bf16[192,3072]{1,0:T(8,128)(2,1)S(1)}, u32[]{:S(2)}, u32[]{:S(2)}) collective-permute-start(bf16[192,3072]{1,0:T(8,128)(2,1)} %get-tuple-element.42), channel_id=1, source_target_pairs={{0,8},{8,0},{1,9},{9,1},{2,10},{10,2},{3,11},{11,3},{4,12},{12,4},... | collective-permute-start | bytes 3538952 | tf_op jit(solution)/shard_map/ppermute | solution.py:27
  62.3 14.8 %collective-permute-start.10 = (bf16[96,1536]{1,0:T(8,128)(2,1)}, bf16[96,1536]{1,0:T(8,128)(2,1)}, u32[]{:S(2)}, u32[]{:S(2)}) collective-permute-start(bf16[96,1536]{1,0:T(8,128)(2,1)} %get-tuple-element.51), channel_id=1, source_target_pairs={{0,16},{8,24},{16,0},{24,8},{1,17},{9,25},{17,1},{25,9},{2,18},{10... | collective-permute-start | bytes 884744 | tf_op jit(solution)/shard_map/ppermute | solution.py:27
  63.8 16.6 %collective-permute-start.11 = (bf16[96,1536]{1,0:T(8,128)(2,1)S(1)}, bf16[96,1536]{1,0:T(8,128)(2,1)}, u32[]{:S(2)}, u32[]{:S(2)}) collective-permute-start(bf16[96,1536]{1,0:T(8,128)(2,1)S(1)} %get-tuple-element.52), channel_id=1, source_target_pairs={{0,24},{8,16},{16,8},{24,0},{1,25},{9,17},{17,9},{25,1},{2,26},{10... | collective-permute-start | bytes 884744 | tf_op jit(solution)/shard_map/ppermute | solution.py:27
  65.3 15.1 %collective-permute-start.9 = (bf16[96,1536]{1,0:T(8,128)(2,1)S(1)}, bf16[96,1536]{1,0:T(8,128)(2,1)}, u32[]{:S(2)}, u32[]{:S(2)}) collective-permute-start(bf16[96,1536]{1,0:T(8,128)(2,1)S(1)} %get-tuple-element.50), channel_id=1, source_target_pairs={{0,8},{8,0},{16,24},{24,16},{1,9},{9,1},{17,25},{25,17},{2,10},{10... | collective-permute-start | bytes 884744 | tf_op jit(solution)/shard_map/ppermute | solution.py:27
  77.2 13.9 %collective-permute-start.8 = (bf16[256,768]{1,0:T(8,128)(2,1)}, bf16[256,768]{1,0:T(8,128)(2,1)}, u32[]{:S(2)}, u32[]{:S(2)}) collective-permute-start(bf16[256,768]{1,0:T(8,128)(2,1)} %get-tuple-element.49), channel_id=1, source_target_pairs={{0,7},{1,2},{2,1},{3,4},{4,3},{5,6},{6,5},{7,0},{8,15},{9,10},{10,... | collective-permute-start | bytes 1179656 | tf_op jit(solution)/shard_map/ppermute | solution.py:33
  86.2 13.4 %collective-permute-start.14 = (bf16[96,1536]{1,0:T(8,128)(2,1)S(1)}, bf16[96,1536]{1,0:T(8,128)(2,1)S(1)}, u32[]{:S(2)}, u32[]{:S(2)}) collective-permute-start(bf16[96,1536]{1,0:T(8,128)(2,1)S(1)} %get-tuple-element.63), channel_id=1, source_target_pairs={{0,8},{8,0},{16,24},{24,16},{1,9},{9,1},{17,25},{25,17},{2,10},{10... | collective-permute-start | bytes 884744 | tf_op jit(solution)/shard_map/ppermute | solution.py:27
  87.7 12.4 %collective-permute-start.15 = (bf16[96,1536]{1,0:T(8,128)(2,1)S(1)}, bf16[96,1536]{1,0:T(8,128)(2,1)S(1)}, u32[]{:S(2)}, u32[]{:S(2)}) collective-permute-start(bf16[96,1536]{1,0:T(8,128)(2,1)S(1)} %get-tuple-element.64), channel_id=1, source_target_pairs={{0,16},{8,24},{16,0},{24,8},{1,17},{9,25},{17,1},{25,9},{2,18},{10... | collective-permute-start | bytes 884744 | tf_op jit(solution)/shard_map/ppermute | solution.py:27
  89.2 11.8 %collective-permute-start.16 = (bf16[96,1536]{1,0:T(8,128)(2,1)S(1)}, bf16[96,1536]{1,0:T(8,128)(2,1)S(1)}, u32[]{:S(2)}, u32[]{:S(2)}) collective-permute-start(bf16[96,1536]{1,0:T(8,128)(2,1)S(1)} %get-tuple-element.65), channel_id=1, source_target_pairs={{0,24},{8,16},{16,8},{24,0},{1,25},{9,17},{17,9},{25,1},{2,26},{10... | collective-permute-start | bytes 884744 | tf_op jit(solution)/shard_map/ppermute | solution.py:27
  89.7 15.8 %collective-permute-start.19 = (bf16[24,1536]{1,0:T(8,128)(2,1)S(1)}, bf16[24,1536]{1,0:T(8,128)(2,1)S(1)}, u32[]{:S(2)}, u32[]{:S(2)}) collective-permute-start(bf16[24,1536]{1,0:T(8,128)(2,1)S(1)} %get-tuple-element.111), channel_id=1, source_target_pairs={{0,2},{1,3},{2,0},{3,1},{4,6},{5,7},{6,4},{7,5},{8,10},{9,11},{10,... | collective-permute-start | bytes 221192 | tf_op jit(solution)/shard_map/ppermute | solution.py:27
  91.1 18.4 %collective-permute-start.20 = (bf16[24,1536]{1,0:T(8,128)(2,1)S(1)}, bf16[24,1536]{1,0:T(8,128)(2,1)S(1)}, u32[]{:S(2)}, u32[]{:S(2)}) collective-permute-start(bf16[24,1536]{1,0:T(8,128)(2,1)S(1)} %get-tuple-element.113), channel_id=1, source_target_pairs={{0,4},{1,5},{2,6},{3,7},{4,0},{5,1},{6,2},{7,3},{8,12},{9,13},{10,... | collective-permute-start | bytes 221192 | tf_op jit(solution)/shard_map/ppermute | solution.py:27
  99.6 11.5 %collective-permute-start.21 = (bf16[24,1536]{1,0:T(8,128)(2,1)S(1)}, bf16[24,1536]{1,0:T(8,128)(2,1)S(1)}, u32[]{:S(2)}, u32[]{:S(2)}) collective-permute-start(bf16[24,1536]{1,0:T(8,128)(2,1)S(1)} %get-tuple-element.112), channel_id=1, source_target_pairs={{0,6},{1,7},{2,4},{3,5},{4,2},{5,3},{6,0},{7,1},{8,14},{9,15},{10,... | collective-permute-start | bytes 221192 | tf_op jit(solution)/shard_map/ppermute | solution.py:27
  103.9 11.6 %collective-permute-start.28 = (bf16[24,1536]{1,0:T(8,128)(2,1)S(1)}, bf16[24,1536]{1,0:T(8,128)(2,1)S(1)}, u32[]{:S(2)}, u32[]{:S(2)}) collective-permute-start(bf16[24,1536]{1,0:T(8,128)(2,1)S(1)} %get-tuple-element.108), channel_id=1, source_target_pairs={{0,2},{1,3},{2,0},{3,1},{4,6},{5,7},{6,4},{7,5},{8,10},{9,11},{10,... | collective-permute-start | bytes 221192 | tf_op jit(solution)/shard_map/ppermute | solution.py:27
  105.5 11.1 %collective-permute-start.29 = (bf16[24,1536]{1,0:T(8,128)(2,1)S(1)}, bf16[24,1536]{1,0:T(8,128)(2,1)S(1)}, u32[]{:S(2)}, u32[]{:S(2)}) collective-permute-start(bf16[24,1536]{1,0:T(8,128)(2,1)S(1)} %get-tuple-element.110), channel_id=1, source_target_pairs={{0,4},{1,5},{2,6},{3,7},{4,0},{5,1},{6,2},{7,3},{8,12},{9,13},{10,... | collective-permute-start | bytes 221192 | tf_op jit(solution)/shard_map/ppermute | solution.py:27
  107.6 9.9 %collective-permute-start.30 = (bf16[24,1536]{1,0:T(8,128)(2,1)S(1)}, bf16[24,1536]{1,0:T(8,128)(2,1)S(1)}, u32[]{:S(2)}, u32[]{:S(2)}) collective-permute-start(bf16[24,1536]{1,0:T(8,128)(2,1)S(1)} %get-tuple-element.109), channel_id=1, source_target_pairs={{0,6},{1,7},{2,4},{3,5},{4,2},{5,3},{6,0},{7,1},{8,14},{9,15},{10,... | collective-permute-start | bytes 221192 | tf_op jit(solution)/shard_map/ppermute | solution.py:27
  112.1 13.6 %collective-permute-start.22 = (bf16[24,1536]{1,0:T(8,128)(2,1)S(1)}, bf16[24,1536]{1,0:T(8,128)(2,1)S(1)}, u32[]{:S(2)}, u32[]{:S(2)}) collective-permute-start(bf16[24,1536]{1,0:T(8,128)(2,1)S(1)} %fusion.43), channel_id=1, source_target_pairs={{0,2},{1,3},{2,0},{3,1},{4,6},{5,7},{6,4},{7,5},{8,10},{9,11},{10,... | collective-permute-start | bytes 221192 | tf_op jit(solution)/shard_map/ppermute | solution.py:27
  113.7 12.1 %collective-permute-start.23 = (bf16[24,1536]{1,0:T(8,128)(2,1)S(1)}, bf16[24,1536]{1,0:T(8,128)(2,1)S(1)}, u32[]{:S(2)}, u32[]{:S(2)}) collective-permute-start(bf16[24,1536]{1,0:T(8,128)(2,1)S(1)} %fusion.43), channel_id=1, source_target_pairs={{0,4},{1,5},{2,6},{3,7},{4,0},{5,1},{6,2},{7,3},{8,12},{9,13},{10,... | collective-permute-start | bytes 221192 | tf_op jit(solution)/shard_map/ppermute | solution.py:27
  115.5 10.9 %collective-permute-start.24 = (bf16[24,1536]{1,0:T(8,128)(2,1)S(1)}, bf16[24,1536]{1,0:T(8,128)(2,1)S(1)}, u32[]{:S(2)}, u32[]{:S(2)}) collective-permute-start(bf16[24,1536]{1,0:T(8,128)(2,1)S(1)} %fusion.43), channel_id=1, source_target_pairs={{0,6},{1,7},{2,4},{3,5},{4,2},{5,3},{6,0},{7,1},{8,14},{9,15},{10,... | collective-permute-start | bytes 221192 | tf_op jit(solution)/shard_map/ppermute | solution.py:27
  116.6 20.0 %collective-permute-start.17 = (bf16[8,16,768]{2,1,0:T(8,128)(2,1)}, bf16[8,16,768]{2,1,0:T(8,128)(2,1)S(1)}, u32[]{:S(2)}, u32[]{:S(2)}) collective-permute-start(bf16[8,16,768]{2,1,0:T(8,128)(2,1)} %ordered.19), channel_id=1, source_target_pairs={{1,2},{3,4},{5,6},{2,1},{4,3},{6,5},{9,10},{11,12},{13,14},{10,9},... | collective-permute-start | bytes 589832 | tf_op jit(solution)/shard_map/ppermute | solution.py:39
  121.7 11.2 %collective-permute-start.33 = (bf16[24,1536]{1,0:T(8,128)(2,1)S(1)}, bf16[24,1536]{1,0:T(8,128)(2,1)S(1)}, u32[]{:S(2)}, u32[]{:S(2)}) collective-permute-start(bf16[24,1536]{1,0:T(8,128)(2,1)S(1)} %fusion.41), channel_id=1, source_target_pairs={{0,6},{1,7},{2,4},{3,5},{4,2},{5,3},{6,0},{7,1},{8,14},{9,15},{10,... | collective-permute-start | bytes 221192 | tf_op jit(solution)/shard_map/ppermute | solution.py:27
  132.9 10.6 %collective-permute-start.25 = (bf16[96,1536]{1,0:T(8,128)(2,1)S(1)}, bf16[96,1536]{1,0:T(8,128)(2,1)S(1)}, u32[]{:S(2)}, u32[]{:S(2)}) collective-permute-start(bf16[96,1536]{1,0:T(8,128)(2,1)S(1)} %pad_maximum_fusion.3.refs_0_), channel_id=1, source_target_pairs={{0,16},{16,0},{1,17},{17,1},{2,18},{18,2},{3,19},{19,3},{4,20},{20... | collective-permute-start | bytes 884744 | tf_op jit(solution)/shard_map/ppermute | solution.py:27
  133.9 15.8 %collective-permute-start.26 = (bf16[96,1536]{1,0:T(8,128)(2,1)S(1)}, bf16[96,1536]{1,0:T(8,128)(2,1)S(1)}, u32[]{:S(2)}, u32[]{:S(2)}) collective-permute-start(bf16[96,1536]{1,0:T(8,128)(2,1)S(1)} %pad_maximum_fusion.3.refs_0_), channel_id=1, source_target_pairs={{0,1},{1,0},{2,3},{3,2},{4,5},{5,4},{6,7},{7,6},{8,9},{9,8},{10,11... | collective-permute-start | bytes 884744 | tf_op jit(solution)/shard_map/ppermute | solution.py:27
  136.6 12.0 %collective-permute-start.38 = (bf16[96,1536]{1,0:T(8,128)(2,1)S(1)}, bf16[96,1536]{1,0:T(8,128)(2,1)S(1)}, u32[]{:S(2)}, u32[]{:S(2)}) collective-permute-start(bf16[96,1536]{1,0:T(8,128)(2,1)S(1)} %pad_maximum_fusion.4.refs_4_), channel_id=1, source_target_pairs={{0,16},{16,0},{1,17},{17,1},{2,18},{18,2},{3,19},{19,3},{4,20},{20... | collective-permute-start | bytes 884744 | tf_op jit(solution)/shard_map/ppermute | solution.py:27
  137.6 12.2 %collective-permute-start.39 = (bf16[96,1536]{1,0:T(8,128)(2,1)S(1)}, bf16[96,1536]{1,0:T(8,128)(2,1)S(1)}, u32[]{:S(2)}, u32[]{:S(2)}) collective-permute-start(bf16[96,1536]{1,0:T(8,128)(2,1)S(1)} %pad_maximum_fusion.4.refs_4_), channel_id=1, source_target_pairs={{0,1},{1,0},{2,3},{3,2},{4,5},{5,4},{6,7},{7,6},{8,9},{9,8},{10,11... | collective-permute-start | bytes 884744 | tf_op jit(solution)/shard_map/ppermute | solution.py:27
  (57 other events, 441.5 us)

commit v6 on v5

--- a/solution.py
+++ b/solution.py
@@ -454,7 +454,7 @@
     )(nums, *first, *second)
 
 
-def sum_steps(x, place):
+def sum_steps(x, place, hold):
     half = x.shape[0] // 2
     low = place.core == 0
     x = jnp.where(low, x[:half], x[half:]) + swapped(
@@ -466,6 +466,8 @@
     yield x
     flip = 2
     while flip < lax.axis_size("seq"):
+        if hold:
+            x = after(x, *hold)
         x = x + swapped(x, "seq", flip)
         yield x
         flip = flip * 2
@@ -488,8 +490,9 @@
 
 
 def shifted_fields(before, slab, behind, lanes):
-    planes = jnp.concatenate([before[:, :, lanes][None], slab[0, :, :, :, lanes], behind[:, :, lanes][None]])
-    planes = planes.astype(F32)
+    middle = slab[0, :, :, :, lanes] if len(slab.shape) == 5 else slab[:, :, :, lanes]
+    planes = [before[:, :, lanes][None], middle, behind[:, :, lanes][None]]
+    planes = jnp.concatenate([p.astype(F32) for p in planes])
     row = jnp.zeros_like(planes[:, :1])
     planes = jnp.concatenate([row, planes, row], axis=1)
     column = jnp.zeros_like(planes[:, :, :1])
@@ -537,6 +540,34 @@
         compiler_params=pltpu.CompilerParams(vmem_limit_bytes=24 * 1024 * 1024),
         cost_estimate=busy(1, 2),
         name="field_forward",
+    )(*operands)
+
+
+def field_gradient_kernel(field, before, behind, weight, out):
+    depth, height, width, channels = field.shape
+    tile = 128
+    for start in range(0, channels, tile):
+        lanes = slice(start, start + tile)
+        total = field[:, :, :, lanes]
+        for e, shifted in enumerate(shifted_fields(before, field, behind, lanes)):
+            for a in range(3):
+                for b in range(3):
+                    t = 9 * (2 - a) + 3 * (2 - b) + 2 - e
+                    factor = weight[t : t + 1, lanes].reshape(1, 1, 1, tile)
+                    total = total + factor * shifted[a : a + depth, b : b + height]
+        out[:, :, :, lanes] = total.astype(BF)
+
+
+def field_gradient(operands):
+    vmem = pl.BlockSpec(memory_space=pltpu.VMEM)
+    return pl.pallas_call(
+        field_gradient_kernel,
+        out_shape=jax.ShapeDtypeStruct(operands[0].shape, BF),
+        in_specs=[vmem] * len(operands),
+        out_specs=vmem,
+        compiler_params=pltpu.CompilerParams(vmem_limit_bytes=24 * 1024 * 1024),
+        cost_estimate=busy(1, 2),
+        name="field_gradient",
     )(*operands)
 
 
@@ -766,7 +797,8 @@
     )
     second_total = sum_square(after(own, small), sends, place)
     first_block = sum_chips(first_total, place, second_total)
-    steps = sum_steps(after(small, second_total), place)
+    hold = []
+    steps = sum_steps(after(small, second_total), place, hold)
     small = next(steps)
     small = next(steps)
     second_block = sum_chips(second_total, place)
@@ -774,17 +806,16 @@
     factor = 1.0 / math.sqrt(
         lax.axis_size("rep") * lax.axis_size("dp") * lax.axis_size("seq") * positions
     )
-    grad_qkv, grad_proj = assemble(
-        nums, gather_blocks(first_block, place), gather_blocks(second_block, place, small), place, factor, group
-    )
+    first_parts = gather_blocks(first_block, place)
+    second_parts = gather_blocks(second_block, place, small)
+    hold.append(second_parts[0])
+    grad_qkv, grad_proj = assemble(nums, first_parts, second_parts, place, factor, group)
     inner = swapped(after(inner, second_total), "seq", 1)
     outer = edge_partner(after(outer, second_total))
-    padded_back = jnp.pad(
-        with_halo(back_mixed, inner.astype(F32), outer.astype(F32), core), spatial
-    )
-    grad_tokens = (
-        back_mixed + tap_sum(padded_back, conv_weight, depth, height, width, True)
-    ).astype(BF)
+    low = core == 0
+    grad_tokens = field_gradient(
+        (back_mixed, jnp.where(low, outer, inner), jnp.where(low, inner, outer), conv_weight)
+    )
     for small in steps:
         pass
     small = small * factor

time: 154 us -> 159 us (1.032)
  starting transfers between devices: 49.8 us -> 54.3 us
  other arithmetic: 18.9 us -> 16.7 us
  local copies, waits for them, and re-layouts: 12.5 us -> 14.1 us
    ppermute x38, starting transfers between devices: 37.2 us -> 41.4 us  [swapped(): return lax.ppermute(x, axis, [(i, i ^ flip) for i in range(count)])]
    broadcast_in_dim x2 -> x0, other arithmetic: 3.47 us -> none  [the longest x1 3.4 us: per_device(): grad_tokens[None]]
    unnamed x76 -> x86, local copies, waits for them, and re-layouts: 8.13 us -> 10.9 us
    pallas_call x0 -> x1, Pallas kernels: none -> 2.45 us  [field_gradient(): pl.pallas_call(field_gradient_kernel, out_shape=jax.ShapeDtypeStruct(oper...]
  transfers between devices with their start and end apart: 43 -> 43, of which waited for: 12 -> 13; matrix products, arithmetic and copies ran while one was open for 14% -> 11% of each run, Pallas kernels for 15% -> 16%
where the time goes in v6:
time: 159 us; the launch traced here: 158 us
  starting transfers between devices  54.3 us (34%)
  Pallas kernels  38.7 us (24%)
  waiting for transfers between devices  31.2 us (20%)
  other arithmetic  16.7 us (11%)
  local copies, waits for them, and re-layouts  14.1 us (9%)
  matrix products  1.84 us (1%)
    ppermute x38, starting transfers between devices, swapped(): return lax.ppermute(x, axis, [(i, i ^ flip) for i in range(count)])  41.4 us
    ppermute x38, waiting for transfers between devices, swapped(): return lax.ppermute(x, axis, [(i, i ^ flip) for i in range(count)])  27.5 us
    pallas_call x2, Pallas kernels, attention_call(): pl.pallas_call(functools.partial(body, group, head_dim), out_shape=shapes...  18.1 us
    ppermute x3, starting transfers between devices, window_partner(): return lax.ppermute(x, 'seq', pairs)  11 us
    unnamed x86, local copies, waits for them, and re-layouts  10.9 us
    pallas_call x1, Pallas kernels, field_back(): pl.pallas_call(field_kernel, grid=(1,), out_shape=(jax.ShapeDtypeStruct(m...  5.91 us
    another operation x2, other arithmetic  4.18 us
    pallas_call x2, Pallas kernels, chip_gradient(): pl.pallas_call(functools.partial(gradient_kernel, width, has_proj), out_s...  3.87 us
  transfers between devices with their start and end apart: 43, of which 13 were waited for; matrix products, arithmetic and copies ran while one was open for 11% of the time, Pallas kernels for 16%

profile of v6, /device:TPU:0, one launch (start us, length us, event | category | flops | bytes accessed | tf_op | source)
XLA Modules:
  0.0 158.0 jit_solution(5742532211283914049)
XLA Ops:
  4.3 4.5 %collective-permute-start.1 = (bf16[128,768]{1,0:T(8,128)(2,1)S(1)}, bf16[128,768]{1,0:T(8,128)(2,1)}, u32[]{:S(2)}, u32[]{:S(2)}) collective-permute-start(bf16[128,768]{1,0:T(8,128)(2,1)S(1)} %bitcast.19), channel_id=1, source_target_pairs={{0,7},{1,2},{2,1},{3,4},{4,3},{5,6},{6,5},{7,0},{8,15},{9,10},{10,... | collective-permute-start | bytes 589832 | tf_op jit(solution)/shard_map/ppermute | solution.py:33
  8.8 2.5 %stage.1 = (bf16[192,3072]{1,0:T(8,128)(2,1)}, bf16[8,16,768]{2,1,0:T(8,128)(2,1)}, bf16[8,16,768]{2,1,0:T(8,128)(2,1)}) custom-call(s32[1]{0:T(128)} %bitcast.2.core, bf16[384,2304]{1,0:T(8,128)(2,1)} %refs_1_.1, bf16[384,768]{1,0:T(8,128)(2,1)} %refs_12_.1, bf16[1,2,8,16,768]{4,3,2,1,0:T(8,128)(2,1)} %refs_6_.1), custom_call_target="tpu_custom_call" | custom-call | flops 12500000 | bytes 400000 | tf_op jit(solution)/shard_map/stage/pallas_call | solution.py:235
  15.7 2.8 %field_forward.1 = (f32[2,8,16,768]{3,2,1,0:T(8,128)S(1)}, bf16[128,768]{1,0:T(8,128)(2,1)S(1)}, bf16[128,768]{1,0:T(8,128)(2,1)S(1)}) custom-call(s32[7]{0:T(128)S(1)} %stack.23.nums.refs_0_.at, bf16[1,2,8,16,768]{4,3,2,1,0:T(8,128)(2,1)S(1)} %copy-done.8, bf16[8,16,768]{2,1,0:T(8,128)(2,1)S(1)} %get-tuple-element.80.before.refs_7_, ...), custom_call_target="tpu_custom_call" | custom-call | flops 5000000 | bytes 200000 | tf_op jit(solution)/shard_map/field_forward/pallas_call | solution.py:535
  19.4 3.3 %collective-permute-start.3 = (bf16[128,768]{1,0:T(8,128)(2,1)S(1)}, bf16[128,768]{1,0:T(8,128)(2,1)S(1)}, u32[]{:S(2)}, u32[]{:S(2)}) collective-permute-start(bf16[128,768]{1,0:T(8,128)(2,1)S(1)} %get-tuple-element.41), channel_id=1, source_target_pairs={{0,7},{1,2},{2,1},{3,4},{4,3},{5,6},{6,5},{7,0},{8,15},{9,10},{10,... | collective-permute-start | bytes 589832 | tf_op jit(solution)/shard_map/ppermute | solution.py:33
  24.0 3.7 %collective-permute-done.3.xg = bf16[128,768]{1,0:T(8,128)(2,1)S(1)} collective-permute-done((bf16[128,768]{1,0:T(8,128)(2,1)S(1)}, bf16[128,768]{1,0:T(8,128)(2,1)S(1)}, u32[]{:S(2)}, u32[]{:S(2)}) %collective-permute-start.3) | collective-permute-done | bytes 196640 | tf_op jit(solution)/shard_map/ppermute | solution.py:33
  32.3 8.6 %collective-permute-done.4.refs_0_ = bf16[192,3072]{1,0:T(8,128)(2,1)S(1)} collective-permute-done((bf16[192,3072]{1,0:T(8,128)(2,1)}, bf16[192,3072]{1,0:T(8,128)(2,1)S(1)}, u32[]{:S(2)}, u32[]{:S(2)}) %collective-permute-start.4) | collective-permute-done | bytes 1179680 | tf_op jit(solution)/shard_map/ppermute | solution.py:27
  42.9 2.0 %collective-permute-done.6.other.refs_3_.refs_14_ = bf16[192,3072]{1,0:T(8,128)(2,1)S(1)} collective-permute-done((bf16[192,3072]{1,0:T(8,128)(2,1)}, bf16[192,3072]{1,0:T(8,128)(2,1)S(1)}, u32[]{:S(2)}, u32[]{:S(2)}) %collective-permute-start.6) | collective-permute-done | bytes 1179680 | tf_op jit(solution)/shard_map/ppermute | solution.py:27
  48.1 8.7 %first_heads.1 = (bf16[1536,256]{1,0:T(8,128)(2,1)S(1)}, bf16[512,256]{1,0:T(8,128)(2,1)S(1)}, bf16[768,256]{1,0:T(8,128)(2,1)S(1)}, f32[16,256]{1,0:T(8,128)S(1)}) custom-call(s32[7]{0:T(128)S(1)} %stack.23.nums.refs_0_.at, f32[24]{0:T(128)S(1)} %copy-done.33, bf16[128,768]{1,0:T(8,128)(2,1)S(1)} %copy-done.20, bf16[128,768]{1,0:T(8,128)(2,1)S(1)} %copy-done.22, ...), custom_call_target="tpu_custom_call" | custom-call | flops 65000000 | bytes 800000 | tf_op jit(solution)/shard_map/first_heads/pallas_call | solution.py:201
  57.1 2.1 %collective-permute-done.7.refs_3_ = bf16[1536,256]{1,0:T(8,128)(2,1)S(1)} collective-permute-done((bf16[1536,256]{1,0:T(8,128)(2,1)S(1)}, bf16[1536,256]{1,0:T(8,128)(2,1)S(1)}, u32[]{:S(2)}, u32[]{:S(2)}) %collective-permute-start.7) | collective-permute-done | bytes 786464 | tf_op jit(solution)/shard_map/ppermute | solution.py:27
  65.5 9.4 %second_heads.1 = (bf16[1152,256]{1,0:T(8,128)(2,1)}, bf16[384,256]{1,0:T(8,128)(2,1)}, bf16[128,768]{1,0:T(8,128)(2,1)}, bf16[256,768]{1,0:T(8,128)(2,1)}, bf16[128,768]{1,0:T(8,128)(2,1)}, /*index=5*/f32[8,256]{1,0:T(8,128)}) custom-call(s32[7]{0:T(128)} %copy-done.29, f32[24]{0:T(128)} %scale.3, bf16[128,768]{1,0:T(8,128)(2,1)} %copy-done.19, ...), custom_call_target="tpu_custom_call" | custom-call | flops 45000000 | bytes 800000 | tf_op jit(solution)/shard_map/second_heads/pallas_call | solution.py:201
  76.1 3.2 %collective-permute-start.8 = (bf16[256,768]{1,0:T(8,128)(2,1)}, bf16[256,768]{1,0:T(8,128)(2,1)S(1)}, u32[]{:S(2)}, u32[]{:S(2)}) collective-permute-start(bf16[256,768]{1,0:T(8,128)(2,1)} %get-tuple-element.49), channel_id=1, source_target_pairs={{0,7},{1,2},{2,1},{3,4},{4,3},{5,6},{6,5},{7,0},{8,15},{9,10},{10,... | collective-permute-start | bytes 1179656 | tf_op jit(solution)/shard_map/ppermute | solution.py:33
  79.9 2.2 %fusion.29 = (bf16[96,1536]{1,0:T(8,128)(2,1)}, f32[96,1536]{1,0:T(8,128)}) fusion(bf16[96,1536]{1,0:T(8,128)(2,1)} %collective-permute-done.11, bf16[96,1536]{1,0:T(8,128)(2,1)} %copy-done.37, f32[96,1536]{1,0:T(8,128)S(1)} %copy-done.14, bf16[96,1536]{1,0:T(8,128)(2,1)} %collective-permute-done.9), kind=kLoop, calls=%fused_computation.69 | loop fusion | flops 1032192 | bytes 2359296 | tf_op jit(solution)/shard_map/convert.5
  84.1 2.0 %chip_gradient.3 = (f32[96,1536]{1,0:T(8,128)S(1)}, bf16[96,1536]{1,0:T(8,128)(2,1)S(1)}, bf16[96,1536]{1,0:T(8,128)(2,1)S(1)}, bf16[96,1536]{1,0:T(8,128)(2,1)S(1)}) custom-call(bf16[384,256]{1,0:T(8,128)(2,1)S(1)} %copy-done.10, bf16[384,256]{1,0:T(8,128)(2,1)} %collective-permute-done.5.refs_1_, bf16[1152,256]{1,0:T(8,128)(2,1)S(1)} %copy-done.24, ...), custom_call_target="tpu_custom_call" | custom-call | flops 7500000 | bytes 350000 | tf_op jit(solution)/shard_map/chip_gradient/pallas_call | solution.py:377
  92.7 5.9 %field_back.1 = (f32[2,8,16,768]{3,2,1,0:T(8,128)}, bf16[8,16,768]{2,1,0:T(8,128)(2,1)}, bf16[8,16,768]{2,1,0:T(8,128)(2,1)}, bf16[2,8,16,768]{3,2,1,0:T(8,128)(2,1)}, f32[32,768]{1,0:T(8,128)}) custom-call(s32[7]{0:T(128)} %copy-done.29, bf16[128,768]{1,0:T(8,128)(2,1)} %get-tuple-element.47.refs_1_, bf16[128,768]{1,0:T(8,128)(2,1)} %get-tuple-element.48.refs_2_, ...), custom_call_target="tpu_custom_call" | custom-call | flops 5000000 | bytes 200000 | tf_op jit(solution)/shard_map/field_back/pallas_call | solution.py:644
  98.7 2.5 %collective-permute-done.16 = bf16[96,1536]{1,0:T(8,128)(2,1)S(1)} collective-permute-done((bf16[96,1536]{1,0:T(8,128)(2,1)S(1)}, bf16[96,1536]{1,0:T(8,128)(2,1)S(1)}, u32[]{:S(2)}, u32[]{:S(2)}) %collective-permute-start.16) | collective-permute-done | bytes 294944 | tf_op jit(solution)/shard_map/ppermute | solution.py:27
  101.2 2.0 %fusion.28 = (bf16[96,1536]{1,0:T(8,128)(2,1)S(1)}, f32[96,1536]{1,0:T(8,128)}) fusion(bf16[96,1536]{1,0:T(8,128)(2,1)S(1)} %collective-permute-done.16, bf16[96,1536]{1,0:T(8,128)(2,1)S(1)} %collective-permute-done.15, f32[96,1536]{1,0:T(8,128)} %ordered.19, bf16[96,1536]{1,0:T(8,128)(2,1)S(1)} %collective-permute-done.14), kind=kLoop, calls=%fused_computation.68 | loop fusion | flops 1032192 | bytes 2359296 | tf_op jit(solution)/shard_map/convert.2
  105.7 2.5 %collective-permute-start.29 = (bf16[24,1536]{1,0:T(8,128)(2,1)S(1)}, bf16[24,1536]{1,0:T(8,128)(2,1)S(1)}, u32[]{:S(2)}, u32[]{:S(2)}) collective-permute-start(bf16[24,1536]{1,0:T(8,128)(2,1)S(1)} %get-tuple-element.83), channel_id=1, source_target_pairs={{0,4},{1,5},{2,6},{3,7},{4,0},{5,1},{6,2},{7,3},{8,12},{9,13},{10,... | collective-permute-start | bytes 221192 | tf_op jit(solution)/shard_map/ppermute | solution.py:27
  113.5 3.5 %collective-permute-start.21 = (bf16[24,1536]{1,0:T(8,128)(2,1)S(1)}, bf16[24,1536]{1,0:T(8,128)(2,1)S(1)}, u32[]{:S(2)}, u32[]{:S(2)}) collective-permute-start(bf16[24,1536]{1,0:T(8,128)(2,1)S(1)} %get-tuple-element.85), channel_id=1, source_target_pairs={{0,6},{1,7},{2,4},{3,5},{4,2},{5,3},{6,0},{7,1},{8,14},{9,15},{10,... | collective-permute-start | bytes 221192 | tf_op jit(solution)/shard_map/ppermute | solution.py:27
  120.0 2.0 %collective-permute-start.31 = (bf16[24,1536]{1,0:T(8,128)(2,1)S(1)}, bf16[24,1536]{1,0:T(8,128)(2,1)S(1)}, u32[]{:S(2)}, u32[]{:S(2)}) collective-permute-start(bf16[24,1536]{1,0:T(8,128)(2,1)S(1)} %fusion.5), channel_id=1, source_target_pairs={{0,2},{1,3},{2,0},{3,1},{4,6},{5,7},{6,4},{7,5},{8,10},{9,11},{10,... | collective-permute-start | bytes 221192 | tf_op jit(solution)/shard_map/ppermute | solution.py:27
  129.8 2.1 %collective-permute-start.24 = (bf16[24,1536]{1,0:T(8,128)(2,1)S(1)}, bf16[24,1536]{1,0:T(8,128)(2,1)S(1)}, u32[]{:S(2)}, u32[]{:S(2)}) collective-permute-start(bf16[24,1536]{1,0:T(8,128)(2,1)S(1)} %fusion.7), channel_id=1, source_target_pairs={{0,6},{1,7},{2,4},{3,5},{4,2},{5,3},{6,0},{7,1},{8,14},{9,15},{10,... | collective-permute-start | bytes 221192 | tf_op jit(solution)/shard_map/ppermute | solution.py:27
  135.6 2.7 %collective-permute-start.41 = (f32[16,768]{1,0:T(8,128)}, f32[16,768]{1,0:T(8,128)S(1)}, u32[]{:S(2)}, u32[]{:S(2)}) collective-permute-start(f32[16,768]{1,0:T(8,128)} %ordered.25), channel_id=1, source_target_pairs={{0,4},{1,5},{2,6},{3,7},{4,0},{5,1},{6,2},{7,3},{8,12},{9,13},{10,... | collective-permute-start | bytes 147464 | tf_op jit(solution)/shard_map/ppermute | solution.py:27
  144.4 2.4 %field_gradient.1 = bf16[2,8,16,768]{3,2,1,0:T(8,128)(2,1)} custom-call(f32[2,8,16,768]{3,2,1,0:T(8,128)S(1)} %copy-done.23, bf16[8,16,768]{2,1,0:T(8,128)(2,1)S(1)} %get-tuple-element.76.before, bf16[8,16,768]{2,1,0:T(8,128)(2,1)S(1)} %get-tuple-element.75.behind, f32[27,768]{1,0:T(8,128)S(1)} %copy-done.26), custom_call_target="tpu_custom_call" | custom-call | flops 5000000 | bytes 200000 | tf_op jit(solution)/shard_map/field_gradient/pallas_call | solution.py:563
  148.3 5.1 %collective-permute-done.38.refs_5_ = bf16[96,1536]{1,0:T(8,128)(2,1)S(1)} collective-permute-done((bf16[96,1536]{1,0:T(8,128)(2,1)}, bf16[96,1536]{1,0:T(8,128)(2,1)S(1)}, u32[]{:S(2)}, u32[]{:S(2)}) %collective-permute-start.38) | collective-permute-done | bytes 294944 | tf_op jit(solution)/shard_map/ppermute | solution.py:27
  154.9 3.1 %assemble.1 = (f32[384,2304]{1,0:T(8,128)}, f32[384,768]{1,0:T(8,128)}) custom-call(s32[7]{0:T(128)S(1)} %copy-done.30, bf16[96,1536]{1,0:T(8,128)(2,1)S(1)} %pad_maximum_fusion.1.refs_0_, bf16[96,1536]{1,0:T(8,128)(2,1)S(1)} %collective-permute-done.25.refs_1_, bf16[96,1536]{1,0:T(8,128)(2,1)S(1)} %collective-permute-done.26.refs_2_, ...), custom_call_target="tpu_custom_call" | custom-call | flops 15000000 | bytes 700000 | tf_op jit(solution)/shard_map/assemble/pallas_call | solution.py:443
  (199 shorter events, 68.0 us)
Async XLA Ops:
  12.3 28.6 %collective-permute-start.4 = (bf16[192,3072]{1,0:T(8,128)(2,1)}, bf16[192,3072]{1,0:T(8,128)(2,1)S(1)}, u32[]{:S(2)}, u32[]{:S(2)}) collective-permute-start(bf16[192,3072]{1,0:T(8,128)(2,1)} %get-tuple-element.42), channel_id=1, source_target_pairs={{0,8},{8,0},{1,9},{9,1},{2,10},{10,2},{3,11},{11,3},{4,12},{12,4},... | collective-permute-start | bytes 3538952 | tf_op jit(solution)/shard_map/ppermute | solution.py:27
  62.0 13.4 %collective-permute-start.10 = (bf16[96,1536]{1,0:T(8,128)(2,1)S(1)}, bf16[96,1536]{1,0:T(8,128)(2,1)S(1)}, u32[]{:S(2)}, u32[]{:S(2)}) collective-permute-start(bf16[96,1536]{1,0:T(8,128)(2,1)S(1)} %get-tuple-element.51), channel_id=1, source_target_pairs={{0,16},{8,24},{16,0},{24,8},{1,17},{9,25},{17,1},{25,9},{2,18},{10... | collective-permute-start | bytes 884744 | tf_op jit(solution)/shard_map/ppermute | solution.py:27
  63.5 15.9 %collective-permute-start.11 = (bf16[96,1536]{1,0:T(8,128)(2,1)S(1)}, bf16[96,1536]{1,0:T(8,128)(2,1)}, u32[]{:S(2)}, u32[]{:S(2)}) collective-permute-start(bf16[96,1536]{1,0:T(8,128)(2,1)S(1)} %get-tuple-element.52), channel_id=1, source_target_pairs={{0,24},{8,16},{16,8},{24,0},{1,25},{9,17},{17,9},{25,1},{2,26},{10... | collective-permute-start | bytes 884744 | tf_op jit(solution)/shard_map/ppermute | solution.py:27
  65.0 14.9 %collective-permute-start.9 = (bf16[96,1536]{1,0:T(8,128)(2,1)S(1)}, bf16[96,1536]{1,0:T(8,128)(2,1)}, u32[]{:S(2)}, u32[]{:S(2)}) collective-permute-start(bf16[96,1536]{1,0:T(8,128)(2,1)S(1)} %get-tuple-element.50), channel_id=1, source_target_pairs={{0,8},{8,0},{16,24},{24,16},{1,9},{9,1},{17,25},{25,17},{2,10},{10... | collective-permute-start | bytes 884744 | tf_op jit(solution)/shard_map/ppermute | solution.py:27
  76.1 15.9 %collective-permute-start.8 = (bf16[256,768]{1,0:T(8,128)(2,1)}, bf16[256,768]{1,0:T(8,128)(2,1)S(1)}, u32[]{:S(2)}, u32[]{:S(2)}) collective-permute-start(bf16[256,768]{1,0:T(8,128)(2,1)} %get-tuple-element.49), channel_id=1, source_target_pairs={{0,7},{1,2},{2,1},{3,4},{4,3},{5,6},{6,5},{7,0},{8,15},{9,10},{10,... | collective-permute-start | bytes 1179656 | tf_op jit(solution)/shard_map/ppermute | solution.py:33
  86.9 11.8 %collective-permute-start.14 = (bf16[96,1536]{1,0:T(8,128)(2,1)S(1)}, bf16[96,1536]{1,0:T(8,128)(2,1)S(1)}, u32[]{:S(2)}, u32[]{:S(2)}) collective-permute-start(bf16[96,1536]{1,0:T(8,128)(2,1)S(1)} %get-tuple-element.63), channel_id=1, source_target_pairs={{0,8},{8,0},{16,24},{24,16},{1,9},{9,1},{17,25},{25,17},{2,10},{10... | collective-permute-start | bytes 884744 | tf_op jit(solution)/shard_map/ppermute | solution.py:27
  87.9 10.8 %collective-permute-start.15 = (bf16[96,1536]{1,0:T(8,128)(2,1)S(1)}, bf16[96,1536]{1,0:T(8,128)(2,1)S(1)}, u32[]{:S(2)}, u32[]{:S(2)}) collective-permute-start(bf16[96,1536]{1,0:T(8,128)(2,1)S(1)} %get-tuple-element.64), channel_id=1, source_target_pairs={{0,16},{8,24},{16,0},{24,8},{1,17},{9,25},{17,1},{25,9},{2,18},{10... | collective-permute-start | bytes 884744 | tf_op jit(solution)/shard_map/ppermute | solution.py:27
  89.4 11.8 %collective-permute-start.16 = (bf16[96,1536]{1,0:T(8,128)(2,1)S(1)}, bf16[96,1536]{1,0:T(8,128)(2,1)S(1)}, u32[]{:S(2)}, u32[]{:S(2)}) collective-permute-start(bf16[96,1536]{1,0:T(8,128)(2,1)S(1)} %get-tuple-element.65), channel_id=1, source_target_pairs={{0,24},{8,16},{16,8},{24,0},{1,25},{9,17},{17,9},{25,1},{2,26},{10... | collective-permute-start | bytes 884744 | tf_op jit(solution)/shard_map/ppermute | solution.py:27
  90.4 20.5 %collective-permute-start.19 = (bf16[24,1536]{1,0:T(8,128)(2,1)S(1)}, bf16[24,1536]{1,0:T(8,128)(2,1)S(1)}, u32[]{:S(2)}, u32[]{:S(2)}) collective-permute-start(bf16[24,1536]{1,0:T(8,128)(2,1)S(1)} %get-tuple-element.84), channel_id=1, source_target_pairs={{0,2},{1,3},{2,0},{3,1},{4,6},{5,7},{6,4},{7,5},{8,10},{9,11},{10,... | collective-permute-start | bytes 221192 | tf_op jit(solution)/shard_map/ppermute | solution.py:27
  104.1 13.0 %collective-permute-start.28 = (bf16[24,1536]{1,0:T(8,128)(2,1)S(1)}, bf16[24,1536]{1,0:T(8,128)(2,1)S(1)}, u32[]{:S(2)}, u32[]{:S(2)}) collective-permute-start(bf16[24,1536]{1,0:T(8,128)(2,1)S(1)} %get-tuple-element.81), channel_id=1, source_target_pairs={{0,2},{1,3},{2,0},{3,1},{4,6},{5,7},{6,4},{7,5},{8,10},{9,11},{10,... | collective-permute-start | bytes 221192 | tf_op jit(solution)/shard_map/ppermute | solution.py:27
  105.7 11.9 %collective-permute-start.29 = (bf16[24,1536]{1,0:T(8,128)(2,1)S(1)}, bf16[24,1536]{1,0:T(8,128)(2,1)S(1)}, u32[]{:S(2)}, u32[]{:S(2)}) collective-permute-start(bf16[24,1536]{1,0:T(8,128)(2,1)S(1)} %get-tuple-element.83), channel_id=1, source_target_pairs={{0,4},{1,5},{2,6},{3,7},{4,0},{5,1},{6,2},{7,3},{8,12},{9,13},{10,... | collective-permute-start | bytes 221192 | tf_op jit(solution)/shard_map/ppermute | solution.py:27
  110.9 12.1 %collective-permute-start.20 = (bf16[24,1536]{1,0:T(8,128)(2,1)S(1)}, bf16[24,1536]{1,0:T(8,128)(2,1)S(1)}, u32[]{:S(2)}, u32[]{:S(2)}) collective-permute-start(bf16[24,1536]{1,0:T(8,128)(2,1)S(1)} %get-tuple-element.86), channel_id=1, source_target_pairs={{0,4},{1,5},{2,6},{3,7},{4,0},{5,1},{6,2},{7,3},{8,12},{9,13},{10,... | collective-permute-start | bytes 221192 | tf_op jit(solution)/shard_map/ppermute | solution.py:27
  113.5 10.2 %collective-permute-start.21 = (bf16[24,1536]{1,0:T(8,128)(2,1)S(1)}, bf16[24,1536]{1,0:T(8,128)(2,1)S(1)}, u32[]{:S(2)}, u32[]{:S(2)}) collective-permute-start(bf16[24,1536]{1,0:T(8,128)(2,1)S(1)} %get-tuple-element.85), channel_id=1, source_target_pairs={{0,6},{1,7},{2,4},{3,5},{4,2},{5,3},{6,0},{7,1},{8,14},{9,15},{10,... | collective-permute-start | bytes 221192 | tf_op jit(solution)/shard_map/ppermute | solution.py:27
  118.6 11.2 %collective-permute-start.33 = (bf16[24,1536]{1,0:T(8,128)(2,1)S(1)}, bf16[24,1536]{1,0:T(8,128)(2,1)S(1)}, u32[]{:S(2)}, u32[]{:S(2)}) collective-permute-start(bf16[24,1536]{1,0:T(8,128)(2,1)S(1)} %fusion.5), channel_id=1, source_target_pairs={{0,6},{1,7},{2,4},{3,5},{4,2},{5,3},{6,0},{7,1},{8,14},{9,15},{10,... | collective-permute-start | bytes 221192 | tf_op jit(solution)/shard_map/ppermute | solution.py:27
  120.0 12.0 %collective-permute-start.31 = (bf16[24,1536]{1,0:T(8,128)(2,1)S(1)}, bf16[24,1536]{1,0:T(8,128)(2,1)S(1)}, u32[]{:S(2)}, u32[]{:S(2)}) collective-permute-start(bf16[24,1536]{1,0:T(8,128)(2,1)S(1)} %fusion.5), channel_id=1, source_target_pairs={{0,2},{1,3},{2,0},{3,1},{4,6},{5,7},{6,4},{7,5},{8,10},{9,11},{10,... | collective-permute-start | bytes 221192 | tf_op jit(solution)/shard_map/ppermute | solution.py:27
  122.0 11.0 %collective-permute-start.32 = (bf16[24,1536]{1,0:T(8,128)(2,1)S(1)}, bf16[24,1536]{1,0:T(8,128)(2,1)S(1)}, u32[]{:S(2)}, u32[]{:S(2)}) collective-permute-start(bf16[24,1536]{1,0:T(8,128)(2,1)S(1)} %fusion.5), channel_id=1, source_target_pairs={{0,4},{1,5},{2,6},{3,7},{4,0},{5,1},{6,2},{7,3},{8,12},{9,13},{10,... | collective-permute-start | bytes 221192 | tf_op jit(solution)/shard_map/ppermute | solution.py:27
  124.7 10.8 %collective-permute-start.22 = (bf16[24,1536]{1,0:T(8,128)(2,1)S(1)}, bf16[24,1536]{1,0:T(8,128)(2,1)S(1)}, u32[]{:S(2)}, u32[]{:S(2)}) collective-permute-start(bf16[24,1536]{1,0:T(8,128)(2,1)S(1)} %fusion.7), channel_id=1, source_target_pairs={{0,2},{1,3},{2,0},{3,1},{4,6},{5,7},{6,4},{7,5},{8,10},{9,11},{10,... | collective-permute-start | bytes 221192 | tf_op jit(solution)/shard_map/ppermute | solution.py:27
  127.3 10.9 %collective-permute-start.23 = (bf16[24,1536]{1,0:T(8,128)(2,1)S(1)}, bf16[24,1536]{1,0:T(8,128)(2,1)S(1)}, u32[]{:S(2)}, u32[]{:S(2)}) collective-permute-start(bf16[24,1536]{1,0:T(8,128)(2,1)S(1)} %fusion.7), channel_id=1, source_target_pairs={{0,4},{1,5},{2,6},{3,7},{4,0},{5,1},{6,2},{7,3},{8,12},{9,13},{10,... | collective-permute-start | bytes 221192 | tf_op jit(solution)/shard_map/ppermute | solution.py:27
  131.9 11.8 %collective-permute-start.17 = (bf16[8,16,768]{2,1,0:T(8,128)(2,1)S(1)}, bf16[8,16,768]{2,1,0:T(8,128)(2,1)S(1)}, u32[]{:S(2)}, u32[]{:S(2)}) collective-permute-start(bf16[8,16,768]{2,1,0:T(8,128)(2,1)S(1)} %copy-done.40), channel_id=1, source_target_pairs={{1,2},{3,4},{5,6},{2,1},{4,3},{6,5},{9,10},{11,12},{13,14},{10,9},... | collective-permute-start | bytes 589832 | tf_op jit(solution)/shard_map/ppermute | solution.py:39
  133.0 10.9 %collective-permute-start.18 = (bf16[8,16,768]{2,1,0:T(8,128)(2,1)}, bf16[8,16,768]{2,1,0:T(8,128)(2,1)S(1)}, u32[]{:S(2)}, u32[]{:S(2)}) collective-permute-start(bf16[8,16,768]{2,1,0:T(8,128)(2,1)} %ordered.21), channel_id=1, source_target_pairs={{0,1},{1,0},{2,3},{3,2},{4,5},{5,4},{6,7},{7,6},{8,9},{9,8},{10,11... | collective-permute-start | bytes 589832 | tf_op jit(solution)/shard_map/ppermute | solution.py:27
  138.3 10.0 %collective-permute-start.25 = (bf16[96,1536]{1,0:T(8,128)(2,1)S(1)}, bf16[96,1536]{1,0:T(8,128)(2,1)S(1)}, u32[]{:S(2)}, u32[]{:S(2)}) collective-permute-start(bf16[96,1536]{1,0:T(8,128)(2,1)S(1)} %pad_maximum_fusion.1.refs_0_), channel_id=1, source_target_pairs={{0,16},{16,0},{1,17},{17,1},{2,18},{18,2},{3,19},{19,3},{4,20},{20... | collective-permute-start | bytes 884744 | tf_op jit(solution)/shard_map/ppermute | solution.py:27
  139.9 14.6 %collective-permute-start.26 = (bf16[96,1536]{1,0:T(8,128)(2,1)S(1)}, bf16[96,1536]{1,0:T(8,128)(2,1)S(1)}, u32[]{:S(2)}, u32[]{:S(2)}) collective-permute-start(bf16[96,1536]{1,0:T(8,128)(2,1)S(1)} %pad_maximum_fusion.1.refs_0_), channel_id=1, source_target_pairs={{0,1},{1,0},{2,3},{3,2},{4,5},{5,4},{6,7},{7,6},{8,9},{9,8},{10,11... | collective-permute-start | bytes 884744 | tf_op jit(solution)/shard_map/ppermute | solution.py:27
  141.5 11.9 %collective-permute-start.38 = (bf16[96,1536]{1,0:T(8,128)(2,1)}, bf16[96,1536]{1,0:T(8,128)(2,1)S(1)}, u32[]{:S(2)}, u32[]{:S(2)}) collective-permute-start(bf16[96,1536]{1,0:T(8,128)(2,1)} %pad_maximum_fusion.2.refs_4_.refs_1_), channel_id=1, source_target_pairs={{0,16},{16,0},{1,17},{17,1},{2,18},{18,2},{3,19},{19,3},{4,20},{20... | collective-permute-start | bytes 884744 | tf_op jit(solution)/shard_map/ppermute | solution.py:27
  143.8 10.7 %collective-permute-start.39 = (bf16[96,1536]{1,0:T(8,128)(2,1)}, bf16[96,1536]{1,0:T(8,128)(2,1)S(1)}, u32[]{:S(2)}, u32[]{:S(2)}) collective-permute-start(bf16[96,1536]{1,0:T(8,128)(2,1)} %pad_maximum_fusion.2.refs_4_.refs_1_), channel_id=1, source_target_pairs={{0,1},{1,0},{2,3},{3,2},{4,5},{5,4},{6,7},{7,6},{8,9},{9,8},{10,11... | collective-permute-start | bytes 884744 | tf_op jit(solution)/shard_map/ppermute | solution.py:27
  (62 other events, 372.3 us)
